TPU v7x, 512 devices: a whole 4x4x16 slice. The times are simulated.
512 devices in a mesh: dp: 16 (over x, y), vocab: 32 (over z, core).
Axes of the slice: x: 4, y: 4, z: 16, core: 2. Of those that a mesh axis runs over, the one named last changes fastest.
Arguments:
- student_hidden: bfloat16 [6144, 896], P('dp'), may hold values from -1500 to 1500
- head_weight: bfloat16 [896, 77824], P('dp', 'vocab'), may hold values from -0.625 to 0.625
- teacher_logits: bfloat16 [6144, 77824], P('dp', 'vocab'), may hold values from -4400 to 4400
Outputs:
- logit_grad: bfloat16 [6144, 77824], P('dp', 'vocab')
- hidden_grad: bfloat16 [6144, 896], P('dp', 'vocab')
All inputs are finite; a program needn't handle non-finite values.
Results may differ from a plain program's by a relative error of at most 0.005.
Values may be sent and summed in bfloat16 or wider, within the bound.
No kernel may reach another device: no remote copies, remote signals or barrier semaphores. Data moves between devices by JAX's collectives and lax.ppermute only.
A program may use at most 64 MiB of HBM per device.

v0:
```python
import jax
import jax.numpy as jnp
from jax import lax
from jax.sharding import PartitionSpec as P

TEMP = 4


EPS = 1e-06


def gradient_terms(prob_student, prob_teacher, row_terms, col_terms):
    row_den, row_rho, row_var = row_terms
    mean_s, mean_t, col_var, col_den, col_rho = col_terms
    inner = prob_teacher / row_den[:, None] - (row_rho / (row_var + EPS))[:, None] * prob_student
    inner = inner + (prob_teacher - mean_t[None, :]) / col_den[None, :]
    inner = inner - (col_rho / (col_var + EPS))[None, :] * (prob_student - mean_s[None, :])
    return -TEMP * inner


def body(student_hidden, head_weight, teacher_logits):
    tok_rows = student_hidden.shape[0]
    vocab_cols = head_weight.shape[1]
    classes = vocab_cols * lax.axis_size("vocab")
    tokens = tok_rows * lax.axis_size("dp")
    whole = lax.all_gather(head_weight, "dp", axis=0, tiled=True)
    logits = jnp.dot(student_hidden, whole, preferred_element_type=jnp.float32)
    scaled_student = logits / TEMP
    scaled_teacher = teacher_logits.astype(jnp.float32) / TEMP
    local_peak_s = jnp.max(scaled_student, axis=1)
    local_peak_t = jnp.max(scaled_teacher, axis=1)
    peak_student, peak_teacher = lax.pmax((local_peak_s, local_peak_t), "vocab")
    exp_student = jnp.exp(scaled_student - peak_student[:, None])
    exp_teacher = jnp.exp(scaled_teacher - peak_teacher[:, None])
    norm_student, norm_teacher, square_student, square_teacher, cross_rows = lax.psum(
        (
            jnp.sum(exp_student, 1),
            jnp.sum(exp_teacher, 1),
            jnp.sum(exp_student * exp_student, 1),
            jnp.sum(exp_teacher * exp_teacher, 1),
            jnp.sum(exp_student * exp_teacher, 1),
        ),
        "vocab",
    )
    row_var = classes * square_student / (norm_student * norm_student) - 1.0
    row_var_t = classes * square_teacher / (norm_teacher * norm_teacher) - 1.0
    cross = classes * cross_rows / (norm_student * norm_teacher) - 1.0
    row_den = jnp.sqrt((row_var + EPS) * (row_var_t + EPS))
    row_terms = (row_den, cross / row_den, row_var)
    prob_student = classes * exp_student / norm_student[:, None]
    prob_teacher = classes * exp_teacher / norm_teacher[:, None]
    sums = lax.psum(
        jnp.stack(
            [
                jnp.sum(prob_student, 0),
                jnp.sum(prob_teacher, 0),
                jnp.sum(prob_student * prob_student, 0),
                jnp.sum(prob_teacher * prob_teacher, 0),
                jnp.sum(prob_student * prob_teacher, 0),
            ]
        ),
        "dp",
    )
    mean_s = sums[0] / tokens
    mean_t = sums[1] / tokens
    col_var = sums[2] / tokens - mean_s * mean_s
    col_var_t = sums[3] / tokens - mean_t * mean_t
    col_cov = sums[4] / tokens - mean_s * mean_t
    col_den = jnp.sqrt((col_var + EPS) * (col_var_t + EPS))
    coeff = gradient_terms(
        prob_student, prob_teacher, row_terms, (mean_s, mean_t, col_var, col_den, col_cov / col_den)
    )
    row_dot = lax.psum(jnp.sum(prob_student * coeff, 1), "vocab") / classes
    logit_grad = (prob_student * (coeff - row_dot[:, None]) / TEMP).astype(jnp.bfloat16)
    partial_grad = lax.dot_general(
        logit_grad, whole, (((1,), (1,)), ((), ())), preferred_element_type=jnp.float32
    )
    hidden_grad = lax.psum_scatter(partial_grad, "vocab", scatter_dimension=1, tiled=True).astype(
        jnp.bfloat16
    )
    return (logit_grad, hidden_grad)


def solution(mesh):
    return jax.shard_map(
        body,
        mesh=mesh,
        in_specs=(P("dp", None), P("dp", "vocab"), P("dp", "vocab")),
        out_specs=(P("dp", "vocab"), P("dp", "vocab")),
        check_vma=False,
    )
```

profile of v0, /device:TPU:97, one launch (start us, length us, event | category | flops | bytes accessed | tf_op | source)
XLA Modules:
  0.0 452.4 jit_solution(6939509764392695774)
XLA Ops:
  7.2 0.0 copy-start
  7.2 0.0 all-gather.2.cloned.1.call-start
  7.2 0.7 all-gather.2.cloned.1.call-update
  7.9 2.0 fusion.1
  9.9 72.2 %all-gather.2.cloned.1.call-done = bf16[896,2432]{1,0:T(8,128)(2,1)} async-done(((bf16[56,2432]{1,0:T(8,128)(2,1)}), bf16[896,2432]{1,0:T(8,128)(2,1)}) %all-gather.2.cloned.1.call-update) | async-done | bytes 4358160 | tf_op jit(solution)/shard_map/all_gather | solution.py:26
  82.1 0.0 copy-done
  82.1 6.3 %fusion.18 = (f32[384]{0:T(512)S(1)}, f32[384,2432]{1,0:T(8,128)}) fusion(bf16[384,896]{1,0:T(8,128)(2,1)S(1)} %copy-done, bf16[896,2432]{1,0:T(8,128)(2,1)} %all-gather.2.cloned.1.call-done), kind=kOutput, calls=%fused_computation.45 | convolution fusion | flops 1675394688 | bytes 8783360 | tf_op jit(solution)/shard_map/dot_general | solution.py:27
  88.5 45.3 %all-reduce.3 = (f32[384]{0:T(512)S(1)}, f32[384]{0:T(512)S(1)}) all-reduce(f32[384]{0:T(512)S(1)} %get-tuple-element.31, f32[384]{0:T(512)S(1)} %fusion.1), channel_id=1, replica_groups=mesh['dp'=16,'vocab'=32] {'vocab'}, use_global_device_ids=true, to_apply=%region_1.0 | all-reduce | flops 768 | bytes 6144 | tf_op jit(solution)/shard_map/pmax | solution.py:32
  133.8 0.0 copy-done.1
  133.8 4.4 multiply_reduce_fusion.6
  138.2 90.0 %all-reduce.2 = (f32[384]{0:T(512)S(1)}, f32[384]{0:T(512)S(1)}, f32[384]{0:T(512)S(1)}, f32[384]{0:T(512)S(1)}, f32[384]{0:T(512)S(1)}) all-reduce(f32[384]{0:T(512)S(1)} %get-tuple-element.3, f32[384]{0:T(512)S(1)} %get-tuple-element.11, f32[384]{0:T(512)S(1)} %get-tuple-element.4, ...), channel_id=1, replica_groups=mesh['dp'=16,'vocab'=32] {'vocab'}, use_global_device_ids=true, to_apply=%region_3.0 | all-reduce | flops 1920 | bytes 15360 | tf_op jit(solution)/shard_map/psum | solution.py:35
  228.2 6.0 %multiply_reduce_fusion.1 = (f32[2432]{0:T(1024)S(1)}, f32[2432]{0:T(1024)S(1)}, f32[2432]{0:T(1024)S(1)}, f32[2432]{0:T(1024)S(1)}, f32[2432]{0:T(1024)S(1)}, /*index=5*/f32[384,2432]{1,0:T(8,128)}) fusion(f32[384]{0:T(512)S(1)} %get-tuple-element.17, f32[384]{0:T(512)S(1)} %get-tuple-element.22, bf16[384,2432]{1,0:T(8,128)(2,1)S(1)} %copy-done.1, ...), kind=kLoop, calls=%fused_computation.5 | loop fusion | flops 14930048 | bytes 9393664 | tf_op jit(solution)/shard_map/reduce_sum | solution.py:59
  234.3 0.1 stack.23
  234.4 59.2 %psum.54 = f32[5,2432]{1,0:T(8,128)S(1)} all-reduce(f32[5,2432]{1,0:T(8,128)S(1)} %stack.23), channel_id=1, replica_groups=mesh['dp'=16,'vocab'=32] {'dp'}, use_global_device_ids=true, to_apply=%region_19.0 | all-reduce | flops 12160 | bytes 97280 | tf_op jit(solution)/shard_map/psum | solution.py:52
  293.6 0.2 fusion.11
  293.8 6.0 %multiply_reduce_fusion = (f32[384]{0:T(512)S(1)}, f32[384,2432]{1,0:T(8,128)}) fusion(f32[384,2432]{1,0:T(8,128)} %get-tuple-element.25, f32[2432]{0:T(1024)S(1)} %get-tuple-element.13, f32[2432]{0:T(1024)S(1)} %get-tuple-element.12, f32[2432]{0:T(1024)S(1)} %get-tuple-element.15, f32[2432]{0:T(1024)S(1)} %get-tuple-element.14, ...), kind=kLoop, calls=%fused_computation.2 | loop fusion | flops 15875712 | bytes 9385472 | tf_op jit(solution)/shard_map/reduce_sum | solution.py:73
  299.7 59.9 %psum.55 = f32[384]{0:T(512)S(1)} all-reduce(f32[384]{0:T(512)S(1)} %get-tuple-element.23), channel_id=1, replica_groups=mesh['dp'=16,'vocab'=32] {'vocab'}, use_global_device_ids=true, to_apply=%region_21.0 | all-reduce | flops 384 | bytes 3072 | tf_op jit(solution)/shard_map/psum | solution.py:73
  359.6 4.3 multiply_convert_fusion
  363.9 0.0 copy-start.2
  363.9 6.5 %fusion.19 = f32[384,896]{0,1:T(8,128)} fusion(bf16[384,2432]{1,0:T(8,128)(2,1)S(1)} %multiply_convert_fusion, bf16[896,2432]{1,0:T(8,128)(2,1)} %all-gather.2.cloned.1.call-done), kind=kOutput, calls=%fused_computation.46 | convolution fusion | flops 1673527296 | bytes 7602176 | tf_op jit(solution)/shard_map/dot_general | solution.py:75
  370.4 54.7 %fusion = f32[384,32]{0,1:T(8,128)S(1)} fusion(f32[384,896]{0,1:T(8,128)} %fusion.19), kind=kCustom, calls=%all-reduce-scatter | all-reduce-scatter fusion | flops 393217 | bytes 1427456
  425.1 5.5 %collective-permute-start = (bf16[384,32]{0,1:T(8,128)(2,1)S(1)}, bf16[384,32]{0,1:T(8,128)(2,1)S(1)}, u32[]{:S(2)}, u32[]{:S(2)}) collective-permute-start(bf16[384,32]{0,1:T(8,128)(2,1)S(1)} %convert.6), channel_id=1, source_target_pairs={{0,1},{1,2},{2,3},{3,4},{4,5},{5,6},{6,7},{7,8},{8,9},{9,10},{10,1... | collective-permute-start | bytes 73736
  430.5 1.9 collective-permute-start.1
  432.5 1.9 collective-permute-start.2
  434.4 7.7 %collective-permute-start.3 = (bf16[384,28]{0,1:T(8,128)(2,1)S(1)}, bf16[384,28]{0,1:T(8,128)(2,1)S(1)}, u32[]{:S(2)}, u32[]{:S(2)}) collective-permute-start(bf16[384,28]{0,1:T(8,128)(2,1)S(1)} %slice.25), channel_id=1, source_target_pairs={{0,4},{1,5},{2,6},{3,7},{4,8},{5,9},{6,10},{7,11},{8,12},{9,13},{1... | collective-permute-start | bytes 64520
  442.1 1.3 dynamic-slice.4
  444.1 0.0 collective-permute-done.3
  444.1 0.0 collective-permute-done
  444.1 0.0 collective-permute-done.1
  444.1 0.0 collective-permute-done.2
  444.1 0.8 concatenate
  444.9 0.6 dynamic-slice_convert_fusion
  (11 shorter events, 0.1 us)
Async XLA Ops:
  7.2 75.0 %copy-start = (bf16[384,896]{1,0:T(8,128)(2,1)S(1)}, bf16[384,896]{1,0:T(8,128)(2,1)}, u32[]{:S(2)}) copy-start(bf16[384,896]{1,0:T(8,128)(2,1)} %param.3) | copy-start | bytes 2064388
  7.2 74.9 %all-gather.2.cloned.1.call-start = ((), (), s32[]{:S(2)}) async-start(), calls=%async_computation | async-start | bytes 4630528 | tf_op jit(solution)/shard_map/all_gather | solution.py:26
  9.9 123.9 %copy-start.1 = (bf16[384,2432]{1,0:T(8,128)(2,1)S(1)}, bf16[384,2432]{1,0:T(8,128)(2,1)}, u32[]{:S(2)}) copy-start(bf16[384,2432]{1,0:T(8,128)(2,1)} %param.5) | copy-start | bytes 5603332
  363.9 6.5 %copy-start.2 = (bf16[384,2432]{1,0:T(8,128)(2,1)}, bf16[384,2432]{1,0:T(8,128)(2,1)S(1)}, u32[]{:S(2)}) copy-start(bf16[384,2432]{1,0:T(8,128)(2,1)S(1)} %multiply_convert_fusion) | copy-start | bytes 5603332
  425.1 19.0 %collective-permute-start = (bf16[384,32]{0,1:T(8,128)(2,1)S(1)}, bf16[384,32]{0,1:T(8,128)(2,1)S(1)}, u32[]{:S(2)}, u32[]{:S(2)}) collective-permute-start(bf16[384,32]{0,1:T(8,128)(2,1)S(1)} %convert.6), channel_id=1, source_target_pairs={{0,1},{1,2},{2,3},{3,4},{4,5},{5,6},{6,7},{7,8},{8,9},{9,10},{10,1... | collective-permute-start | bytes 73736
  430.5 13.5 %collective-permute-start.1 = (bf16[384,32]{0,1:T(8,128)(2,1)S(1)}, bf16[384,32]{0,1:T(8,128)(2,1)S(1)}, u32[]{:S(2)}, u32[]{:S(2)}) collective-permute-start(bf16[384,32]{0,1:T(8,128)(2,1)S(1)} %convert.6), channel_id=1, source_target_pairs={{0,2},{1,3},{2,4},{3,5},{4,6},{5,7},{6,8},{7,9},{8,10},{9,11},{10,... | collective-permute-start | bytes 73736
  432.5 11.6 %collective-permute-start.2 = (bf16[384,32]{0,1:T(8,128)(2,1)S(1)}, bf16[384,32]{0,1:T(8,128)(2,1)S(1)}, u32[]{:S(2)}, u32[]{:S(2)}) collective-permute-start(bf16[384,32]{0,1:T(8,128)(2,1)S(1)} %convert.6), channel_id=1, source_target_pairs={{0,3},{1,4},{2,5},{3,6},{4,7},{5,8},{6,9},{7,10},{8,11},{9,12},{10... | collective-permute-start | bytes 73736
  434.4 9.6 %collective-permute-start.3 = (bf16[384,28]{0,1:T(8,128)(2,1)S(1)}, bf16[384,28]{0,1:T(8,128)(2,1)S(1)}, u32[]{:S(2)}, u32[]{:S(2)}) collective-permute-start(bf16[384,28]{0,1:T(8,128)(2,1)S(1)} %slice.25), channel_id=1, source_target_pairs={{0,4},{1,5},{2,6},{3,7},{4,8},{5,9},{6,10},{7,11},{8,12},{9,13},{1... | collective-permute-start | bytes 64520
Sparse Core Ops, SparseCore 0:
  11.1 70.9 all-gather.1
where the time goes:
time: 453 us; the launch traced here: 452 us
  blocking collectives  309 us (68%)
  waiting for transfers between devices  72.9 us (16%)
  other arithmetic  22.8 us (5%)
  starting transfers between devices  17 us (4%)
  between operations  14.9 us (3%)
  matrix products  12.8 us (3%)
    psum x1, blocking collectives, body(): lax.psum((jnp.sum(exp_student, 1), jnp.sum(exp_teacher, 1), jnp.sum(exp_s...  90 us
    all_gather x1, waiting for transfers between devices, body(): whole = lax.all_gather(head_weight, 'dp', axis=0, tiled=True)  72.2 us
    psum x1, blocking collectives, body(): row_dot = lax.psum(jnp.sum(prob_student * coeff, 1), 'vocab') / classes  59.9 us
    psum x1, blocking collectives, body(): lax.psum(jnp.stack([jnp.sum(prob_student, 0), jnp.sum(prob_teacher, 0), j...  59.2 us
    unnamed x1, blocking collectives  54.7 us
    pmax x1, blocking collectives, body(): peak_student, peak_teacher = lax.pmax((local_peak_s, local_peak_t), 'vocab')  45.3 us
    unnamed x4, starting transfers between devices  17 us
  transfers between devices with their start and end apart: 5, of which 1 were waited for; matrix products, arithmetic and copies ran while one was open for 1% of the time, Pallas kernels for 0%

commit v1 on v0

v1 whole, which is shorter than its diff:
```python
import jax
import jax.numpy as jnp
from jax import lax
from jax.sharding import PartitionSpec as P

TEMP = 4
EPS = 1e-06
SIDE = 4
CHIPS = 16
CORES = 2
DP = SIDE * SIDE
VOCAB = CHIPS * CORES
AXES = ("dp", "vocab")


def _plane_groups(flip):
    groups = []
    for z in range(CHIPS):
        for core in range(CORES):
            for other in range(SIDE):
                along_x = (core ^ flip) == 0
                groups.append(
                    [
                        ((i * SIDE + other) if along_x else (other * SIDE + i)) * VOCAB + z * CORES + core
                        for i in range(SIDE)
                    ]
                )
    return groups


FIRST, SECOND = _plane_groups(0), _plane_groups(1)
COLUMN = [[z * CORES + core for z in range(CHIPS)] for core in range(CORES)]
PAIR = [(i, i ^ 1) for i in range(VOCAB)]


def spread(block, count, axis, groups=None):
    copies = jnp.broadcast_to(block[None], (count,) + block.shape)
    return lax.all_to_all(copies, axis, 0, 0, tiled=True, axis_index_groups=groups)


def merge(parts):
    peak_s, peak_t = jnp.max(parts[:, 0], 0), jnp.max(parts[:, 1], 0)
    ws, wt = jnp.exp(parts[:, 0] - peak_s), jnp.exp(parts[:, 1] - peak_t)
    return jnp.stack(
        [
            peak_s,
            peak_t,
            jnp.sum(parts[:, 2] * ws, 0),
            jnp.sum(parts[:, 3] * wt, 0),
            jnp.sum(parts[:, 4] * (ws * ws), 0),
            jnp.sum(parts[:, 5] * (wt * wt), 0),
            jnp.sum(parts[:, 6] * (ws * wt), 0),
        ]
    )


def body(student_hidden, head_weight, teacher_logits):
    tok_rows, width = student_hidden.shape
    rows, vocab_cols = head_weight.shape
    classes = vocab_cols * VOCAB
    tokens = tok_rows * DP
    core = lax.axis_index("vocab") % CORES

    line = spread(head_weight, SIDE, AXES, FIRST).reshape(SIDE * rows, vocab_cols)
    whole = spread(line, SIDE, AXES, SECOND).reshape(DP * rows, vocab_cols)
    hid = student_hidden.reshape(tok_rows, SIDE, SIDE, rows)
    hid = jnp.where(core == 0, jnp.swapaxes(hid, 1, 2), hid).reshape(tok_rows, width)

    logits = jnp.dot(hid, whole, preferred_element_type=jnp.float32)
    scaled_student = logits / TEMP
    scaled_teacher = teacher_logits.astype(jnp.float32) / TEMP
    own_s = jnp.max(scaled_student, axis=1)
    own_t = jnp.max(scaled_teacher, axis=1)
    exp_s = jnp.exp(scaled_student - own_s[:, None])
    exp_t = jnp.exp(scaled_teacher - own_t[:, None])
    stats = jnp.stack(
        [
            own_s,
            own_t,
            jnp.sum(exp_s, 1),
            jnp.sum(exp_t, 1),
            jnp.sum(exp_s * exp_s, 1),
            jnp.sum(exp_t * exp_t, 1),
            jnp.sum(exp_s * exp_t, 1),
        ]
    )
    stats = merge(jnp.stack([stats, lax.ppermute(stats, "vocab", PAIR)]))
    stats = merge(spread(stats, CHIPS, "vocab", COLUMN))
    norm_s, norm_t = stats[2], stats[3]
    row_var = classes * stats[4] / (norm_s * norm_s) - 1.0
    row_var_t = classes * stats[5] / (norm_t * norm_t) - 1.0
    cross = classes * stats[6] / (norm_s * norm_t) - 1.0
    row_den = jnp.sqrt((row_var + EPS) * (row_var_t + EPS))
    row_rho = cross / row_den
    prob_s = exp_s * (classes * jnp.exp(own_s - stats[0]) / norm_s)[:, None]
    prob_t = exp_t * (classes * jnp.exp(own_t - stats[1]) / norm_t)[:, None]

    sums = jnp.stack(
        [
            jnp.sum(prob_s, 0),
            jnp.sum(prob_t, 0),
            jnp.sum(prob_s * prob_s, 0),
            jnp.sum(prob_t * prob_t, 0),
            jnp.sum(prob_s * prob_t, 0),
        ]
    )
    sums = jnp.sum(spread(sums, SIDE, AXES, FIRST), 0)
    sums = jnp.sum(spread(sums, SIDE, AXES, SECOND), 0)
    mean_s = sums[0] / tokens
    mean_t = sums[1] / tokens
    col_var = sums[2] / tokens - mean_s * mean_s
    col_var_t = sums[3] / tokens - mean_t * mean_t
    col_cov = sums[4] / tokens - mean_s * mean_t
    col_den = jnp.sqrt((col_var + EPS) * (col_var_t + EPS))
    col_rho = col_cov / col_den

    inner = prob_t / row_den[:, None] - (row_rho / (row_var + EPS))[:, None] * prob_s
    inner = inner + (prob_t - mean_t[None, :]) / col_den[None, :]
    inner = inner - (col_rho / (col_var + EPS))[None, :] * (prob_s - mean_s[None, :])
    coeff = -TEMP * inner
    row_dot = jnp.sum(prob_s * coeff, 1)
    row_dot = jnp.sum(spread(row_dot[None], VOCAB, "vocab"), (0, 1)) / classes
    logit_grad = (prob_s * (coeff - row_dot[:, None]) / TEMP).astype(jnp.bfloat16)

    part = lax.dot_general(
        whole, logit_grad, (((1,), (1,)), ((), ())), preferred_element_type=jnp.float32
    )
    part = part.reshape(SIDE, SIDE, rows, tok_rows)
    part = jnp.where(core == 0, jnp.swapaxes(part, 0, 1), part)
    part = part.reshape(DP, CORES, rows // CORES, tok_rows)
    low, high = part[:, 0], part[:, 1]
    keep = jnp.where(core == 0, low, high)
    send = jnp.where(core == 0, high, low)
    keep = keep + lax.ppermute(send, "vocab", PAIR)
    share = lax.all_to_all(
        keep.astype(jnp.bfloat16), "vocab", 0, 0, tiled=True, axis_index_groups=COLUMN
    )
    hidden_grad = jnp.sum(share.astype(jnp.float32), 0).T.astype(jnp.bfloat16)
    return (logit_grad, hidden_grad)


def solution(mesh):
    return jax.shard_map(
        body,
        mesh=mesh,
        in_specs=(P("dp", None), P("dp", "vocab"), P("dp", "vocab")),
        out_specs=(P("dp", "vocab"), P("dp", "vocab")),
        check_vma=False,
    )
```

time: 453 us -> 193 us (0.43)
  the two profiles are of different devices: /device:TPU:97 before, /device:TPU:2 now
where the time goes in v1:
time: 193 us; the launch traced here: 192 us
  blocking collectives  110 us (57%)
  waiting for transfers between devices  31 us (16%)
  other arithmetic  22.7 us (12%)
  local copies, waits for them, and re-layouts  9.14 us (5%)
  matrix products  8.95 us (5%)
  starting transfers between devices  8.85 us (5%)
    all_to_all x5, blocking collectives, spread(): lax.all_to_all(copies, axis, 0, 0, tiled=True, axis_index_groups=groups)  83.4 us
    all_to_all x1, waiting for transfers between devices, spread(): lax.all_to_all(copies, axis, 0, 0, tiled=True, axis_index_groups=groups)  27.8 us
    all_to_all x1, blocking collectives, body(): lax.all_to_all(keep.astype(jnp.bfloat16), 'vocab', 0, 0, tiled=True, axis...  27.1 us
    reduce_sum x1, other arithmetic, body(): row_dot = jnp.sum(prob_s * coeff, 1)  6.18 us
    all_to_all x1, starting transfers between devices, spread(): lax.all_to_all(copies, axis, 0, 0, tiled=True, axis_index_groups=groups)  5.01 us
    reduce_sum x1, other arithmetic, body(): jnp.sum(prob_s * prob_t, 0)  4.97 us
    convert_element_type x1, other arithmetic, body(): (prob_s * (coeff - row_dot[:, None]) / TEMP).astype(jnp.bfloat16)  4.85 us
    dot_general x1, matrix products, body(): logits = jnp.dot(hid, whole, preferred_element_type=jnp.float32)  4.54 us
  transfers between devices with their start and end apart: 3, of which 3 were waited for; matrix products, arithmetic and copies ran while one was open for 0% of the time, Pallas kernels for 0%

profile of v1, /device:TPU:2, one launch (start us, length us, event | category | flops | bytes accessed | tf_op | source)
XLA Modules:
  0.0 192.0 jit_solution(2787283096247882591)
XLA Ops:
  0.6 1.0 broadcast_in_dim.14
  1.7 18.0 %all_to_all.35 = bf16[4,56,2432]{2,1,0:T(8,128)(2,1)S(1)} all-to-all(bf16[4,56,2432]{2,1,0:T(8,128)(2,1)S(1)} %broadcast_in_dim.14), channel_id=1, replica_groups={{0,128,256,384},{32,160,288,416},{64,192,320,448},{96,224,352,480},{1,3..., dimensions={0} | all-to-all | bytes 2179072 | tf_op jit(solution)/shard_map/all_to_all | solution.py:38
  19.6 2.3 %broadcast_in_dim.16 = bf16[4,224,2432]{2,1,0:T(8,128)(2,1)} broadcast(bf16[224,2432]{1,0:T(8,128)(2,1)S(1)} %bitcast.121), dimensions={1,2} | broadcast | bytes 5447680 | tf_op jit(solution)/shard_map/broadcast_in_dim | solution.py:37
  22.0 5.0 %all-to-all-start.1 = ((bf16[4,224,2432]{2,1,0:T(8,128)(2,1)}), bf16[4,224,2432]{2,1,0:T(8,128)(2,1)}, u32[]{:S(2)}, u32[]{:S(2)}) async-start(bf16[4,224,2432]{2,1,0:T(8,128)(2,1)} %broadcast_in_dim.16), calls=%async_computation.1 | async-start | bytes 8716288 | tf_op jit(solution)/shard_map/all_to_all | solution.py:38
  27.0 0.4 fusion
  27.4 0.4 copy.65
  27.9 27.8 %all-to-all-done.1 = bf16[4,224,2432]{2,1,0:T(8,128)(2,1)} async-done(((bf16[4,224,2432]{2,1,0:T(8,128)(2,1)}), bf16[4,224,2432]{2,1,0:T(8,128)(2,1)}, u32[]{:S(2)}, u32[]{:S(2)}) %all-to-all-start.1) | async-done | bytes 4358176 | tf_op jit(solution)/shard_map/all_to_all | solution.py:38
  55.6 4.5 %fusion.48 = (f32[384]{0:T(512)S(1)}, f32[384,2432]{1,0:T(8,128)S(1)}) fusion(bf16[384,896]{0,1:T(8,128)(2,1)S(1)} %bitcast.120, bf16[896,2432]{1,0:T(8,128)(2,1)} %bitcast.4), kind=kOutput, calls=%fused_computation.108 | convolution fusion | flops 1675394688 | bytes 8783360 | tf_op jit(solution)/shard_map/dot_general | solution.py:69
  60.2 1.8 copy-done
  62.0 2.2 %multiply_reduce_fusion.4 = (f32[384]{0:T(512)S(1)}, f32[384]{0:T(512)S(1)}, f32[384]{0:T(512)S(1)}, f32[384]{0:T(512)S(1)}, f32[384]{0:T(512)S(1)}) fusion(bf16[384,2432]{1,0:T(8,128)(2,1)S(1)} %copy-done.1, f32[384]{0:T(512)S(1)} %fusion, f32[384,2432]{1,0:T(8,128)S(1)} %get-tuple-element.50, f32[384]{0:T(512)S(1)} %get-tuple-element.49), kind=kLoop, calls=%fused_computation.8 | loop fusion | flops 11204736 | bytes 5614080 | tf_op jit(solution)/shard_map/reduce_sum | solution.py:84
  64.3 1.9 %collective-permute-start = (f32[7,384]{1,0:T(8,128)S(1)}, f32[7,384]{1,0:T(8,128)S(1)}, u32[]{:S(2)}, u32[]{:S(2)}) collective-permute-start(f32[7,384]{1,0:T(8,128)S(1)} %stack.82), channel_id=1, source_target_pairs={{0,1},{1,0},{2,3},{3,2},{4,5},{5,4},{6,7},{7,6},{8,9},{9,8},{10,11... | collective-permute-start | bytes 32264 | tf_op jit(solution)/shard_map/ppermute | solution.py:87
  66.2 1.1 collective-permute-done
  67.6 26.9 %all_to_all.36 = f32[16,7,384]{2,1,0:T(8,128)S(1)} all-to-all(f32[16,7,384]{2,1,0:T(8,128)S(1)} %broadcast_in_dim.17), channel_id=1, replica_groups={{0,2,4,6,8,10,12,14,16,18,20,22,24,26,28,30},{1,3,5,7,9,11,13,15,17,19,..., dimensions={0} | all-to-all | bytes 344064 | tf_op jit(solution)/shard_map/all_to_all | solution.py:38
  94.5 0.1 slice_reduce_fusion
  94.7 5.0 %multiply_reduce_fusion.1 = (f32[2432]{0:T(1024)S(1)}, f32[2432]{0:T(1024)S(1)}, f32[2432]{0:T(1024)S(1)}, f32[2432]{0:T(1024)S(1)}, f32[2432]{0:T(1024)S(1)}) fusion(bf16[384,2432]{1,0:T(8,128)(2,1)S(1)} %copy-done.1, f32[384]{0:T(512)S(1)} %get-tuple-element.47, f32[384]{0:T(512)S(1)} %get-tuple-element.48, f32[384]{0:T(512)S(1)} %fusion, ...), kind=kLoop, calls=%fused_computation.5 | loop fusion | flops 13062272 | bytes 5658112 | tf_op jit(solution)/shard_map/reduce_sum | solution.py:104
  99.9 9.3 %all_to_all.37 = f32[4,5,2432]{2,1,0:T(8,128)S(1)} all-to-all(f32[4,5,2432]{2,1,0:T(8,128)S(1)} %broadcast_in_dim.18), channel_id=1, replica_groups={{0,128,256,384},{32,160,288,416},{64,192,320,448},{96,224,352,480},{1,3..., dimensions={0} | all-to-all | bytes 389120 | tf_op jit(solution)/shard_map/all_to_all | solution.py:38
  109.2 9.3 %all_to_all.38 = f32[4,5,2432]{2,1,0:T(8,128)S(1)} all-to-all(f32[4,5,2432]{2,1,0:T(8,128)S(1)} %broadcast_in_dim.19), channel_id=1, replica_groups={{0,32,64,96},{128,160,192,224},{256,288,320,352},{384,416,448,480},{1,1..., dimensions={0} | all-to-all | bytes 389120 | tf_op jit(solution)/shard_map/all_to_all | solution.py:38
  118.6 0.2 fusion.23
  118.7 6.2 %multiply_reduce_fusion = (f32[384]{0:T(512)S(1)}, f32[384,2432]{1,0:T(8,128)}) fusion(f32[2432]{0:T(1024)S(1)} %get-tuple-element.15, f32[2432]{0:T(1024)S(1)} %get-tuple-element.14, f32[384]{0:T(512)S(1)} %get-tuple-element.48, f32[384,2432]{1,0:T(8,128)} %copy-done, f32[384]{0:T(512)S(1)} %get-tuple-element.49, f32[2432]{0:T(1024)S(1)} %get-tuple-element.27, ...), kind=kLoop, calls=%fused_computation.2 | loop fusion | flops 16809600 | bytes 9388544 | tf_op jit(solution)/shard_map/reduce_sum | solution.py:121
  125.0 19.9 %all_to_all.39 = f32[32,1,384]{2,1,0:T(1,128)S(1)} all-to-all(f32[32,1,384]{2,1,0:T(1,128)S(1)} %broadcast_in_dim.20), channel_id=1, replica_groups=mesh['dp'=16,'vocab'=32] {'vocab'}, dimensions={0} | all-to-all | bytes 98304 | tf_op jit(solution)/shard_map/all_to_all | solution.py:38
  144.9 4.9 %multiply_convert_fusion = bf16[384,2432]{1,0:T(8,128)(2,1)S(1)} fusion(f32[384,2432]{1,0:T(8,128)} %get-tuple-element.29, f32[384]{0:T(512)S(1)} %broadcast_multiply_fusion, f32[2432]{0:T(1024)S(1)} %get-tuple-element.15, f32[2432]{0:T(1024)S(1)} %get-tuple-element.14, f32[384]{0:T(512)S(1)} %get-tuple-element.48, f32[384,2432]{1,0:T(8,128)} %copy-done, ...), kind=kLoop, calls=%fused_computation.1 | loop fusion | flops 9338880 | bytes 9362944 | tf_op jit(solution)/shard_map/convert_element_type | solution.py:123
  149.8 1.2 copy-done.2
  151.0 4.4 %convolution_bitcast_fusion = f32[896,384]{0,1:T(8,128)S(1)} fusion(bf16[384,2432]{1,0:T(8,128)(2,1)S(1)} %multiply_convert_fusion, bf16[896,2432]{1,0:T(8,128)(2,1)} %bitcast.4), kind=kOutput, calls=%fused_computation.19 | convolution fusion | flops 1673527296 | bytes 7602176 | tf_op jit(solution)/shard_map/dot_general | solution.py:125
  155.5 0.4 copy.77
  155.9 1.2 bitcast_select_fusion
  157.1 1.4 reshape.99
  158.6 0.8 select_bitcast_fusion
  159.4 1.9 %collective-permute-start.1 = (f32[16,28,384]{2,0,1:T(8,128)S(1)}, f32[16,28,384]{2,0,1:T(8,128)S(1)}, u32[]{:S(2)}, u32[]{:S(2)}) collective-permute-start(f32[16,28,384]{2,0,1:T(8,128)S(1)} %select_bitcast_fusion), channel_id=1, source_target_pairs={{0,1},{1,0},{2,3},{3,2},{4,5},{5,4},{6,7},{7,6},{8,9},{9,8},{10,11... | collective-permute-start | bytes 2064392 | tf_op jit(solution)/shard_map/ppermute | solution.py:134
  161.3 2.1 %collective-permute-done.1 = f32[16,28,384]{2,0,1:T(8,128)S(1)} collective-permute-done((f32[16,28,384]{2,0,1:T(8,128)S(1)}, f32[16,28,384]{2,0,1:T(8,128)S(1)}, u32[]{:S(2)}, u32[]{:S(2)}) %collective-permute-start.1) | collective-permute-done | bytes 688160 | tf_op jit(solution)/shard_map/ppermute | solution.py:134
  163.4 0.8 fusion.4
  164.3 27.1 %all_to_all.40 = bf16[16,28,384]{2,1,0:T(8,128)(2,1)S(1)} all-to-all(bf16[16,28,384]{2,1,0:T(8,128)(2,1)S(1)} %copy.80), channel_id=1, replica_groups={{0,2,4,6,8,10,12,14,16,18,20,22,24,26,28,30},{1,3,5,7,9,11,13,15,17,19,..., dimensions={0} | all-to-all | bytes 688128 | tf_op jit(solution)/shard_map/all_to_all | solution.py:135
  191.4 0.7 reduce_sum.252
  (45 shorter events, 0.9 us)
Async XLA Ops:
  21.9 5.0 %copy-start.1 = (bf16[384,2432]{1,0:T(8,128)(2,1)S(1)}, bf16[384,2432]{1,0:T(8,128)(2,1)}, u32[]{:S(2)}) copy-start(bf16[384,2432]{1,0:T(8,128)(2,1)} %param.5) | copy-start | bytes 5603332
  22.0 5.5 %copy-start.3 = (bf16[384,896]{1,0:T(8,128)(2,1)S(1)}, bf16[384,896]{1,0:T(8,128)(2,1)}, u32[]{:S(2)}) copy-start(bf16[384,896]{1,0:T(8,128)(2,1)} %param.3) | copy-start | bytes 2064388
  22.0 33.7 %all-to-all-start.1 = ((bf16[4,224,2432]{2,1,0:T(8,128)(2,1)}), bf16[4,224,2432]{2,1,0:T(8,128)(2,1)}, u32[]{:S(2)}, u32[]{:S(2)}) async-start(bf16[4,224,2432]{2,1,0:T(8,128)(2,1)} %broadcast_in_dim.16), calls=%async_computation.1 | async-start | bytes 8716288 | tf_op jit(solution)/shard_map/all_to_all | solution.py:38
  60.2 1.8 copy-start
  64.3 3.1 %collective-permute-start = (f32[7,384]{1,0:T(8,128)S(1)}, f32[7,384]{1,0:T(8,128)S(1)}, u32[]{:S(2)}, u32[]{:S(2)}) collective-permute-start(f32[7,384]{1,0:T(8,128)S(1)} %stack.82), channel_id=1, source_target_pairs={{0,1},{1,0},{2,3},{3,2},{4,5},{5,4},{6,7},{7,6},{8,9},{9,8},{10,11... | collective-permute-start | bytes 32264 | tf_op jit(solution)/shard_map/ppermute | solution.py:87
  149.8 1.2 copy-start.2
  159.4 4.0 %collective-permute-start.1 = (f32[16,28,384]{2,0,1:T(8,128)S(1)}, f32[16,28,384]{2,0,1:T(8,128)S(1)}, u32[]{:S(2)}, u32[]{:S(2)}) collective-permute-start(f32[16,28,384]{2,0,1:T(8,128)S(1)} %select_bitcast_fusion), channel_id=1, source_target_pairs={{0,1},{1,0},{2,3},{3,2},{4,5},{5,4},{6,7},{7,6},{8,9},{9,8},{10,11... | collective-permute-start | bytes 2064392 | tf_op jit(solution)/shard_map/ppermute | solution.py:134

commit v2 on v1

v2 whole, which is shorter than its diff:
```python
import jax
import jax.numpy as jnp
from jax import lax
from jax.experimental import pallas as pl
from jax.experimental.pallas import tpu as pltpu
from jax.sharding import PartitionSpec as P

TEMP = 4
EPS = 1e-06
SIDE = 4
CHIPS = 16
CORES = 2
DP = SIDE * SIDE
VOCAB = CHIPS * CORES
AXES = ("dp", "vocab")
TILE = 128
GRANT = 22 * 1024 * 1024
F32, BF16 = jnp.float32, jnp.bfloat16


def _plane_groups(flip):
    groups = []
    for z in range(CHIPS):
        for core in range(CORES):
            for other in range(SIDE):
                along_x = (core ^ flip) == 0
                groups.append(
                    [
                        ((i * SIDE + other) if along_x else (other * SIDE + i)) * VOCAB + z * CORES + core
                        for i in range(SIDE)
                    ]
                )
    return groups


FIRST, SECOND = _plane_groups(0), _plane_groups(1)
COLUMN = [[z * CORES + core for z in range(CHIPS)] for core in range(CORES)]
PAIR = [(i, i ^ 1) for i in range(VOCAB)]


def spread(block, count, axis, groups=None):
    copies = jnp.broadcast_to(block[None], (count,) + block.shape)
    return lax.all_to_all(copies, axis, 0, 0, tiled=True, axis_index_groups=groups)


def _chunks(total, size):
    return [(at, min(at + size, total)) for at in range(0, total, size)]


def _rows(i, size):
    return pl.ds(pl.multiple_of(i * size, size), size)


def _loop(count, step, unroll):
    lax.fori_loop(0, count, lambda i, c: (step(i), c)[1], 0, unroll=unroll)


def _place(lane, *values):
    out = jnp.zeros(lane.shape, F32)
    for k, v in enumerate(values):
        out = jnp.where(lane == k, v, out)
    return out


def teacher_kernel(t_ref, e_ref, stat_ref, cols):
    lane = lax.broadcasted_iota(jnp.int32, (16, TILE), 1)

    def step(i):
        rows = _rows(i, 16)
        x = t_ref[rows, :].astype(F32) * (1.0 / TEMP)
        peak = jnp.max(x, axis=1, keepdims=True)
        e = jnp.exp(x - peak)
        e_ref[rows, :] = e
        cols[rows, :] = _place(
            lane, peak, jnp.sum(e, axis=1, keepdims=True), jnp.sum(e * e, axis=1, keepdims=True)
        )

    _loop(TILE // 16, step, 2)
    stat_ref[...] = cols[...].T[:8]


def student_kernel(h_ref, w_ref, et_ref, tstat_ref, e_ref, stat_ref, cols):
    width = w_ref.shape[1]
    lane = lax.broadcasted_iota(jnp.int32, (8, TILE), 1)
    for lo, hi in _chunks(width, 640):
        e_ref[:, lo:hi] = jnp.dot(
            h_ref[...], w_ref[:, lo:hi], preferred_element_type=F32
        ) * (1.0 / TEMP)

    def step(i):
        rows = _rows(i, 8)
        x = e_ref[rows, :]
        peak = jnp.max(x, axis=1, keepdims=True)
        e = jnp.exp(x - peak)
        e_ref[rows, :] = e
        cols[rows, :] = _place(
            lane,
            peak,
            jnp.sum(e, axis=1, keepdims=True),
            jnp.sum(e * e, axis=1, keepdims=True),
            jnp.sum(e * et_ref[rows, :], axis=1, keepdims=True),
        )

    _loop(TILE // 8, step, 4)
    mine = cols[...].T
    other = tstat_ref[...]
    stat_ref[0:1] = mine[0:1]
    stat_ref[1:2] = other[0:1]
    stat_ref[2:3] = mine[1:2]
    stat_ref[3:4] = other[1:2]
    stat_ref[4:5] = mine[2:3]
    stat_ref[5:6] = other[2:3]
    stat_ref[6:7] = mine[3:4]
    stat_ref[7:8] = jnp.zeros((1, TILE), F32)


def column_kernel(classes, es_ref, et_ref, own_ref, all_ref, sums_ref, terms_ref, acc, side):
    at = pl.program_id(0)
    parts = [all_ref[:, k, :] for k in range(7)]
    peak_s = jnp.max(parts[0], axis=0, keepdims=True)
    peak_t = jnp.max(parts[1], axis=0, keepdims=True)
    ws, wt = jnp.exp(parts[0] - peak_s), jnp.exp(parts[1] - peak_t)
    norm_s = jnp.sum(parts[2] * ws, axis=0, keepdims=True)
    norm_t = jnp.sum(parts[3] * wt, axis=0, keepdims=True)
    square_s = jnp.sum(parts[4] * (ws * ws), axis=0, keepdims=True)
    square_t = jnp.sum(parts[5] * (wt * wt), axis=0, keepdims=True)
    cross = jnp.sum(parts[6] * (ws * wt), axis=0, keepdims=True)
    row_var = classes * square_s / (norm_s * norm_s) - 1.0
    row_var_t = classes * square_t / (norm_t * norm_t) - 1.0
    row_den = jnp.sqrt((row_var + EPS) * (row_var_t + EPS))
    row_rho = (classes * cross / (norm_s * norm_t) - 1.0) / row_den
    side[0:1] = classes * jnp.exp(own_ref[0:1] - peak_s) / norm_s
    side[1:2] = classes * jnp.exp(own_ref[1:2] - peak_t) / norm_t
    side[2:3] = 1.0 / row_den
    side[3:4] = row_rho / (row_var + EPS)
    side[4:] = jnp.zeros((TILE - 4, TILE), F32)
    terms_ref[...] = side[...].T

    @pl.when(at == 0)
    def _():
        acc[...] = jnp.zeros_like(acc)

    for lo, hi in _chunks(es_ref.shape[1], 640):

        def step(i, carry, lo=lo, hi=hi):
            rows = _rows(i, 8)
            qs = es_ref[rows, lo:hi] * terms_ref[rows, 0:1]
            qt = et_ref[rows, lo:hi] * terms_ref[rows, 1:2]
            s, t, ss, tt, st = carry
            return (s + qs, t + qt, ss + qs * qs, tt + qt * qt, st + qs * qt)

        carry = tuple(acc[k, :, lo:hi] for k in range(5))
        carry = lax.fori_loop(0, TILE // 8, step, carry, unroll=4)
        for k in range(5):
            acc[k, :, lo:hi] = carry[k]

    @pl.when(at == pl.num_programs(0) - 1)
    def _():
        for k in range(5):
            total = jnp.sum(acc[k], axis=0, keepdims=True)
            for copy in range(SIDE):
                sums_ref[copy, k : k + 1, :] = total


def coefficient_kernel(
    tokens, es_ref, et_ref, terms_ref, sums_ref, g_ref, dots_ref, lines_ref, copies_ref, coef
):
    lane = lax.broadcasted_iota(jnp.int32, (8, TILE), 1)

    @pl.when(pl.program_id(0) == 0)
    def _():
        sums = [jnp.sum(sums_ref[:, k, :], axis=0, keepdims=True) / tokens for k in range(5)]
        mean_s, mean_t = sums[0], sums[1]
        var_s = sums[2] - mean_s * mean_s
        var_t = sums[3] - mean_t * mean_t
        den = jnp.sqrt((var_s + EPS) * (var_t + EPS))
        rho = (sums[4] - mean_s * mean_t) / den
        for k, v in enumerate((mean_s, mean_t, 1.0 / den, rho / (var_s + EPS))):
            coef[k] = jnp.broadcast_to(v, coef.shape[1:])

    def step(i):
        rows = _rows(i, 8)
        qs = es_ref[rows, :] * terms_ref[rows, 0:1]
        qt = et_ref[rows, :] * terms_ref[rows, 1:2]
        inner = qt * terms_ref[rows, 2:3] - qs * terms_ref[rows, 3:4]
        inner = inner + (qt - coef[1]) * coef[2] - (qs - coef[0]) * coef[3]
        g = -TEMP * inner
        g_ref[rows, :] = g
        dot = jnp.sum(qs * g, axis=1, keepdims=True)
        mass = jnp.sum(qs, axis=1, keepdims=True)
        dots_ref[rows, :] = _place(lane, dot, dot / jnp.maximum(mass, 1e-30))

    _loop(TILE // 8, step, 4)
    lines_ref[...] = dots_ref[...].T[:8]
    copies_ref[...] = jnp.broadcast_to(lines_ref[0:1].reshape(1, 1, TILE), copies_ref.shape)


def product_kernel(place_ref, es_ref, g_ref, terms_ref, dots_ref, w_ref, out_ref, left, res):
    def step(i):
        rows = _rows(i, 16)
        qs = es_ref[rows, :] * terms_ref[rows, 0:1]
        left[rows, :] = (qs * (g_ref[rows, :] - dots_ref[rows, 1:2]) * (1.0 / TEMP)).astype(BF16)
        left[pl.ds(pl.multiple_of(TILE + i * 16, 16), 16), :] = (qs * (1.0 / TEMP)).astype(BF16)

    _loop(TILE // 16, step, 2)
    res[...] = lax.dot_general(
        w_ref[...], left[...], (((1,), (1,)), ((), ())), preferred_element_type=F32
    )
    half = out_ref.shape[3]
    for j in range(DP):
        for core in range(CORES):
            lo = (j * CORES + core) * half
            away = (place_ref[DP] + core) % CORES
            for k in range(2):
                out_ref[k, away, place_ref[j]] = res[lo : lo + half, k * TILE : (k + 1) * TILE]


def pair_kernel(own_ref, other_ref, out_ref):
    a = [own_ref[k : k + 1] for k in range(7)]
    b = [other_ref[k : k + 1] for k in range(7)]
    peak_s, peak_t = jnp.maximum(a[0], b[0]), jnp.maximum(a[1], b[1])
    as_, bs = jnp.exp(a[0] - peak_s), jnp.exp(b[0] - peak_s)
    at, bt = jnp.exp(a[1] - peak_t), jnp.exp(b[1] - peak_t)
    both = (
        peak_s,
        peak_t,
        a[2] * as_ + b[2] * bs,
        a[3] * at + b[3] * bt,
        a[4] * (as_ * as_) + b[4] * (bs * bs),
        a[5] * (at * at) + b[5] * (bt * bt),
        a[6] * (as_ * at) + b[6] * (bs * bt),
        jnp.zeros_like(peak_s),
    )
    for k, v in enumerate(both):
        out_ref[:, k, :] = jnp.broadcast_to(v, (out_ref.shape[0], v.shape[1]))


def middle_kernel(parts_ref, out_ref):
    total = jnp.sum(parts_ref[...], axis=0)
    for k in range(out_ref.shape[0]):
        out_ref[k] = total


def shift_kernel(classes, products_ref, lines_ref, shares_ref, keep_ref, send_ref):
    total = jnp.sum(shares_ref[:, 0, :], axis=0, keepdims=True) / classes
    shift = lines_ref[1:2] - total
    for j in range(keep_ref.shape[0]):
        keep_ref[j] = products_ref[0, 0, j] + shift * products_ref[1, 0, j]
        send_ref[j] = products_ref[0, 1, j] + shift * products_ref[1, 1, j]


def add_kernel(a_ref, b_ref, out_ref):
    for j in range(out_ref.shape[0]):
        out_ref[j] = (a_ref[j] + b_ref[j]).astype(BF16)


def last_kernel(share_ref, out_ref):
    total = share_ref[0].astype(F32)
    for j in range(1, share_ref.shape[0]):
        total = total + share_ref[j].astype(F32)
    out_ref[...] = total


def gradient_kernel(classes, es_ref, g_ref, terms_ref, dots_ref, out_ref, side):
    total = jnp.sum(dots_ref[:, 0, :], axis=0, keepdims=True) / classes
    side[...] = jnp.broadcast_to(total, (TILE, TILE)).T

    def step(i):
        rows = _rows(i, 16)
        qs = es_ref[rows, :] * terms_ref[rows, 0:1]
        out_ref[rows, :] = (qs * (g_ref[rows, :] - side[rows, 0:1]) * (1.0 / TEMP)).astype(BF16)

    _loop(TILE // 16, step, 2)


def _call(kernel, steps, in_specs, out_specs, out_shape, scratch, flops, nbytes):
    return pl.pallas_call(
        kernel,
        grid=(steps,),
        in_specs=in_specs,
        out_specs=out_specs,
        out_shape=out_shape,
        scratch_shapes=scratch,
        compiler_params=pltpu.CompilerParams(
            dimension_semantics=("arbitrary",), vmem_limit_bytes=GRANT
        ),
        cost_estimate=pl.CostEstimate(flops=flops, bytes_accessed=nbytes, transcendentals=0),
    )


def _small(kernel, out_shape, *args):
    return pl.pallas_call(
        kernel,
        out_shape=out_shape,
        compiler_params=pltpu.CompilerParams(vmem_limit_bytes=GRANT),
        cost_estimate=pl.CostEstimate(flops=1000000, bytes_accessed=4000000, transcendentals=0),
    )(*args)


def body(student_hidden, head_weight, teacher_logits):
    tok, width = student_hidden.shape
    rows, cols = head_weight.shape
    classes = cols * VOCAB
    tokens = tok * DP
    steps = tok // TILE
    half = rows // CORES
    core = lax.axis_index("vocab") % CORES

    tile = pl.BlockSpec((TILE, cols), lambda i: (i, 0))
    strip = pl.BlockSpec((8, TILE), lambda i: (0, i))
    side = pl.BlockSpec((TILE, TILE), lambda i: (i, 0))
    whole_w = pl.BlockSpec((width, cols), lambda i: (0, 0), pipeline_mode=pl.Buffered(1))
    full = jax.ShapeDtypeStruct((tok, cols), F32)
    flat = jax.ShapeDtypeStruct((8, tok), F32)
    tall = jax.ShapeDtypeStruct((tok, TILE), F32)
    small = pltpu.VMEM((TILE, TILE), F32)
    area = tok * cols

    line = spread(head_weight, SIDE, AXES, FIRST).reshape(SIDE * rows, cols)
    whole = spread(line, SIDE, AXES, SECOND).reshape(width, cols)
    hid = student_hidden.reshape(tok, SIDE, SIDE, rows)
    hid = jnp.where(core == 0, jnp.swapaxes(hid, 1, 2), hid).reshape(tok, width)

    exp_t, stat_t = _call(
        teacher_kernel, steps, [tile], [tile, strip], [full, flat], [small], 8 * area, 6 * area
    )(teacher_logits)
    exp_s, stats = _call(
        student_kernel,
        steps,
        [pl.BlockSpec((TILE, width), lambda i: (i, 0)), whole_w, tile, strip],
        [tile, strip],
        [full, flat],
        [small],
        2 * area * width,
        8 * area,
    )(hid, whole, exp_t, stat_t)

    pair = _small(
        pair_kernel,
        jax.ShapeDtypeStruct((CHIPS, 8, tok), F32),
        stats,
        lax.ppermute(stats, "vocab", PAIR),
    )
    everyone = lax.all_to_all(pair, "vocab", 0, 0, tiled=True, axis_index_groups=COLUMN)
    sums, terms = _call(
        lambda *refs: column_kernel(classes, *refs),
        steps,
        [tile, tile, strip, pl.BlockSpec((CHIPS, 8, TILE), lambda i: (0, 0, i))],
        [pl.BlockSpec((SIDE, 5, cols), lambda i: (0, 0, 0)), side],
        [jax.ShapeDtypeStruct((SIDE, 5, cols), F32), tall],
        [pltpu.VMEM((5, 8, cols), F32), small],
        10 * area,
        8 * area,
    )(exp_s, exp_t, stats, everyone)

    sums = lax.all_to_all(sums, AXES, 0, 0, tiled=True, axis_index_groups=FIRST)
    sums = _small(middle_kernel, jax.ShapeDtypeStruct(sums.shape, F32), sums)
    sums = lax.all_to_all(sums, AXES, 0, 0, tiled=True, axis_index_groups=SECOND)
    coeff, dots, lines, copies = _call(
        lambda *refs: coefficient_kernel(tokens, *refs),
        steps,
        [tile, tile, side, pl.BlockSpec((SIDE, 5, cols), lambda i: (0, 0, 0))],
        [tile, side, strip, pl.BlockSpec((VOCAB, 1, TILE), lambda i: (0, 0, i))],
        [full, tall, flat, jax.ShapeDtypeStruct((VOCAB, 1, tok), F32)],
        [pltpu.VMEM((4, 8, cols), F32)],
        14 * area,
        12 * area,
    )(exp_s, exp_t, terms, sums)

    shares = lax.all_to_all(copies, "vocab", 0, 0, tiled=True)
    slot = jnp.arange(DP, dtype=jnp.int32)
    slot = jnp.where(core == 0, (slot % SIDE) * SIDE + slot // SIDE, slot)
    slot = jnp.concatenate([slot, core.astype(jnp.int32)[None]])
    products = _call(
        product_kernel,
        steps,
        [pl.BlockSpec(memory_space=pltpu.SMEM), tile, tile, side, side, whole_w],
        pl.BlockSpec((2, CORES, DP, half, TILE), lambda i: (0, 0, 0, 0, i)),
        jax.ShapeDtypeStruct((2, CORES, DP, half, tok), F32),
        [pltpu.VMEM((2 * TILE, cols), BF16), pltpu.VMEM((width, 2 * TILE), F32)],
        4 * area * width,
        16 * area,
    )(slot, exp_s, coeff, terms, dots, whole)
    piece = jax.ShapeDtypeStruct((DP, half, tok), F32)
    keep, send = _small(
        lambda *refs: shift_kernel(classes, *refs), [piece, piece], products, lines, shares
    )
    share = _small(
        add_kernel,
        jax.ShapeDtypeStruct((DP, half, tok), BF16),
        keep,
        lax.ppermute(send, "vocab", PAIR),
    )
    share = lax.all_to_all(share, "vocab", 0, 0, tiled=True, axis_index_groups=COLUMN)
    logit_grad = _call(
        lambda *refs: gradient_kernel(classes, *refs),
        steps,
        [tile, tile, side, pl.BlockSpec((VOCAB, 1, TILE), lambda i: (0, 0, i))],
        tile,
        jax.ShapeDtypeStruct((tok, cols), BF16),
        [small],
        4 * area,
        10 * area,
    )(exp_s, coeff, terms, shares)
    hidden_grad = _small(last_kernel, jax.ShapeDtypeStruct((half, tok), F32), share)
    return (logit_grad, hidden_grad.T.astype(BF16))


def solution(mesh):
    return jax.shard_map(
        body,
        mesh=mesh,
        in_specs=(P("dp", None), P("dp", "vocab"), P("dp", "vocab")),
        out_specs=(P("dp", "vocab"), P("dp", "vocab")),
        check_vma=False,
    )
```

time: 193 us -> 201 us (1.041)
  blocking collectives: 110 us -> 54.2 us
  Pallas kernels: 0 us -> 38.6 us
  other arithmetic: 22.7 us -> 0.78 us
  starting transfers between devices: 8.85 us -> 30.3 us
  waiting for transfers between devices: 31 us -> 50 us
  local copies, waits for them, and re-layouts: 9.14 us -> 25.1 us
  matrix products: 8.95 us -> 0 us
    all_to_all x5 -> x1, blocking collectives: 83.4 us -> 18 us  [spread(): lax.all_to_all(copies, axis, 0, 0, tiled=True, axis_index_groups=groups)]
    pallas_call x0 -> x11, Pallas kernels: none -> 38.6 us  [the longest x1 11.4 us: body(): _call(student_kernel, steps, [pl.BlockSpec((TILE, width), lambda i: (i, 0...]
    all_to_all x0 -> x3, waiting for transfers between devices: none -> 24.4 us  [the longest x1 17.3 us: body(): lax.all_to_all(share, 'vocab', 0, 0, tiled=True, axis_index_groups=COLUMN)]
    all_to_all x0 -> x3, starting transfers between devices: none -> 21.5 us  [the longest x1 11.6 us: body(): lax.all_to_all(share, 'vocab', 0, 0, tiled=True, axis_index_groups=COLUMN)]
    unnamed x9 -> x31, local copies, waits for them, and re-layouts: 3.41 us -> 20.7 us
    reduce_sum x9 -> x0, other arithmetic: 14.2 us -> none  [the longest x1 6.18 us: body(): row_dot = jnp.sum(prob_s * coeff, 1)]
    all_to_all x1 -> x2, blocking collectives: 27.1 us -> 36.2 us  [the longest x1 26.9 us: body(): lax.all_to_all(pair, 'vocab', 0, 0, tiled=True, axis_index_groups=COLUMN)]
    dot_general x2 -> x0, matrix products: 8.95 us -> none  [the longest x1 4.54 us: body(): logits = jnp.dot(hid, whole, preferred_element_type=jnp.float32)]
  transfers between devices with their start and end apart: 3 -> 6, of which waited for: 3 -> 6; matrix products, arithmetic and copies ran while one was open for 0% -> 0% of each run, Pallas kernels for 0% -> 7%
where the time goes in v2:
time: 201 us; the launch traced here: 200 us
  blocking collectives  54.2 us (27%)
  waiting for transfers between devices  50 us (25%)
  Pallas kernels  38.6 us (19%)
  starting transfers between devices  30.3 us (15%)
  local copies, waits for them, and re-layouts  25.1 us (12%)
    all_to_all x1, blocking collectives, body(): lax.all_to_all(pair, 'vocab', 0, 0, tiled=True, axis_index_groups=COLUMN)  26.9 us
    all_to_all x1, waiting for transfers between devices, spread(): lax.all_to_all(copies, axis, 0, 0, tiled=True, axis_index_groups=groups)  22.3 us
    unnamed x31, local copies, waits for them, and re-layouts  20.7 us
    all_to_all x1, blocking collectives, spread(): lax.all_to_all(copies, axis, 0, 0, tiled=True, axis_index_groups=groups)  18 us
    all_to_all x1, waiting for transfers between devices, body(): lax.all_to_all(share, 'vocab', 0, 0, tiled=True, axis_index_groups=COLUMN)  17.3 us
    all_to_all x1, starting transfers between devices, body(): lax.all_to_all(share, 'vocab', 0, 0, tiled=True, axis_index_groups=COLUMN)  11.6 us
    pallas_call x1, Pallas kernels, body(): _call(student_kernel, steps, [pl.BlockSpec((TILE, width), lambda i: (i, 0...  11.4 us
    all_to_all x1, blocking collectives, body(): sums = lax.all_to_all(sums, AXES, 0, 0, tiled=True, axis_index_groups=FIRST)  9.32 us
  transfers between devices with their start and end apart: 6, of which 6 were waited for; matrix products, arithmetic and copies ran while one was open for 0% of the time, Pallas kernels for 7%

profile of v2, /device:TPU:2, one launch (start us, length us, event | category | flops | bytes accessed | tf_op | source)
XLA Modules:
  0.0 199.7 jit_solution(1823884786745001057)
XLA Ops:
  0.6 1.0 broadcast_in_dim.16
  1.7 18.0 %all_to_all.35 = bf16[4,56,2432]{2,1,0:T(8,128)(2,1)S(1)} all-to-all(bf16[4,56,2432]{2,1,0:T(8,128)(2,1)S(1)} %broadcast_in_dim.16), channel_id=1, replica_groups={{0,128,256,384},{32,160,288,416},{64,192,320,448},{96,224,352,480},{1,3..., dimensions={0} | all-to-all | bytes 2179072 | tf_op jit(solution)/shard_map/all_to_all | solution.py:43
  19.6 2.4 %broadcast_in_dim.18 = bf16[4,224,2432]{2,1,0:T(8,128)(2,1)} broadcast(bf16[224,2432]{1,0:T(8,128)(2,1)S(1)} %bitcast.9), dimensions={1,2} | broadcast | bytes 5447680 | tf_op jit(solution)/shard_map/broadcast_in_dim | solution.py:42
  22.0 5.0 %all-to-all-start.1 = ((bf16[4,224,2432]{2,1,0:T(8,128)(2,1)}), bf16[4,224,2432]{2,1,0:T(8,128)(2,1)}, u32[]{:S(2)}, u32[]{:S(2)}) async-start(bf16[4,224,2432]{2,1,0:T(8,128)(2,1)} %broadcast_in_dim.18), calls=%async_computation.1 | async-start | bytes 8716288 | tf_op jit(solution)/shard_map/all_to_all | solution.py:43
  28.5 3.0 %shard_map.50 = (f32[384,2432]{1,0:T(8,128)S(1)}, f32[8,384]{1,0:T(8,128)S(1)}) custom-call(bf16[384,2432]{1,0:T(8,128)(2,1)S(1)} %copy-done.11), custom_call_target="tpu_custom_call" | custom-call | flops 7471104 | bytes 5603328 | tf_op jit(solution)/shard_map/pallas_call | solution.py:324
  31.5 1.9 copy-done.4
  33.4 22.3 %all-to-all-done.1 = bf16[4,224,2432]{2,1,0:T(8,128)(2,1)} async-done(((bf16[4,224,2432]{2,1,0:T(8,128)(2,1)}), bf16[4,224,2432]{2,1,0:T(8,128)(2,1)}, u32[]{:S(2)}, u32[]{:S(2)}) %all-to-all-start.1) | async-done | bytes 4358176 | tf_op jit(solution)/shard_map/all_to_all | solution.py:43
  55.7 2.1 %copy-done.5 = f32[384,2432]{1,0:T(8,128)S(1)} copy-done((f32[384,2432]{1,0:T(8,128)S(1)}, f32[384,2432]{1,0:T(8,128)}, u32[]{:S(2)}) %copy-start.5) | copy-done | bytes 3735576
  57.7 11.4 %shard_map.51 = (f32[384,2432]{1,0:T(8,128)S(1)}, f32[8,384]{1,0:T(8,128)S(1)}) custom-call(bf16[384,896]{1,0:T(8,128)(2,1)S(1)} %copy.11.h_ref, bf16[896,2432]{1,0:T(8,128)(2,1)} %bitcast.4.w_ref, f32[384,2432]{1,0:T(8,128)S(1)} %copy-done.5, f32[8,384]{1,0:T(8,128)S(1)} %get-tuple-element.15.tstat_ref), custom_call_target="tpu_custom_call" | custom-call | flops 1673527296 | bytes 7471104 | tf_op jit(solution)/shard_map/pallas_call | solution.py:327
  69.1 1.9 collective-permute-start
  71.1 1.1 collective-permute-done.other_ref
  72.3 26.9 %all_to_all.36.refs_3_ = f32[16,8,384]{2,1,0:T(8,128)S(1)} all-to-all(f32[16,8,384]{2,1,0:T(8,128)S(1)} %shard_map.52), channel_id=1, replica_groups={{0,2,4,6,8,10,12,14,16,18,20,22,24,26,28,30},{1,3,5,7,9,11,13,15,17,19,..., dimensions={0} | all-to-all | bytes 393216 | tf_op jit(solution)/shard_map/all_to_all | solution.py:344
  99.2 5.6 %shard_map.53 = (f32[4,5,2432]{2,1,0:T(8,128)S(1)}, f32[384,128]{1,0:T(8,128)S(1)}) custom-call(f32[384,2432]{1,0:T(8,128)S(1)} %get-tuple-element.16.refs_0_.es_ref, f32[384,2432]{1,0:T(8,128)S(1)} %copy-done.6, f32[8,384]{1,0:T(8,128)S(1)} %get-tuple-element.17.own_ref.refs_2_, f32[16,8,384]{2,1,0:T(8,128)S(1)} %all_to_all.36.refs_3_), custom_call_target="tpu_custom_call" | custom-call | flops 9338880 | bytes 7471104 | tf_op jit(solution)/shard_map/pallas_call | solution.py:345
  104.8 9.3 %all_to_all.37.parts_ref = f32[4,5,2432]{2,1,0:T(8,128)S(1)} all-to-all(f32[4,5,2432]{2,1,0:T(8,128)S(1)} %get-tuple-element.19), channel_id=1, replica_groups={{0,128,256,384},{32,160,288,416},{64,192,320,448},{96,224,352,480},{1,3..., dimensions={0} | all-to-all | bytes 389120 | tf_op jit(solution)/shard_map/all_to_all | solution.py:356
  114.9 3.5 %all-to-all-start.4 = ((f32[4,5,2432]{2,1,0:T(8,128)}), f32[4,5,2432]{2,1,0:T(8,128)S(1)}, u32[]{:S(2)}, u32[]{:S(2)}) async-start(f32[4,5,2432]{2,1,0:T(8,128)} %shard_map.54), calls=%async_computation.4 | async-start | bytes 622592 | tf_op jit(solution)/shard_map/all_to_all | solution.py:358
  118.4 6.8 %all-to-all-done.4.refs_3_ = f32[4,5,2432]{2,1,0:T(8,128)S(1)} async-done(((f32[4,5,2432]{2,1,0:T(8,128)}), f32[4,5,2432]{2,1,0:T(8,128)S(1)}, u32[]{:S(2)}, u32[]{:S(2)}) %all-to-all-start.4) | async-done | bytes 194592 | tf_op jit(solution)/shard_map/all_to_all | solution.py:358
  125.2 2.1 %copy-done.1 = f32[384,2432]{1,0:T(8,128)S(1)} copy-done((f32[384,2432]{1,0:T(8,128)S(1)}, f32[384,2432]{1,0:T(8,128)}, u32[]{:S(2)}) %copy-start.1) | copy-done | bytes 3735576
  127.3 2.1 %copy-done.7 = f32[384,2432]{1,0:T(8,128)S(1)} copy-done((f32[384,2432]{1,0:T(8,128)S(1)}, f32[384,2432]{1,0:T(8,128)}, u32[]{:S(2)}) %copy-start.7) | copy-done | bytes 3735576
  129.3 5.5 %shard_map.55 = (f32[384,2432]{1,0:T(8,128)S(1)}, f32[384,128]{1,0:T(8,128)S(1)}, f32[8,384]{1,0:T(8,128)S(1)}, f32[32,1,384]{2,1,0:T(1,128)}) custom-call(f32[384,2432]{1,0:T(8,128)S(1)} %copy-done.1, f32[384,2432]{1,0:T(8,128)S(1)} %copy-done.7, f32[384,128]{1,0:T(8,128)S(1)} %get-tuple-element.18.refs_2_.terms_ref, f32[4,5,2432]{2,1,0:T(8,128)S(1)} %all-to-all-done.4.refs_3_), custom_call_target="tpu_custom_call" | custom-call | flops 13074432 | bytes 11206656 | tf_op jit(solution)/shard_map/pallas_call | solution.py:359
  134.9 1.8 copy-done.8
  137.4 6.4 %all-to-all-start.5 = ((f32[32,1,384]{2,1,0:T(1,128)}), f32[32,1,384]{2,1,0:T(1,128)S(1)}, u32[]{:S(2)}, u32[]{:S(2)}) async-start(f32[32,1,384]{2,1,0:T(1,128)} %get-tuple-element.21), calls=%async_computation.5 | async-start | bytes 98304 | tf_op jit(solution)/shard_map/all_to_all | solution.py:370
  143.8 2.0 %copy-done.2 = f32[384,2432]{1,0:T(8,128)S(1)} copy-done((f32[384,2432]{1,0:T(8,128)S(1)}, f32[384,2432]{1,0:T(8,128)}, u32[]{:S(2)}) %copy-start.2) | copy-done | bytes 3735576
  145.8 2.1 %copy-done.9 = f32[384,2432]{1,0:T(8,128)S(1)} copy-done((f32[384,2432]{1,0:T(8,128)S(1)}, f32[384,2432]{1,0:T(8,128)}, u32[]{:S(2)}) %copy-start.9) | copy-done | bytes 3735576
  147.9 0.9 copy-done.13
  148.8 8.3 %shard_map.57.refs_0_ = f32[2,2,16,28,384]{4,3,2,1,0:T(8,128)S(1)} custom-call(s32[17]{0:T(128)S(1)} %pad_add_fusion.place_ref, f32[384,2432]{1,0:T(8,128)S(1)} %copy-done.2, f32[384,2432]{1,0:T(8,128)S(1)} %copy-done.9, f32[384,128]{1,0:T(8,128)S(1)} %get-tuple-element.18.refs_2_.terms_ref, f32[384,128]{1,0:T(8,128)S(1)} %copy-done.13, ...), custom_call_target="tpu_custom_call" | custom-call | flops 3347054592 | bytes 14942208 | tf_op jit(solution)/shard_map/pallas_call | solution.py:374
  158.0 1.9 collective-permute-start.1
  160.0 2.1 %collective-permute-done.1 = f32[16,28,384]{2,0,1:T(8,128)S(1)} collective-permute-done((f32[16,28,384]{2,0,1:T(8,128)S(1)}, f32[16,28,384]{2,0,1:T(8,128)S(1)}, u32[]{:S(2)}, u32[]{:S(2)}) %collective-permute-start.1) | collective-permute-done | bytes 688160 | tf_op jit(solution)/shard_map/ppermute | solution.py:392
  163.1 11.6 %all-to-all-start.6 = ((bf16[16,28,384]{2,1,0:T(8,128)(2,1)}), bf16[16,28,384]{2,1,0:T(8,128)(2,1)S(1)}, u32[]{:S(2)}, u32[]{:S(2)}) async-start(bf16[16,28,384]{2,1,0:T(8,128)(2,1)} %shard_map.59), calls=%async_computation.6 | async-start | bytes 786432 | tf_op jit(solution)/shard_map/all_to_all | solution.py:394
  174.8 2.0 %copy-done.3 = f32[384,2432]{1,0:T(8,128)S(1)} copy-done((f32[384,2432]{1,0:T(8,128)S(1)}, f32[384,2432]{1,0:T(8,128)}, u32[]{:S(2)}) %copy-start.3) | copy-done | bytes 3735576
  176.8 2.1 %copy-done.10 = f32[384,2432]{1,0:T(8,128)S(1)} copy-done((f32[384,2432]{1,0:T(8,128)S(1)}, f32[384,2432]{1,0:T(8,128)}, u32[]{:S(2)}) %copy-start.10) | copy-done | bytes 3735576
  178.9 2.9 %shard_map.56 = bf16[384,2432]{1,0:T(8,128)(2,1)} custom-call(f32[384,2432]{1,0:T(8,128)S(1)} %copy-done.3, f32[384,2432]{1,0:T(8,128)S(1)} %copy-done.10, f32[384,128]{1,0:T(8,128)S(1)} %get-tuple-element.18.refs_2_.terms_ref, f32[32,1,384]{2,1,0:T(1,128)S(1)} %all-to-all-done.5.refs_3_.refs_2_), custom_call_target="tpu_custom_call" | custom-call | flops 3735552 | bytes 9338880 | tf_op jit(solution)/shard_map/pallas_call | solution.py:395
  181.8 17.3 %all-to-all-done.6.share_ref = bf16[16,28,384]{2,1,0:T(8,128)(2,1)S(1)} async-done(((bf16[16,28,384]{2,1,0:T(8,128)(2,1)}), bf16[16,28,384]{2,1,0:T(8,128)(2,1)S(1)}, u32[]{:S(2)}, u32[]{:S(2)}) %all-to-all-start.6) | async-done | bytes 344096 | tf_op jit(solution)/shard_map/all_to_all | solution.py:394
  (34 shorter events, 5.7 us)
Async XLA Ops:
  22.0 5.0 %copy-start.14 = (bf16[384,896]{1,0:T(8,128)(2,1)S(1)}, bf16[384,896]{1,0:T(8,128)(2,1)}, u32[]{:S(2)}) copy-start(bf16[384,896]{1,0:T(8,128)(2,1)} %param.3) | copy-start | bytes 2064388
  22.0 33.7 %all-to-all-start.1 = ((bf16[4,224,2432]{2,1,0:T(8,128)(2,1)}), bf16[4,224,2432]{2,1,0:T(8,128)(2,1)}, u32[]{:S(2)}, u32[]{:S(2)}) async-start(bf16[4,224,2432]{2,1,0:T(8,128)(2,1)} %broadcast_in_dim.18), calls=%async_computation.1 | async-start | bytes 8716288 | tf_op jit(solution)/shard_map/all_to_all | solution.py:43
  27.0 1.5 copy-start.11
  31.5 1.9 copy-start.4
  55.7 2.1 %copy-start.5 = (f32[384,2432]{1,0:T(8,128)S(1)}, f32[384,2432]{1,0:T(8,128)}, u32[]{:S(2)}) copy-start(f32[384,2432]{1,0:T(8,128)} %copy-done.4) | copy-start | bytes 11206660
  57.7 41.4 %copy-start.6 = (f32[384,2432]{1,0:T(8,128)S(1)}, f32[384,2432]{1,0:T(8,128)}, u32[]{:S(2)}) copy-start(f32[384,2432]{1,0:T(8,128)} %copy-done.4) | copy-start | bytes 11206660
  69.1 35.6 %copy-start = (f32[384,2432]{1,0:T(8,128)}, f32[384,2432]{1,0:T(8,128)S(1)}, u32[]{:S(2)}) copy-start(f32[384,2432]{1,0:T(8,128)S(1)} %get-tuple-element.16.refs_0_.es_ref) | copy-start | bytes 11206660
  69.1 3.1 %collective-permute-start = (f32[8,384]{1,0:T(8,128)S(1)}, f32[8,384]{1,0:T(8,128)S(1)}, u32[]{:S(2)}, u32[]{:S(2)}) collective-permute-start(f32[8,384]{1,0:T(8,128)S(1)} %get-tuple-element.17.own_ref.refs_2_), channel_id=1, source_target_pairs={{0,1},{1,0},{2,3},{3,2},{4,5},{5,4},{6,7},{7,6},{8,9},{9,8},{10,11... | collective-permute-start | bytes 36872 | tf_op jit(solution)/shard_map/ppermute | solution.py:342
  114.9 10.4 %all-to-all-start.4 = ((f32[4,5,2432]{2,1,0:T(8,128)}), f32[4,5,2432]{2,1,0:T(8,128)S(1)}, u32[]{:S(2)}, u32[]{:S(2)}) async-start(f32[4,5,2432]{2,1,0:T(8,128)} %shard_map.54), calls=%async_computation.4 | async-start | bytes 622592 | tf_op jit(solution)/shard_map/all_to_all | solution.py:358
  125.2 2.1 %copy-start.1 = (f32[384,2432]{1,0:T(8,128)S(1)}, f32[384,2432]{1,0:T(8,128)}, u32[]{:S(2)}) copy-start(f32[384,2432]{1,0:T(8,128)} %copy-done) | copy-start | bytes 11206660
  127.3 2.1 %copy-start.7 = (f32[384,2432]{1,0:T(8,128)S(1)}, f32[384,2432]{1,0:T(8,128)}, u32[]{:S(2)}) copy-start(f32[384,2432]{1,0:T(8,128)} %copy-done.4) | copy-start | bytes 11206660
  134.8 1.8 copy-start.8
  136.7 0.7 copy-start.12
  137.4 20.1 %all-to-all-start.5 = ((f32[32,1,384]{2,1,0:T(1,128)}), f32[32,1,384]{2,1,0:T(1,128)S(1)}, u32[]{:S(2)}, u32[]{:S(2)}) async-start(f32[32,1,384]{2,1,0:T(1,128)} %get-tuple-element.21), calls=%async_computation.5 | async-start | bytes 98304 | tf_op jit(solution)/shard_map/all_to_all | solution.py:370
  143.7 2.1 %copy-start.2 = (f32[384,2432]{1,0:T(8,128)S(1)}, f32[384,2432]{1,0:T(8,128)}, u32[]{:S(2)}) copy-start(f32[384,2432]{1,0:T(8,128)} %copy-done) | copy-start | bytes 11206660
  145.8 2.1 %copy-start.9 = (f32[384,2432]{1,0:T(8,128)S(1)}, f32[384,2432]{1,0:T(8,128)}, u32[]{:S(2)}) copy-start(f32[384,2432]{1,0:T(8,128)} %copy-done.8) | copy-start | bytes 11206660
  147.9 0.9 copy-start.13
  158.0 4.0 %collective-permute-start.1 = (f32[16,28,384]{2,0,1:T(8,128)S(1)}, f32[16,28,384]{2,0,1:T(8,128)S(1)}, u32[]{:S(2)}, u32[]{:S(2)}) collective-permute-start(f32[16,28,384]{2,0,1:T(8,128)S(1)} %copy.12), channel_id=1, source_target_pairs={{0,1},{1,0},{2,3},{3,2},{4,5},{5,4},{6,7},{7,6},{8,9},{9,8},{10,11... | collective-permute-start | bytes 2064392 | tf_op jit(solution)/shard_map/ppermute | solution.py:392
  163.1 35.9 %all-to-all-start.6 = ((bf16[16,28,384]{2,1,0:T(8,128)(2,1)}), bf16[16,28,384]{2,1,0:T(8,128)(2,1)S(1)}, u32[]{:S(2)}, u32[]{:S(2)}) async-start(bf16[16,28,384]{2,1,0:T(8,128)(2,1)} %shard_map.59), calls=%async_computation.6 | async-start | bytes 786432 | tf_op jit(solution)/shard_map/all_to_all | solution.py:394
  174.8 2.1 %copy-start.3 = (f32[384,2432]{1,0:T(8,128)S(1)}, f32[384,2432]{1,0:T(8,128)}, u32[]{:S(2)}) copy-start(f32[384,2432]{1,0:T(8,128)} %copy-done) | copy-start | bytes 11206660
  176.8 2.1 %copy-start.10 = (f32[384,2432]{1,0:T(8,128)S(1)}, f32[384,2432]{1,0:T(8,128)}, u32[]{:S(2)}) copy-start(f32[384,2432]{1,0:T(8,128)} %copy-done.8) | copy-start | bytes 11206660

commit v3 on v1

--- a/solution.py
+++ b/solution.py
@@ -1,6 +1,8 @@
 import jax
 import jax.numpy as jnp
 from jax import lax
+from jax.experimental import pallas as pl
+from jax.experimental.pallas import tpu as pltpu
 from jax.sharding import PartitionSpec as P
 
 TEMP = 4
@@ -11,6 +13,9 @@
 DP = SIDE * SIDE
 VOCAB = CHIPS * CORES
 AXES = ("dp", "vocab")
+TILE = 128
+GRANT = 22 * 1024 * 1024
+F32, BF16 = jnp.float32, jnp.bfloat16
 
 
 def _plane_groups(flip):
@@ -29,6 +34,17 @@
 
 
 FIRST, SECOND = _plane_groups(0), _plane_groups(1)
+def _step_pairs(step):
+    pairs = []
+    for x in range(SIDE):
+        for y in range(SIDE):
+            for v in range(VOCAB):
+                tx, ty = (x, (y + step) % SIDE) if v % CORES == 0 else ((x + step) % SIDE, y)
+                pairs.append(((x * SIDE + y) * VOCAB + v, (tx * SIDE + ty) * VOCAB + v))
+    return pairs
+
+
+AHEAD, BACK = _step_pairs(1), _step_pairs(SIDE - 1)
 COLUMN = [[z * CORES + core for z in range(CHIPS)] for core in range(CORES)]
 PAIR = [(i, i ^ 1) for i in range(VOCAB)]
 
@@ -36,6 +52,87 @@
 def spread(block, count, axis, groups=None):
     copies = jnp.broadcast_to(block[None], (count,) + block.shape)
     return lax.all_to_all(copies, axis, 0, 0, tiled=True, axis_index_groups=groups)
+
+
+def _chunks(total, size):
+    return [(at, min(at + size, total)) for at in range(0, total, size)]
+
+
+def _rows(i, size):
+    return pl.ds(pl.multiple_of(i * size, size), size)
+
+
+def _loop(count, step, unroll):
+    lax.fori_loop(0, count, lambda i, c: (step(i), c)[1], 0, unroll=unroll)
+
+
+def product_kernel(place_ref, q_ref, g_ref, mean_ref, near_ref, far_ref, out_ref, left, res):
+    def step(i):
+        rows = _rows(i, 16)
+        qs = q_ref[rows, :]
+        left[rows, :] = (qs * (g_ref[rows, :] - mean_ref[rows, :]) * (1.0 / TEMP)).astype(BF16)
+        left[pl.ds(pl.multiple_of(TILE + i * 16, 16), 16), :] = (qs * (1.0 / TEMP)).astype(BF16)
+
+    _loop(TILE // 16, step, 2)
+    cut = near_ref.shape[0]
+    for part_ref, lo, hi in ((near_ref, 0, cut), (far_ref, cut, res.shape[0])):
+        res[lo:hi] = lax.dot_general(
+            part_ref[...], left[...], (((1,), (1,)), ((), ())), preferred_element_type=F32
+        )
+    half = out_ref.shape[3]
+    for j in range(DP):
+        for core in range(CORES):
+            lo = (j * CORES + core) * half
+            away = (place_ref[DP] + core) % CORES
+            for k in range(2):
+                out_ref[k, away, place_ref[j]] = res[lo : lo + half, k * TILE : (k + 1) * TILE]
+
+
+def shift_kernel(classes, mean_ref, shares_ref, products_ref, keep_ref, send_ref):
+    shift = mean_ref[...] - jnp.sum(shares_ref[:, 0, :], axis=0, keepdims=True) / classes
+    for j in range(keep_ref.shape[0]):
+        keep_ref[j] = products_ref[0, 0, j] + shift * products_ref[1, 0, j]
+        send_ref[j] = products_ref[0, 1, j] + shift * products_ref[1, 1, j]
+
+
+def add_kernel(a_ref, b_ref, out_ref):
+    for j in range(out_ref.shape[0]):
+        out_ref[j] = (a_ref[j] + b_ref[j]).astype(BF16)
+
+
+def last_kernel(share_ref, out_ref):
+    total = share_ref[0].astype(F32)
+    for j in range(1, share_ref.shape[0]):
+        total = total + share_ref[j].astype(F32)
+    out_ref[...] = total
+
+
+def _call(kernel, steps, in_specs, out_specs, out_shape, scratch, flops, nbytes):
+    return pl.pallas_call(
+        kernel,
+        grid=(steps,),
+        in_specs=in_specs,
+        out_specs=out_specs,
+        out_shape=out_shape,
+        scratch_shapes=scratch,
+        compiler_params=pltpu.CompilerParams(
+            dimension_semantics=("arbitrary",), vmem_limit_bytes=GRANT
+        ),
+        cost_estimate=pl.CostEstimate(flops=flops, bytes_accessed=nbytes, transcendentals=0),
+    )
+
+
+def _far(x):
+    return pltpu.with_memory_space_constraint(x, pltpu.HBM)
+
+
+def _small(kernel, out_shape, *args):
+    return pl.pallas_call(
+        kernel,
+        out_shape=out_shape,
+        compiler_params=pltpu.CompilerParams(vmem_limit_bytes=GRANT),
+        cost_estimate=pl.CostEstimate(flops=1000000, bytes_accessed=4000000, transcendentals=0),
+    )(*args)
 
 
 def merge(parts):
@@ -62,11 +159,30 @@
     core = lax.axis_index("vocab") % CORES
 
     line = spread(head_weight, SIDE, AXES, FIRST).reshape(SIDE * rows, vocab_cols)
-    whole = spread(line, SIDE, AXES, SECOND).reshape(DP * rows, vocab_cols)
+    mine = lax.axis_index("dp")
+    place = jnp.where(core == 0, mine % SIDE, mine // SIDE)
+    offsets = (0, SIDE - 1, 1, 2)
     hid = student_hidden.reshape(tok_rows, SIDE, SIDE, rows)
-    hid = jnp.where(core == 0, jnp.swapaxes(hid, 1, 2), hid).reshape(tok_rows, width)
-
-    logits = jnp.dot(hid, whole, preferred_element_type=jnp.float32)
+    hid = jnp.where(core == 0, jnp.swapaxes(hid, 1, 2), hid).reshape(tok_rows, SIDE, SIDE * rows)
+    hid = [
+        lax.dynamic_slice_in_dim(hid, (place + o) % SIDE, 1, 1).reshape(tok_rows, SIDE * rows)
+        for o in offsets
+    ]
+    line, hid_near, hid_far = lax.optimization_barrier(
+        (line, jnp.concatenate(hid[:3], 1), hid[3])
+    )
+    top, low_half = line[: SIDE * rows // 2], line[SIDE * rows // 2 :]
+    left_top = lax.ppermute(top, AXES, AHEAD)
+    right_low = lax.ppermute(low_half, AXES, BACK)
+    left_low = lax.ppermute(low_half, AXES, AHEAD)
+    right_top = lax.ppermute(top, AXES, BACK)
+    far = jnp.concatenate(
+        [lax.ppermute(left_top, AXES, AHEAD), lax.ppermute(right_low, AXES, BACK)], 0
+    )
+    near = jnp.concatenate([line, left_top, left_low, right_top, right_low], 0)
+
+    logits = jnp.dot(hid_near, near, preferred_element_type=F32)
+    logits = logits + jnp.dot(hid_far, far, preferred_element_type=F32)
     scaled_student = logits / TEMP
     scaled_teacher = teacher_logits.astype(jnp.float32) / TEMP
     own_s = jnp.max(scaled_student, axis=1)
@@ -118,25 +234,49 @@
     inner = inner + (prob_t - mean_t[None, :]) / col_den[None, :]
     inner = inner - (col_rho / (col_var + EPS))[None, :] * (prob_s - mean_s[None, :])
     coeff = -TEMP * inner
-    row_dot = jnp.sum(prob_s * coeff, 1)
-    row_dot = jnp.sum(spread(row_dot[None], VOCAB, "vocab"), (0, 1)) / classes
-    logit_grad = (prob_s * (coeff - row_dot[:, None]) / TEMP).astype(jnp.bfloat16)
-
-    part = lax.dot_general(
-        whole, logit_grad, (((1,), (1,)), ((), ())), preferred_element_type=jnp.float32
-    )
-    part = part.reshape(SIDE, SIDE, rows, tok_rows)
-    part = jnp.where(core == 0, jnp.swapaxes(part, 0, 1), part)
-    part = part.reshape(DP, CORES, rows // CORES, tok_rows)
-    low, high = part[:, 0], part[:, 1]
-    keep = jnp.where(core == 0, low, high)
-    send = jnp.where(core == 0, high, low)
-    keep = keep + lax.ppermute(send, "vocab", PAIR)
-    share = lax.all_to_all(
-        keep.astype(jnp.bfloat16), "vocab", 0, 0, tiled=True, axis_index_groups=COLUMN
-    )
-    hidden_grad = jnp.sum(share.astype(jnp.float32), 0).T.astype(jnp.bfloat16)
-    return (logit_grad, hidden_grad)
+    steps = tok_rows // TILE
+    half = rows // CORES
+    area = tok_rows * vocab_cols
+    own_dot = jnp.sum(prob_s * coeff, 1)
+    mean = own_dot / jnp.maximum(jnp.sum(prob_s, 1), 1e-30)
+    shares = spread(own_dot[None], VOCAB, "vocab")
+    turn = jnp.repeat((place + jnp.array(offsets, jnp.int32)) % SIDE, SIDE)
+    along = jnp.tile(jnp.arange(SIDE, dtype=jnp.int32), SIDE)
+    slot = jnp.where(core == 0, along * SIDE + turn, turn * SIDE + along)
+    slot = jnp.concatenate([slot, core.astype(jnp.int32)[None]])
+    tile = pl.BlockSpec((TILE, vocab_cols), lambda i: (i, 0))
+    products = _call(
+        product_kernel,
+        steps,
+        [
+            pl.BlockSpec(memory_space=pltpu.SMEM),
+            tile,
+            tile,
+            pl.BlockSpec((TILE, 1), lambda i: (i, 0)),
+            pl.BlockSpec(near.shape, lambda i: (0, 0), pipeline_mode=pl.Buffered(1)),
+            pl.BlockSpec(far.shape, lambda i: (0, 0), pipeline_mode=pl.Buffered(1)),
+        ],
+        pl.BlockSpec((2, CORES, DP, half, TILE), lambda i: (0, 0, 0, 0, i)),
+        jax.ShapeDtypeStruct((2, CORES, DP, half, tok_rows), F32),
+        [pltpu.VMEM((2 * TILE, vocab_cols), BF16), pltpu.VMEM((width, 2 * TILE), F32)],
+        4 * area * width,
+        16 * area,
+    )(slot, _far(prob_s), _far(coeff), mean[:, None], _far(near), _far(far))
+    row_dot = jnp.sum(shares, (0, 1)) / classes
+    piece = jax.ShapeDtypeStruct((DP, half, tok_rows), F32)
+    keep, send = _small(
+        lambda *refs: shift_kernel(classes, *refs), [piece, piece], mean[None], shares, products
+    )
+    share = _small(
+        add_kernel,
+        jax.ShapeDtypeStruct((DP, half, tok_rows), BF16),
+        keep,
+        lax.ppermute(send, "vocab", PAIR),
+    )
+    share = lax.all_to_all(share, "vocab", 0, 0, tiled=True, axis_index_groups=COLUMN)
+    logit_grad = (prob_s * (coeff - row_dot[:, None]) / TEMP).astype(BF16)
+    hidden_grad = _small(last_kernel, jax.ShapeDtypeStruct((half, tok_rows), F32), share)
+    return (logit_grad, hidden_grad.T.astype(BF16))
 
 
 def solution(mesh):

time: 193 us -> 182 us (0.943)
  blocking collectives: 110 us -> 26 us
  starting transfers between devices: 8.85 us -> 58.1 us
  waiting for transfers between devices: 31 us -> 48.9 us
  Pallas kernels: 0 us -> 10.3 us
  matrix products: 8.95 us -> 2.57 us
    all_to_all x5 -> x1, blocking collectives: 83.4 us -> 26 us  [spread(): lax.all_to_all(copies, axis, 0, 0, tiled=True, axis_index_groups=groups)]
    all_to_all x1 -> x0, blocking collectives: 27.1 us -> none  [body(): lax.all_to_all(keep.astype(jnp.bfloat16), 'vocab', 0, 0, tiled=True, axis...]
    ppermute x1 -> x7, starting transfers between devices: 1.92 us -> 23.1 us  [the longest x1 5.13 us: body(): right_top = lax.ppermute(top, AXES, BACK)]
    all_to_all x1 -> x4, starting transfers between devices: 5.01 us -> 25.6 us  [spread(): lax.all_to_all(copies, axis, 0, 0, tiled=True, axis_index_groups=groups)]
    all_to_all x0 -> x1, waiting for transfers between devices: none -> 19.3 us  [body(): lax.all_to_all(share, 'vocab', 0, 0, tiled=True, axis_index_groups=COLUMN)]
    pallas_call x0 -> x4, Pallas kernels: none -> 10.3 us  [the longest x1 9.24 us: body(): _call(product_kernel, steps, [pl.BlockSpec(memory_space=pltpu.SMEM), tile...]
    all_to_all x0 -> x1, starting transfers between devices: none -> 7.5 us  [body(): lax.all_to_all(share, 'vocab', 0, 0, tiled=True, axis_index_groups=COLUMN)]
    dot_general x2, matrix products: 8.95 us -> 2.57 us  [the longest x1 1.74 us: body(): logits = jnp.dot(hid_near, near, preferred_element_type=F32)]
  transfers between devices with their start and end apart: 3 -> 13, of which waited for: 3 -> 9; matrix products, arithmetic and copies ran while one was open for 0% -> 7% of each run, Pallas kernels for 0% -> 5%
where the time goes in v3:
time: 182 us; the launch traced here: 181 us
  starting transfers between devices  58.1 us (32%)
  waiting for transfers between devices  48.9 us (27%)
  blocking collectives  26 us (14%)
  other arithmetic  22.9 us (13%)
  local copies, waits for them, and re-layouts  11 us (6%)
  Pallas kernels  10.3 us (6%)
  matrix products  2.57 us (1%)
    all_to_all x1, blocking collectives, spread(): lax.all_to_all(copies, axis, 0, 0, tiled=True, axis_index_groups=groups)  26 us
    all_to_all x4, starting transfers between devices, spread(): lax.all_to_all(copies, axis, 0, 0, tiled=True, axis_index_groups=groups)  25.6 us
    all_to_all x4, waiting for transfers between devices, spread(): lax.all_to_all(copies, axis, 0, 0, tiled=True, axis_index_groups=groups)  21.6 us
    all_to_all x1, waiting for transfers between devices, body(): lax.all_to_all(share, 'vocab', 0, 0, tiled=True, axis_index_groups=COLUMN)  19.3 us
    pallas_call x1, Pallas kernels, body(): _call(product_kernel, steps, [pl.BlockSpec(memory_space=pltpu.SMEM), tile...  9.24 us
    all_to_all x1, starting transfers between devices, body(): lax.all_to_all(share, 'vocab', 0, 0, tiled=True, axis_index_groups=COLUMN)  7.5 us
    reduce_sum x1, other arithmetic, body(): mean = own_dot / jnp.maximum(jnp.sum(prob_s, 1), 1e-30)  6.3 us
    reduce_sum x1, other arithmetic, body(): jnp.sum(prob_s * prob_t, 0)  6.24 us
  transfers between devices with their start and end apart: 13, of which 9 were waited for; matrix products, arithmetic and copies ran while one was open for 7% of the time, Pallas kernels for 5%

profile of v3, /device:TPU:2, one launch (start us, length us, event | category | flops | bytes accessed | tf_op | source)
XLA Modules:
  0.0 180.8 jit_solution(11074961782424005819)
XLA Ops:
  0.6 2.0 %broadcast_in_dim.14 = bf16[4,56,2432]{2,1,0:T(8,128)(2,1)} broadcast(bf16[56,2432]{1,0:T(8,128)(2,1)} %param.5), dimensions={1,2} | broadcast | bytes 1361920 | tf_op jit(solution)/shard_map/broadcast_in_dim | solution.py:53
  2.6 9.4 %all-to-all-start = ((bf16[4,56,2432]{2,1,0:T(8,128)(2,1)}), bf16[4,56,2432]{2,1,0:T(8,128)(2,1)S(1)}, u32[]{:S(2)}, u32[]{:S(2)}) async-start(bf16[4,56,2432]{2,1,0:T(8,128)(2,1)} %broadcast_in_dim.14), calls=%async_computation | async-start | bytes 2179072 | tf_op jit(solution)/shard_map/all_to_all | solution.py:54
  12.0 2.4 %copy.57 = bf16[384,896]{0,1:T(8,128)(2,1)} copy(bf16[384,896]{1,0:T(8,128)(2,1)} %param.4) | data formatting | bytes 1376256 | tf_op args[0]
  14.4 1.4 bitcast_select_fusion
  16.6 5.1 %all-to-all-done = bf16[4,56,2432]{2,1,0:T(8,128)(2,1)S(1)} async-done(((bf16[4,56,2432]{2,1,0:T(8,128)(2,1)}), bf16[4,56,2432]{2,1,0:T(8,128)(2,1)S(1)}, u32[]{:S(2)}, u32[]{:S(2)}) %all-to-all-start) | async-done | bytes 1089568 | tf_op jit(solution)/shard_map/all_to_all | solution.py:54
  21.8 1.9 %collective-permute-start = (bf16[112,2432]{1,0:T(8,128)(2,1)S(1)}, bf16[112,2432]{1,0:T(8,128)(2,1)S(1)}, u32[]{:S(2)}, u32[]{:S(2)}) collective-permute-start(bf16[112,2432]{1,0:T(8,128)(2,1)S(1)} %get-tuple-element.49), channel_id=1, source_target_pairs={{0,32},{1,129},{2,34},{3,131},{4,36},{5,133},{6,38},{7,135},{8,40}... | collective-permute-start | bytes 1634312 | tf_op jit(solution)/shard_map/ppermute | solution.py:175
  23.7 5.1 %collective-permute-start.3 = (bf16[112,2432]{1,0:T(8,128)(2,1)S(1)}, bf16[112,2432]{1,0:T(8,128)(2,1)S(1)}, u32[]{:S(2)}, u32[]{:S(2)}) collective-permute-start(bf16[112,2432]{1,0:T(8,128)(2,1)S(1)} %get-tuple-element.48), channel_id=1, source_target_pairs={{0,96},{1,385},{2,98},{3,387},{4,100},{5,389},{6,102},{7,391},{8,1... | collective-permute-start | bytes 1634312 | tf_op jit(solution)/shard_map/ppermute | solution.py:176
  29.3 1.9 %collective-permute-start.1 = (bf16[112,2432]{1,0:T(8,128)(2,1)S(1)}, bf16[112,2432]{1,0:T(8,128)(2,1)S(1)}, u32[]{:S(2)}, u32[]{:S(2)}) collective-permute-start(bf16[112,2432]{1,0:T(8,128)(2,1)S(1)} %get-tuple-element.48), channel_id=1, source_target_pairs={{0,32},{1,129},{2,34},{3,131},{4,36},{5,133},{6,38},{7,135},{8,40}... | collective-permute-start | bytes 1634312 | tf_op jit(solution)/shard_map/ppermute | solution.py:177
  31.2 5.1 %collective-permute-start.2 = (bf16[112,2432]{1,0:T(8,128)(2,1)S(1)}, bf16[112,2432]{1,0:T(8,128)(2,1)S(1)}, u32[]{:S(2)}, u32[]{:S(2)}) collective-permute-start(bf16[112,2432]{1,0:T(8,128)(2,1)S(1)} %get-tuple-element.49), channel_id=1, source_target_pairs={{0,96},{1,385},{2,98},{3,387},{4,100},{5,389},{6,102},{7,391},{8,1... | collective-permute-start | bytes 1634312 | tf_op jit(solution)/shard_map/ppermute | solution.py:178
  36.5 1.9 %collective-permute-start.4 = (bf16[112,2432]{1,0:T(8,128)(2,1)S(1)}, bf16[112,2432]{1,0:T(8,128)(2,1)S(1)}, u32[]{:S(2)}, u32[]{:S(2)}) collective-permute-start(bf16[112,2432]{1,0:T(8,128)(2,1)S(1)} %collective-permute-done), channel_id=1, source_target_pairs={{0,32},{1,129},{2,34},{3,131},{4,36},{5,133},{6,38},{7,135},{8,40}... | collective-permute-start | bytes 1634312 | tf_op jit(solution)/shard_map/ppermute | solution.py:180
  38.4 5.1 %collective-permute-start.5 = (bf16[112,2432]{1,0:T(8,128)(2,1)S(1)}, bf16[112,2432]{1,0:T(8,128)(2,1)S(1)}, u32[]{:S(2)}, u32[]{:S(2)}) collective-permute-start(bf16[112,2432]{1,0:T(8,128)(2,1)S(1)} %collective-permute-done.3), channel_id=1, source_target_pairs={{0,96},{1,385},{2,98},{3,387},{4,100},{5,389},{6,102},{7,391},{8,1... | collective-permute-start | bytes 1634312 | tf_op jit(solution)/shard_map/ppermute | solution.py:180
  43.8 1.7 fusion.53
  45.6 3.4 %collective-permute-done.4 = bf16[112,2432]{1,0:T(8,128)(2,1)S(1)} collective-permute-done((bf16[112,2432]{1,0:T(8,128)(2,1)S(1)}, bf16[112,2432]{1,0:T(8,128)(2,1)S(1)}, u32[]{:S(2)}, u32[]{:S(2)}) %collective-permute-start.4) | collective-permute-done | bytes 544800 | tf_op jit(solution)/shard_map/ppermute | solution.py:180
  49.0 1.4 collective-permute-done.5
  51.5 1.8 %copy-done.1 = f32[384,2432]{1,0:T(8,128)} copy-done((f32[384,2432]{1,0:T(8,128)}, f32[384,2432]{1,0:T(8,128)S(1)}, u32[]{:S(2)}) %copy-start.1) | copy-done | bytes 3735576
  53.3 2.2 %multiply_reduce_fusion.4 = (f32[384]{0:T(512)S(1)}, f32[384]{0:T(512)S(1)}, f32[384]{0:T(512)S(1)}, f32[384]{0:T(512)S(1)}, f32[384]{0:T(512)S(1)}) fusion(bf16[384,2432]{1,0:T(8,128)(2,1)S(1)} %copy-done.2, f32[384,2432]{1,0:T(8,128)S(1)} %get-tuple-element.66, f32[384]{0:T(512)S(1)} %fusion.1, f32[384]{0:T(512)S(1)} %get-tuple-element.65), kind=kLoop, calls=%fused_computation.8 | loop fusion | flops 11204736 | bytes 5614080 | tf_op jit(solution)/shard_map/reduce_sum | solution.py:200
  55.6 1.9 %collective-permute-start.6 = (f32[7,384]{1,0:T(8,128)S(1)}, f32[7,384]{1,0:T(8,128)S(1)}, u32[]{:S(2)}, u32[]{:S(2)}) collective-permute-start(f32[7,384]{1,0:T(8,128)S(1)} %stack.82), channel_id=1, source_target_pairs={{0,1},{1,0},{2,3},{3,2},{4,5},{5,4},{6,7},{7,6},{8,9},{9,8},{10,11... | collective-permute-start | bytes 32264 | tf_op jit(solution)/shard_map/ppermute | solution.py:203
  58.9 26.0 %all_to_all.30 = f32[16,7,384]{2,1,0:T(8,128)S(1)} all-to-all(f32[16,7,384]{2,1,0:T(8,128)S(1)} %broadcast_in_dim.15), channel_id=1, replica_groups={{0,2,4,6,8,10,12,14,16,18,20,22,24,26,28,30},{1,3,5,7,9,11,13,15,17,19,..., dimensions={0} | all-to-all | bytes 344064 | tf_op jit(solution)/shard_map/all_to_all | solution.py:54
  85.2 6.2 %multiply_reduce_fusion.1 = (f32[2432]{0:T(1024)S(1)}, f32[2432]{0:T(1024)S(1)}, f32[2432]{0:T(1024)S(1)}, f32[2432]{0:T(1024)S(1)}, f32[2432]{0:T(1024)S(1)}, /*index=5*/f32[384,2432]{1,0:T(8,128)}) fusion(bf16[384,2432]{1,0:T(8,128)(2,1)S(1)} %copy-done.2, f32[384]{0:T(512)S(1)} %get-tuple-element.63, f32[384]{0:T(512)S(1)} %fusion.1, ...), kind=kLoop, calls=%fused_computation.5 | loop fusion | flops 13062272 | bytes 9393664 | tf_op jit(solution)/shard_map/reduce_sum | solution.py:220
  92.3 4.9 %all-to-all-start.2 = ((f32[4,5,2432]{2,1,0:T(8,128)}), f32[4,5,2432]{2,1,0:T(8,128)S(1)}, u32[]{:S(2)}, u32[]{:S(2)}) async-start(f32[4,5,2432]{2,1,0:T(8,128)} %broadcast_in_dim.16), calls=%async_computation.2 | async-start | bytes 622592 | tf_op jit(solution)/shard_map/all_to_all | solution.py:54
  97.4 5.2 %all-to-all-done.2 = f32[4,5,2432]{2,1,0:T(8,128)S(1)} async-done(((f32[4,5,2432]{2,1,0:T(8,128)}), f32[4,5,2432]{2,1,0:T(8,128)S(1)}, u32[]{:S(2)}, u32[]{:S(2)}) %all-to-all-start.2) | async-done | bytes 194592 | tf_op jit(solution)/shard_map/all_to_all | solution.py:54
  103.4 5.0 %all-to-all-start.3 = ((f32[4,5,2432]{2,1,0:T(8,128)}), f32[4,5,2432]{2,1,0:T(8,128)S(1)}, u32[]{:S(2)}, u32[]{:S(2)}) async-start(f32[4,5,2432]{2,1,0:T(8,128)} %broadcast_in_dim.17), calls=%async_computation.3 | async-start | bytes 622592 | tf_op jit(solution)/shard_map/all_to_all | solution.py:54
  108.5 6.9 %all-to-all-done.3 = f32[4,5,2432]{2,1,0:T(8,128)S(1)} async-done(((f32[4,5,2432]{2,1,0:T(8,128)}), f32[4,5,2432]{2,1,0:T(8,128)S(1)}, u32[]{:S(2)}, u32[]{:S(2)}) %all-to-all-start.3) | async-done | bytes 194592 | tf_op jit(solution)/shard_map/all_to_all | solution.py:54
  115.5 6.3 %fusion.45 = (f32[384]{0:T(512)S(1)}, f32[384]{0:T(512)S(1)}, f32[384,2432]{1,0:T(8,128)}) fusion(f32[384,2432]{1,0:T(8,128)} %get-tuple-element.43.q_ref, f32[2432]{0:T(1024)S(1)} %get-tuple-element.27, f32[2432]{0:T(1024)S(1)} %get-tuple-element.28, f32[2432]{0:T(1024)S(1)} %get-tuple-element.39, f32[2432]{0:T(1024)S(1)} %get-tuple-element.26, ...), kind=kLoop, calls=%fused_computation.120 | loop fusion | flops 15875328 | bytes 9387008 | tf_op jit(solution)/shard_map/reduce_sum | solution.py:241
  122.6 6.4 %all-to-all-start.4 = ((f32[32,1,384]{2,1,0:T(1,128)}), f32[32,1,384]{2,1,0:T(1,128)S(1)}, u32[]{:S(2)}, u32[]{:S(2)}) async-start(f32[32,1,384]{2,1,0:T(1,128)} %broadcast_in_dim.18), calls=%async_computation.4 | async-start | bytes 98304 | tf_op jit(solution)/shard_map/all_to_all | solution.py:54
  129.0 9.2 %shard_map.59.refs_2_ = f32[2,2,16,28,384]{4,3,2,1,0:T(8,128)S(1)} custom-call(s32[17]{0:T(128)S(1)} %pad_add_fusion.place_ref, f32[384,2432]{1,0:T(8,128)} %get-tuple-element.43.q_ref, f32[384,2432]{1,0:T(8,128)} %get-tuple-element.40.g_ref, f32[384,1]{1,0:T(8,128)S(1)} %div.157.mean_ref, bf16[672,2432]{1,0:T(8,128)(2,1)} %copy-done, ...), custom_call_target="tpu_custom_call" | custom-call | flops 3347054592 | bytes 14942208 | tf_op jit(solution)/shard_map/pallas_call | solution.py:248
  138.3 4.4 %all-to-all-done.4.refs_1_ = f32[32,1,384]{2,1,0:T(1,128)S(1)} async-done(((f32[32,1,384]{2,1,0:T(1,128)}), f32[32,1,384]{2,1,0:T(1,128)S(1)}, u32[]{:S(2)}, u32[]{:S(2)}) %all-to-all-start.4) | async-done | bytes 49184 | tf_op jit(solution)/shard_map/all_to_all | solution.py:54
  143.3 1.9 %collective-permute-start.7 = (f32[16,28,384]{2,0,1:T(8,128)S(1)}, f32[16,28,384]{2,0,1:T(8,128)S(1)}, u32[]{:S(2)}, u32[]{:S(2)}) collective-permute-start(f32[16,28,384]{2,0,1:T(8,128)S(1)} %copy.69), channel_id=1, source_target_pairs={{0,1},{1,0},{2,3},{3,2},{4,5},{5,4},{6,7},{7,6},{8,9},{9,8},{10,11... | collective-permute-start | bytes 2064392 | tf_op jit(solution)/shard_map/ppermute | solution.py:274
  145.2 2.1 %collective-permute-done.7 = f32[16,28,384]{2,0,1:T(8,128)S(1)} collective-permute-done((f32[16,28,384]{2,0,1:T(8,128)S(1)}, f32[16,28,384]{2,0,1:T(8,128)S(1)}, u32[]{:S(2)}, u32[]{:S(2)}) %collective-permute-start.7) | collective-permute-done | bytes 688160 | tf_op jit(solution)/shard_map/ppermute | solution.py:274
  148.4 7.5 %all-to-all-start.5 = ((bf16[16,28,384]{2,1,0:T(8,128)(2,1)}), bf16[16,28,384]{2,1,0:T(8,128)(2,1)S(1)}, u32[]{:S(2)}, u32[]{:S(2)}) async-start(bf16[16,28,384]{2,1,0:T(8,128)(2,1)} %shard_map.61), calls=%async_computation.5 | async-start | bytes 786432 | tf_op jit(solution)/shard_map/all_to_all | solution.py:276
  155.9 4.9 %multiply_convert_fusion = bf16[384,2432]{1,0:T(8,128)(2,1)} fusion(f32[384,2432]{1,0:T(8,128)} %get-tuple-element.43.q_ref, f32[384,2432]{1,0:T(8,128)} %get-tuple-element.40.g_ref, f32[384]{0:T(512)S(1)} %broadcast_multiply_fusion), kind=kLoop, calls=%fused_computation.2 | loop fusion | flops 3735552 | bytes 9340416 | tf_op jit(solution)/shard_map/convert_element_type | solution.py:277
  160.9 19.3 %all-to-all-done.5.share_ref = bf16[16,28,384]{2,1,0:T(8,128)(2,1)S(1)} async-done(((bf16[16,28,384]{2,1,0:T(8,128)(2,1)}), bf16[16,28,384]{2,1,0:T(8,128)(2,1)S(1)}, u32[]{:S(2)}, u32[]{:S(2)}) %all-to-all-start.5) | async-done | bytes 344096 | tf_op jit(solution)/shard_map/all_to_all | solution.py:276
  (82 shorter events, 9.6 us)
Async XLA Ops:
  2.6 19.1 %all-to-all-start = ((bf16[4,56,2432]{2,1,0:T(8,128)(2,1)}), bf16[4,56,2432]{2,1,0:T(8,128)(2,1)S(1)}, u32[]{:S(2)}, u32[]{:S(2)}) async-start(bf16[4,56,2432]{2,1,0:T(8,128)(2,1)} %broadcast_in_dim.14), calls=%async_computation | async-start | bytes 2179072 | tf_op jit(solution)/shard_map/all_to_all | solution.py:54
  12.0 16.8 %copy-start.2 = (bf16[384,2432]{1,0:T(8,128)(2,1)S(1)}, bf16[384,2432]{1,0:T(8,128)(2,1)}, u32[]{:S(2)}) copy-start(bf16[384,2432]{1,0:T(8,128)(2,1)} %param.6) | copy-start | bytes 5603332
  21.8 14.7 %collective-permute-start = (bf16[112,2432]{1,0:T(8,128)(2,1)S(1)}, bf16[112,2432]{1,0:T(8,128)(2,1)S(1)}, u32[]{:S(2)}, u32[]{:S(2)}) collective-permute-start(bf16[112,2432]{1,0:T(8,128)(2,1)S(1)} %get-tuple-element.49), channel_id=1, source_target_pairs={{0,32},{1,129},{2,34},{3,131},{4,36},{5,133},{6,38},{7,135},{8,40}... | collective-permute-start | bytes 1634312 | tf_op jit(solution)/shard_map/ppermute | solution.py:175
  23.7 14.7 %collective-permute-start.3 = (bf16[112,2432]{1,0:T(8,128)(2,1)S(1)}, bf16[112,2432]{1,0:T(8,128)(2,1)S(1)}, u32[]{:S(2)}, u32[]{:S(2)}) collective-permute-start(bf16[112,2432]{1,0:T(8,128)(2,1)S(1)} %get-tuple-element.48), channel_id=1, source_target_pairs={{0,96},{1,385},{2,98},{3,387},{4,100},{5,389},{6,102},{7,391},{8,1... | collective-permute-start | bytes 1634312 | tf_op jit(solution)/shard_map/ppermute | solution.py:176
  29.3 14.3 %collective-permute-start.1 = (bf16[112,2432]{1,0:T(8,128)(2,1)S(1)}, bf16[112,2432]{1,0:T(8,128)(2,1)S(1)}, u32[]{:S(2)}, u32[]{:S(2)}) collective-permute-start(bf16[112,2432]{1,0:T(8,128)(2,1)S(1)} %get-tuple-element.48), channel_id=1, source_target_pairs={{0,32},{1,129},{2,34},{3,131},{4,36},{5,133},{6,38},{7,135},{8,40}... | collective-permute-start | bytes 1634312 | tf_op jit(solution)/shard_map/ppermute | solution.py:177
  31.2 12.5 %collective-permute-start.2 = (bf16[112,2432]{1,0:T(8,128)(2,1)S(1)}, bf16[112,2432]{1,0:T(8,128)(2,1)S(1)}, u32[]{:S(2)}, u32[]{:S(2)}) collective-permute-start(bf16[112,2432]{1,0:T(8,128)(2,1)S(1)} %get-tuple-element.49), channel_id=1, source_target_pairs={{0,96},{1,385},{2,98},{3,387},{4,100},{5,389},{6,102},{7,391},{8,1... | collective-permute-start | bytes 1634312 | tf_op jit(solution)/shard_map/ppermute | solution.py:178
  36.5 12.5 %collective-permute-start.4 = (bf16[112,2432]{1,0:T(8,128)(2,1)S(1)}, bf16[112,2432]{1,0:T(8,128)(2,1)S(1)}, u32[]{:S(2)}, u32[]{:S(2)}) collective-permute-start(bf16[112,2432]{1,0:T(8,128)(2,1)S(1)} %collective-permute-done), channel_id=1, source_target_pairs={{0,32},{1,129},{2,34},{3,131},{4,36},{5,133},{6,38},{7,135},{8,40}... | collective-permute-start | bytes 1634312 | tf_op jit(solution)/shard_map/ppermute | solution.py:180
  38.4 12.0 %collective-permute-start.5 = (bf16[112,2432]{1,0:T(8,128)(2,1)S(1)}, bf16[112,2432]{1,0:T(8,128)(2,1)S(1)}, u32[]{:S(2)}, u32[]{:S(2)}) collective-permute-start(bf16[112,2432]{1,0:T(8,128)(2,1)S(1)} %collective-permute-done.3), channel_id=1, source_target_pairs={{0,96},{1,385},{2,98},{3,387},{4,100},{5,389},{6,102},{7,391},{8,1... | collective-permute-start | bytes 1634312 | tf_op jit(solution)/shard_map/ppermute | solution.py:180
  43.8 1.8 copy-start
  43.8 6.7 %copy-start.4 = (bf16[384,224]{0,1:T(8,128)(2,1)S(1)}, bf16[384,224]{0,1:T(8,128)(2,1)}, u32[]{:S(2)}) copy-start(bf16[384,224]{0,1:T(8,128)(2,1)} %get-tuple-element.9) | copy-start | bytes 516100
  50.5 1.0 copy-start.3
  51.5 1.8 %copy-start.1 = (f32[384,2432]{1,0:T(8,128)}, f32[384,2432]{1,0:T(8,128)S(1)}, u32[]{:S(2)}) copy-start(f32[384,2432]{1,0:T(8,128)S(1)} %get-tuple-element.66) | copy-start | bytes 11206660
  55.6 3.1 %collective-permute-start.6 = (f32[7,384]{1,0:T(8,128)S(1)}, f32[7,384]{1,0:T(8,128)S(1)}, u32[]{:S(2)}, u32[]{:S(2)}) collective-permute-start(f32[7,384]{1,0:T(8,128)S(1)} %stack.82), channel_id=1, source_target_pairs={{0,1},{1,0},{2,3},{3,2},{4,5},{5,4},{6,7},{7,6},{8,9},{9,8},{10,11... | collective-permute-start | bytes 32264 | tf_op jit(solution)/shard_map/ppermute | solution.py:203
  85.1 12.0 %copy-start.5 = (s32[4]{0:T(128)S(1)}, s32[4]{0:T(128)}, u32[]{:S(2)}) copy-start(s32[4]{0:T(128)} %constant.108.clone) | copy-start | bytes 52
  92.3 10.4 %all-to-all-start.2 = ((f32[4,5,2432]{2,1,0:T(8,128)}), f32[4,5,2432]{2,1,0:T(8,128)S(1)}, u32[]{:S(2)}, u32[]{:S(2)}) async-start(f32[4,5,2432]{2,1,0:T(8,128)} %broadcast_in_dim.16), calls=%async_computation.2 | async-start | bytes 622592 | tf_op jit(solution)/shard_map/all_to_all | solution.py:54
  103.4 11.9 %all-to-all-start.3 = ((f32[4,5,2432]{2,1,0:T(8,128)}), f32[4,5,2432]{2,1,0:T(8,128)S(1)}, u32[]{:S(2)}, u32[]{:S(2)}) async-start(f32[4,5,2432]{2,1,0:T(8,128)} %broadcast_in_dim.17), calls=%async_computation.3 | async-start | bytes 622592 | tf_op jit(solution)/shard_map/all_to_all | solution.py:54
  122.6 20.1 %all-to-all-start.4 = ((f32[32,1,384]{2,1,0:T(1,128)}), f32[32,1,384]{2,1,0:T(1,128)S(1)}, u32[]{:S(2)}, u32[]{:S(2)}) async-start(f32[32,1,384]{2,1,0:T(1,128)} %broadcast_in_dim.18), calls=%async_computation.4 | async-start | bytes 98304 | tf_op jit(solution)/shard_map/all_to_all | solution.py:54
  143.3 4.0 %collective-permute-start.7 = (f32[16,28,384]{2,0,1:T(8,128)S(1)}, f32[16,28,384]{2,0,1:T(8,128)S(1)}, u32[]{:S(2)}, u32[]{:S(2)}) collective-permute-start(f32[16,28,384]{2,0,1:T(8,128)S(1)} %copy.69), channel_id=1, source_target_pairs={{0,1},{1,0},{2,3},{3,2},{4,5},{5,4},{6,7},{7,6},{8,9},{9,8},{10,11... | collective-permute-start | bytes 2064392 | tf_op jit(solution)/shard_map/ppermute | solution.py:274
  148.4 31.8 %all-to-all-start.5 = ((bf16[16,28,384]{2,1,0:T(8,128)(2,1)}), bf16[16,28,384]{2,1,0:T(8,128)(2,1)S(1)}, u32[]{:S(2)}, u32[]{:S(2)}) async-start(bf16[16,28,384]{2,1,0:T(8,128)(2,1)} %shard_map.61), calls=%async_computation.5 | async-start | bytes 786432 | tf_op jit(solution)/shard_map/all_to_all | solution.py:276

commit v4 on v3

--- a/solution.py
+++ b/solution.py
@@ -34,17 +34,19 @@
 
 
 FIRST, SECOND = _plane_groups(0), _plane_groups(1)
-def _step_pairs(step):
+def _step_pairs(step, second):
     pairs = []
     for x in range(SIDE):
         for y in range(SIDE):
             for v in range(VOCAB):
-                tx, ty = (x, (y + step) % SIDE) if v % CORES == 0 else ((x + step) % SIDE, y)
+                along_x = (v % CORES == 0) != second
+                tx, ty = ((x + step) % SIDE, y) if along_x else (x, (y + step) % SIDE)
                 pairs.append(((x * SIDE + y) * VOCAB + v, (tx * SIDE + ty) * VOCAB + v))
     return pairs
 
 
-AHEAD, BACK = _step_pairs(1), _step_pairs(SIDE - 1)
+OVER = [_step_pairs(step, False) for step in (1, SIDE - 1, 2)]
+AHEAD, BACK = _step_pairs(1, True), _step_pairs(SIDE - 1, True)
 COLUMN = [[z * CORES + core for z in range(CHIPS)] for core in range(CORES)]
 PAIR = [(i, i ^ 1) for i in range(VOCAB)]
 
@@ -158,29 +160,39 @@
     tokens = tok_rows * DP
     core = lax.axis_index("vocab") % CORES
 
-    line = spread(head_weight, SIDE, AXES, FIRST).reshape(SIDE * rows, vocab_cols)
+    behind, before, across = (lax.ppermute(head_weight, AXES, pairs) for pairs in OVER)
+
     mine = lax.axis_index("dp")
-    place = jnp.where(core == 0, mine % SIDE, mine // SIDE)
+    down, right = mine // SIDE, mine % SIDE
+    first = jnp.where(core == 0, down, right)
+    second = jnp.where(core == 0, right, down)
     offsets = (0, SIDE - 1, 1, 2)
     hid = student_hidden.reshape(tok_rows, SIDE, SIDE, rows)
-    hid = jnp.where(core == 0, jnp.swapaxes(hid, 1, 2), hid).reshape(tok_rows, SIDE, SIDE * rows)
+    hid = jnp.where(core == 0, jnp.swapaxes(hid, 1, 2), hid)
+    hid = jnp.concatenate(
+        [lax.dynamic_slice_in_dim(hid, (first + o) % SIDE, 1, 2) for o in offsets], 2
+    ).reshape(tok_rows, SIDE, SIDE * rows)
     hid = [
-        lax.dynamic_slice_in_dim(hid, (place + o) % SIDE, 1, 1).reshape(tok_rows, SIDE * rows)
+        lax.dynamic_slice_in_dim(hid, (second + o) % SIDE, 1, 1).reshape(tok_rows, SIDE * rows)
         for o in offsets
     ]
-    line, hid_near, hid_far = lax.optimization_barrier(
-        (line, jnp.concatenate(hid[:3], 1), hid[3])
-    )
-    top, low_half = line[: SIDE * rows // 2], line[SIDE * rows // 2 :]
-    left_top = lax.ppermute(top, AXES, AHEAD)
-    right_low = lax.ppermute(low_half, AXES, BACK)
-    left_low = lax.ppermute(low_half, AXES, AHEAD)
-    right_top = lax.ppermute(top, AXES, BACK)
+    turn = jnp.stack([(second + offsets[k // SIDE]) % SIDE for k in range(DP)])
+    along = jnp.stack([(first + offsets[k % SIDE]) % SIDE for k in range(DP)])
+    slot = jnp.where(core == 0, along * SIDE + turn, turn * SIDE + along)
+    slot = jnp.concatenate([slot, core[None]]).astype(jnp.int32)
+    behind, hid_near, hid_far, slot = lax.optimization_barrier(
+        (behind, jnp.concatenate(hid[:3], 1), hid[3], slot)
+    )
+    early = jnp.concatenate([head_weight, behind], 0)
+    left_early = lax.ppermute(early, AXES, AHEAD)
+    right_early = lax.ppermute(early, AXES, BACK)
+    late = jnp.concatenate([before, across], 0)
+    right_late = lax.ppermute(late, AXES, BACK)
+    left_late = lax.ppermute(late, AXES, AHEAD)
     far = jnp.concatenate(
-        [lax.ppermute(left_top, AXES, AHEAD), lax.ppermute(right_low, AXES, BACK)], 0
-    )
-    near = jnp.concatenate([line, left_top, left_low, right_top, right_low], 0)
-
+        [lax.ppermute(left_early, AXES, AHEAD), lax.ppermute(right_late, AXES, BACK)], 0
+    )
+    near = jnp.concatenate([early, late, left_early, left_late, right_early, right_late], 0)
     logits = jnp.dot(hid_near, near, preferred_element_type=F32)
     logits = logits + jnp.dot(hid_far, far, preferred_element_type=F32)
     scaled_student = logits / TEMP
@@ -240,10 +252,6 @@
     own_dot = jnp.sum(prob_s * coeff, 1)
     mean = own_dot / jnp.maximum(jnp.sum(prob_s, 1), 1e-30)
     shares = spread(own_dot[None], VOCAB, "vocab")
-    turn = jnp.repeat((place + jnp.array(offsets, jnp.int32)) % SIDE, SIDE)
-    along = jnp.tile(jnp.arange(SIDE, dtype=jnp.int32), SIDE)
-    slot = jnp.where(core == 0, along * SIDE + turn, turn * SIDE + along)
-    slot = jnp.concatenate([slot, core.astype(jnp.int32)[None]])
     tile = pl.BlockSpec((TILE, vocab_cols), lambda i: (i, 0))
     products = _call(
         product_kernel,

time: 182 us -> 179 us (0.984)
  blocking collectives: 26 us -> 49.1 us
  waiting for transfers between devices: 48.9 us -> 37 us
  starting transfers between devices: 58.1 us -> 50.2 us
  local copies, waits for them, and re-layouts: 11 us -> 6.07 us
    all_to_all x1 -> x3, blocking collectives: 26 us -> 49.1 us  [spread(): lax.all_to_all(copies, axis, 0, 0, tiled=True, axis_index_groups=groups)]
    all_to_all x4 -> x1, starting transfers between devices: 25.6 us -> 6.39 us  [spread(): lax.all_to_all(copies, axis, 0, 0, tiled=True, axis_index_groups=groups)]
    all_to_all x4 -> x1, waiting for transfers between devices: 21.6 us -> 4.41 us  [spread(): lax.all_to_all(copies, axis, 0, 0, tiled=True, axis_index_groups=groups)]
    ppermute x6 -> x9, starting transfers between devices: 21.2 us -> 32.4 us  [the longest x3 13.7 us: body(): lax.ppermute(head_weight, AXES, pairs)]
    ppermute x6 -> x9, waiting for transfers between devices: 4.82 us -> 10 us  [the longest x1 5.61 us: body(): lax.ppermute(left_early, AXES, AHEAD)]
    broadcast_in_dim x5 -> x4, local copies, waits for them, and re-layouts: 4.14 us -> 0.7 us  [spread(): copies = jnp.broadcast_to(block[None], (count,) + block.shape)]
    unnamed x18 -> x17, local copies, waits for them, and re-layouts: 4.65 us -> 3.79 us
  transfers between devices with their start and end apart: 13 -> 13, of which waited for: 9 -> 7; matrix products, arithmetic and copies ran while one was open for 7% -> 5% of each run, Pallas kernels for 5% -> 5%
where the time goes in v4:
time: 179 us; the launch traced here: 178 us
  starting transfers between devices  50.2 us (28%)
  blocking collectives  49.1 us (27%)
  waiting for transfers between devices  37 us (21%)
  other arithmetic  21.7 us (12%)
  Pallas kernels  10.3 us (6%)
  local copies, waits for them, and re-layouts  6.07 us (3%)
  matrix products  2.57 us (1%)
    all_to_all x3, blocking collectives, spread(): lax.all_to_all(copies, axis, 0, 0, tiled=True, axis_index_groups=groups)  49.1 us
    all_to_all x1, waiting for transfers between devices, body(): lax.all_to_all(share, 'vocab', 0, 0, tiled=True, axis_index_groups=COLUMN)  19.3 us
    ppermute x3, starting transfers between devices, body(): lax.ppermute(head_weight, AXES, pairs)  13.7 us
    pallas_call x1, Pallas kernels, body(): _call(product_kernel, steps, [pl.BlockSpec(memory_space=pltpu.SMEM), tile...  9.24 us
    all_to_all x1, starting transfers between devices, body(): lax.all_to_all(share, 'vocab', 0, 0, tiled=True, axis_index_groups=COLUMN)  7.48 us
    all_to_all x1, starting transfers between devices, spread(): lax.all_to_all(copies, axis, 0, 0, tiled=True, axis_index_groups=groups)  6.39 us
    reduce_sum x1, other arithmetic, body(): mean = own_dot / jnp.maximum(jnp.sum(prob_s, 1), 1e-30)  6.3 us
    reduce_sum x1, other arithmetic, body(): jnp.sum(prob_s * prob_t, 0)  6.25 us
  transfers between devices with their start and end apart: 13, of which 7 were waited for; matrix products, arithmetic and copies ran while one was open for 5% of the time, Pallas kernels for 5%

profile of v4, /device:TPU:2, one launch (start us, length us, event | category | flops | bytes accessed | tf_op | source)
XLA Modules:
  0.0 178.2 jit_solution(17296696440904351667)
XLA Ops:
  0.6 3.4 %collective-permute-start = (bf16[56,2432]{1,0:T(8,128)(2,1)}, bf16[56,2432]{1,0:T(8,128)(2,1)S(1)}, u32[]{:S(2)}, u32[]{:S(2)}) collective-permute-start(bf16[56,2432]{1,0:T(8,128)(2,1)} %param.4), channel_id=1, source_target_pairs={{0,128},{1,33},{2,130},{3,35},{4,132},{5,37},{6,134},{7,39},{8,136... | collective-permute-start | bytes 817160 | tf_op jit(solution)/shard_map/ppermute | solution.py:163
  4.0 6.3 %collective-permute-start.1 = (bf16[56,2432]{1,0:T(8,128)(2,1)}, bf16[56,2432]{1,0:T(8,128)(2,1)S(1)}, u32[]{:S(2)}, u32[]{:S(2)}) collective-permute-start(bf16[56,2432]{1,0:T(8,128)(2,1)} %param.4), channel_id=1, source_target_pairs={{0,384},{1,97},{2,386},{3,99},{4,388},{5,101},{6,390},{7,103},{8,3... | collective-permute-start | bytes 817160 | tf_op jit(solution)/shard_map/ppermute | solution.py:163
  10.4 4.0 %collective-permute-start.2 = (bf16[56,2432]{1,0:T(8,128)(2,1)}, bf16[56,2432]{1,0:T(8,128)(2,1)S(1)}, u32[]{:S(2)}, u32[]{:S(2)}) collective-permute-start(bf16[56,2432]{1,0:T(8,128)(2,1)} %param.4), channel_id=1, source_target_pairs={{0,256},{1,65},{2,258},{3,67},{4,260},{5,69},{6,262},{7,71},{8,264... | collective-permute-start | bytes 817160 | tf_op jit(solution)/shard_map/ppermute | solution.py:163
  14.6 1.5 copy.56
  17.0 3.5 %collective-permute-done.2 = bf16[56,2432]{1,0:T(8,128)(2,1)S(1)} collective-permute-done((bf16[56,2432]{1,0:T(8,128)(2,1)}, bf16[56,2432]{1,0:T(8,128)(2,1)S(1)}, u32[]{:S(2)}, u32[]{:S(2)}) %collective-permute-start.2) | collective-permute-done | bytes 272416 | tf_op jit(solution)/shard_map/ppermute | solution.py:163
  20.5 1.9 %collective-permute-start.6 = (bf16[112,2432]{1,0:T(8,128)(2,1)S(1)}, bf16[112,2432]{1,0:T(8,128)(2,1)S(1)}, u32[]{:S(2)}, u32[]{:S(2)}) collective-permute-start(bf16[112,2432]{1,0:T(8,128)(2,1)S(1)} %get-tuple-element.58), channel_id=1, source_target_pairs={{0,96},{1,385},{2,98},{3,387},{4,100},{5,389},{6,102},{7,391},{8,1... | collective-permute-start | bytes 1634312 | tf_op jit(solution)/shard_map/ppermute | solution.py:190
  22.4 3.9 %collective-permute-start.3 = (bf16[112,2432]{1,0:T(8,128)(2,1)S(1)}, bf16[112,2432]{1,0:T(8,128)(2,1)S(1)}, u32[]{:S(2)}, u32[]{:S(2)}) collective-permute-start(bf16[112,2432]{1,0:T(8,128)(2,1)S(1)} %get-tuple-element.62), channel_id=1, source_target_pairs={{0,32},{1,129},{2,34},{3,131},{4,36},{5,133},{6,38},{7,135},{8,40}... | collective-permute-start | bytes 1634312 | tf_op jit(solution)/shard_map/ppermute | solution.py:187
  26.4 1.9 %collective-permute-start.4 = (bf16[112,2432]{1,0:T(8,128)(2,1)S(1)}, bf16[112,2432]{1,0:T(8,128)(2,1)S(1)}, u32[]{:S(2)}, u32[]{:S(2)}) collective-permute-start(bf16[112,2432]{1,0:T(8,128)(2,1)S(1)} %get-tuple-element.58), channel_id=1, source_target_pairs={{0,32},{1,129},{2,34},{3,131},{4,36},{5,133},{6,38},{7,135},{8,40}... | collective-permute-start | bytes 1634312 | tf_op jit(solution)/shard_map/ppermute | solution.py:191
  28.8 5.1 %collective-permute-start.5 = (bf16[112,2432]{1,0:T(8,128)(2,1)S(1)}, bf16[112,2432]{1,0:T(8,128)(2,1)S(1)}, u32[]{:S(2)}, u32[]{:S(2)}) collective-permute-start(bf16[112,2432]{1,0:T(8,128)(2,1)S(1)} %get-tuple-element.62), channel_id=1, source_target_pairs={{0,96},{1,385},{2,98},{3,387},{4,100},{5,389},{6,102},{7,391},{8,1... | collective-permute-start | bytes 1634312 | tf_op jit(solution)/shard_map/ppermute | solution.py:188
  33.9 1.9 %collective-permute-start.8 = (bf16[112,2432]{1,0:T(8,128)(2,1)S(1)}, bf16[112,2432]{1,0:T(8,128)(2,1)S(1)}, u32[]{:S(2)}, u32[]{:S(2)}) collective-permute-start(bf16[112,2432]{1,0:T(8,128)(2,1)S(1)} %collective-permute-done.6), channel_id=1, source_target_pairs={{0,96},{1,385},{2,98},{3,387},{4,100},{5,389},{6,102},{7,391},{8,1... | collective-permute-start | bytes 1634312 | tf_op jit(solution)/shard_map/ppermute | solution.py:193
  35.9 3.9 %collective-permute-start.7 = (bf16[112,2432]{1,0:T(8,128)(2,1)S(1)}, bf16[112,2432]{1,0:T(8,128)(2,1)S(1)}, u32[]{:S(2)}, u32[]{:S(2)}) collective-permute-start(bf16[112,2432]{1,0:T(8,128)(2,1)S(1)} %collective-permute-done.3), channel_id=1, source_target_pairs={{0,32},{1,129},{2,34},{3,131},{4,36},{5,133},{6,38},{7,135},{8,40}... | collective-permute-start | bytes 1634312 | tf_op jit(solution)/shard_map/ppermute | solution.py:193
  39.8 0.9 collective-permute-done.4
  41.0 1.7 fusion.51
  42.8 5.6 %collective-permute-done.7 = bf16[112,2432]{1,0:T(8,128)(2,1)S(1)} collective-permute-done((bf16[112,2432]{1,0:T(8,128)(2,1)S(1)}, bf16[112,2432]{1,0:T(8,128)(2,1)S(1)}, u32[]{:S(2)}, u32[]{:S(2)}) %collective-permute-start.7) | collective-permute-done | bytes 544800 | tf_op jit(solution)/shard_map/ppermute | solution.py:193
  48.5 0.8 fusion.50
  49.5 1.8 %copy-done = f32[384,2432]{1,0:T(8,128)} copy-done((f32[384,2432]{1,0:T(8,128)}, f32[384,2432]{1,0:T(8,128)S(1)}, u32[]{:S(2)}) %copy-start) | copy-done | bytes 3735576
  51.3 2.2 %multiply_reduce_fusion.4 = (f32[384]{0:T(512)S(1)}, f32[384]{0:T(512)S(1)}, f32[384]{0:T(512)S(1)}, f32[384]{0:T(512)S(1)}, f32[384]{0:T(512)S(1)}) fusion(bf16[384,2432]{1,0:T(8,128)(2,1)S(1)} %copy-done.1, f32[384,2432]{1,0:T(8,128)S(1)} %get-tuple-element.78, f32[384]{0:T(512)S(1)} %fusion.1, f32[384]{0:T(512)S(1)} %get-tuple-element.77), kind=kLoop, calls=%fused_computation.8 | loop fusion | flops 11204736 | bytes 5614080 | tf_op jit(solution)/shard_map/reduce_sum | solution.py:212
  53.6 1.9 %collective-permute-start.9 = (f32[7,384]{1,0:T(8,128)S(1)}, f32[7,384]{1,0:T(8,128)S(1)}, u32[]{:S(2)}, u32[]{:S(2)}) collective-permute-start(f32[7,384]{1,0:T(8,128)S(1)} %stack.146), channel_id=1, source_target_pairs={{0,1},{1,0},{2,3},{3,2},{4,5},{5,4},{6,7},{7,6},{8,9},{9,8},{10,11... | collective-permute-start | bytes 32264 | tf_op jit(solution)/shard_map/ppermute | solution.py:215
  55.5 1.1 collective-permute-done.9
  56.9 29.7 %all_to_all.25 = f32[16,7,384]{2,1,0:T(8,128)S(1)} all-to-all(f32[16,7,384]{2,1,0:T(8,128)S(1)} %broadcast_in_dim.11), channel_id=1, replica_groups={{0,2,4,6,8,10,12,14,16,18,20,22,24,26,28,30},{1,3,5,7,9,11,13,15,17,19,..., dimensions={0} | all-to-all | bytes 344064 | tf_op jit(solution)/shard_map/all_to_all | solution.py:56
  86.8 6.2 %multiply_reduce_fusion.1 = (f32[2432]{0:T(1024)S(1)}, f32[2432]{0:T(1024)S(1)}, f32[2432]{0:T(1024)S(1)}, f32[2432]{0:T(1024)S(1)}, f32[2432]{0:T(1024)S(1)}, /*index=5*/f32[384,2432]{1,0:T(8,128)}) fusion(bf16[384,2432]{1,0:T(8,128)(2,1)S(1)} %copy-done.1, f32[384]{0:T(512)S(1)} %get-tuple-element.75, f32[384]{0:T(512)S(1)} %fusion.1, ...), kind=kLoop, calls=%fused_computation.5 | loop fusion | flops 13062272 | bytes 9393664 | tf_op jit(solution)/shard_map/reduce_sum | solution.py:232
  93.2 10.1 %all_to_all.26 = f32[4,5,2432]{2,1,0:T(8,128)S(1)} all-to-all(f32[4,5,2432]{2,1,0:T(8,128)S(1)} %broadcast_in_dim.12), channel_id=1, replica_groups={{0,128,256,384},{32,160,288,416},{64,192,320,448},{96,224,352,480},{1,3..., dimensions={0} | all-to-all | bytes 389120 | tf_op jit(solution)/shard_map/all_to_all | solution.py:56
  103.4 9.3 %all_to_all.27 = f32[4,5,2432]{2,1,0:T(8,128)S(1)} all-to-all(f32[4,5,2432]{2,1,0:T(8,128)S(1)} %broadcast_in_dim.13), channel_id=1, replica_groups={{0,32,64,96},{128,160,192,224},{256,288,320,352},{384,416,448,480},{1,1..., dimensions={0} | all-to-all | bytes 389120 | tf_op jit(solution)/shard_map/all_to_all | solution.py:56
  112.9 6.3 %fusion.44 = (f32[384]{0:T(512)S(1)}, f32[384]{0:T(512)S(1)}, f32[384,2432]{1,0:T(8,128)}) fusion(f32[384,2432]{1,0:T(8,128)} %get-tuple-element.45.q_ref, f32[2432]{0:T(1024)S(1)} %get-tuple-element.29, f32[2432]{0:T(1024)S(1)} %get-tuple-element.30, f32[2432]{0:T(1024)S(1)} %get-tuple-element.41, f32[2432]{0:T(1024)S(1)} %get-tuple-element.28, ...), kind=kLoop, calls=%fused_computation.128 | loop fusion | flops 15875328 | bytes 9387008 | tf_op jit(solution)/shard_map/reduce_sum | solution.py:253
  120.0 6.4 %all-to-all-start.3 = ((f32[32,1,384]{2,1,0:T(1,128)}), f32[32,1,384]{2,1,0:T(1,128)S(1)}, u32[]{:S(2)}, u32[]{:S(2)}) async-start(f32[32,1,384]{2,1,0:T(1,128)} %broadcast_in_dim.14), calls=%async_computation.3 | async-start | bytes 98304 | tf_op jit(solution)/shard_map/all_to_all | solution.py:56
  126.4 9.2 %shard_map.50.refs_2_ = f32[2,2,16,28,384]{4,3,2,1,0:T(8,128)S(1)} custom-call(s32[17]{0:T(128)S(1)} %pad_add_fusion.place_ref, f32[384,2432]{1,0:T(8,128)} %get-tuple-element.45.q_ref, f32[384,2432]{1,0:T(8,128)} %get-tuple-element.42.g_ref, f32[384,1]{1,0:T(8,128)S(1)} %div.157.mean_ref, bf16[672,2432]{1,0:T(8,128)(2,1)} %copy-done.2, ...), custom_call_target="tpu_custom_call" | custom-call | flops 3347054592 | bytes 14942208 | tf_op jit(solution)/shard_map/pallas_call | solution.py:256
  135.6 4.4 %all-to-all-done.3.refs_1_ = f32[32,1,384]{2,1,0:T(1,128)S(1)} async-done(((f32[32,1,384]{2,1,0:T(1,128)}), f32[32,1,384]{2,1,0:T(1,128)S(1)}, u32[]{:S(2)}, u32[]{:S(2)}) %all-to-all-start.3) | async-done | bytes 49184 | tf_op jit(solution)/shard_map/all_to_all | solution.py:56
  140.6 1.9 %collective-permute-start.10 = (f32[16,28,384]{2,0,1:T(8,128)S(1)}, f32[16,28,384]{2,0,1:T(8,128)S(1)}, u32[]{:S(2)}, u32[]{:S(2)}) collective-permute-start(f32[16,28,384]{2,0,1:T(8,128)S(1)} %copy.68), channel_id=1, source_target_pairs={{0,1},{1,0},{2,3},{3,2},{4,5},{5,4},{6,7},{7,6},{8,9},{9,8},{10,11... | collective-permute-start | bytes 2064392 | tf_op jit(solution)/shard_map/ppermute | solution.py:282
  142.6 2.1 %collective-permute-done.10 = f32[16,28,384]{2,0,1:T(8,128)S(1)} collective-permute-done((f32[16,28,384]{2,0,1:T(8,128)S(1)}, f32[16,28,384]{2,0,1:T(8,128)S(1)}, u32[]{:S(2)}, u32[]{:S(2)}) %collective-permute-start.10) | collective-permute-done | bytes 688160 | tf_op jit(solution)/shard_map/ppermute | solution.py:282
  145.7 7.5 %all-to-all-start.4 = ((bf16[16,28,384]{2,1,0:T(8,128)(2,1)}), bf16[16,28,384]{2,1,0:T(8,128)(2,1)S(1)}, u32[]{:S(2)}, u32[]{:S(2)}) async-start(bf16[16,28,384]{2,1,0:T(8,128)(2,1)} %shard_map.52), calls=%async_computation.4 | async-start | bytes 786432 | tf_op jit(solution)/shard_map/all_to_all | solution.py:284
  153.3 4.9 %multiply_convert_fusion = bf16[384,2432]{1,0:T(8,128)(2,1)} fusion(f32[384,2432]{1,0:T(8,128)} %get-tuple-element.45.q_ref, f32[384,2432]{1,0:T(8,128)} %get-tuple-element.42.g_ref, f32[384]{0:T(512)S(1)} %broadcast_multiply_fusion), kind=kLoop, calls=%fused_computation.2 | loop fusion | flops 3735552 | bytes 9340416 | tf_op jit(solution)/shard_map/convert_element_type | solution.py:285
  158.2 19.3 %all-to-all-done.4.share_ref = bf16[16,28,384]{2,1,0:T(8,128)(2,1)S(1)} async-done(((bf16[16,28,384]{2,1,0:T(8,128)(2,1)}), bf16[16,28,384]{2,1,0:T(8,128)(2,1)S(1)}, u32[]{:S(2)}, u32[]{:S(2)}) %all-to-all-start.4) | async-done | bytes 344096 | tf_op jit(solution)/shard_map/all_to_all | solution.py:284
  (82 shorter events, 5.8 us)
Async XLA Ops:
  0.6 16.3 %collective-permute-start = (bf16[56,2432]{1,0:T(8,128)(2,1)}, bf16[56,2432]{1,0:T(8,128)(2,1)S(1)}, u32[]{:S(2)}, u32[]{:S(2)}) collective-permute-start(bf16[56,2432]{1,0:T(8,128)(2,1)} %param.4), channel_id=1, source_target_pairs={{0,128},{1,33},{2,130},{3,35},{4,132},{5,37},{6,134},{7,39},{8,136... | collective-permute-start | bytes 817160 | tf_op jit(solution)/shard_map/ppermute | solution.py:163
  4.0 12.9 %collective-permute-start.1 = (bf16[56,2432]{1,0:T(8,128)(2,1)}, bf16[56,2432]{1,0:T(8,128)(2,1)S(1)}, u32[]{:S(2)}, u32[]{:S(2)}) collective-permute-start(bf16[56,2432]{1,0:T(8,128)(2,1)} %param.4), channel_id=1, source_target_pairs={{0,384},{1,97},{2,386},{3,99},{4,388},{5,101},{6,390},{7,103},{8,3... | collective-permute-start | bytes 817160 | tf_op jit(solution)/shard_map/ppermute | solution.py:163
  10.4 10.1 %collective-permute-start.2 = (bf16[56,2432]{1,0:T(8,128)(2,1)}, bf16[56,2432]{1,0:T(8,128)(2,1)S(1)}, u32[]{:S(2)}, u32[]{:S(2)}) collective-permute-start(bf16[56,2432]{1,0:T(8,128)(2,1)} %param.4), channel_id=1, source_target_pairs={{0,256},{1,65},{2,258},{3,67},{4,260},{5,69},{6,262},{7,71},{8,264... | collective-permute-start | bytes 817160 | tf_op jit(solution)/shard_map/ppermute | solution.py:163
  14.5 2.3 %copy-start.4 = (bf16[56,2432]{1,0:T(8,128)(2,1)S(1)}, bf16[56,2432]{1,0:T(8,128)(2,1)}, u32[]{:S(2)}) copy-start(bf16[56,2432]{1,0:T(8,128)(2,1)} %param.4) | copy-start | bytes 817156
  16.5 11.8 %copy-start.1 = (bf16[384,2432]{1,0:T(8,128)(2,1)S(1)}, bf16[384,2432]{1,0:T(8,128)(2,1)}, u32[]{:S(2)}) copy-start(bf16[384,2432]{1,0:T(8,128)(2,1)} %param.5) | copy-start | bytes 5603332
  20.5 13.4 %collective-permute-start.6 = (bf16[112,2432]{1,0:T(8,128)(2,1)S(1)}, bf16[112,2432]{1,0:T(8,128)(2,1)S(1)}, u32[]{:S(2)}, u32[]{:S(2)}) collective-permute-start(bf16[112,2432]{1,0:T(8,128)(2,1)S(1)} %get-tuple-element.58), channel_id=1, source_target_pairs={{0,96},{1,385},{2,98},{3,387},{4,100},{5,389},{6,102},{7,391},{8,1... | collective-permute-start | bytes 1634312 | tf_op jit(solution)/shard_map/ppermute | solution.py:190
  22.4 13.4 %collective-permute-start.3 = (bf16[112,2432]{1,0:T(8,128)(2,1)S(1)}, bf16[112,2432]{1,0:T(8,128)(2,1)S(1)}, u32[]{:S(2)}, u32[]{:S(2)}) collective-permute-start(bf16[112,2432]{1,0:T(8,128)(2,1)S(1)} %get-tuple-element.62), channel_id=1, source_target_pairs={{0,32},{1,129},{2,34},{3,131},{4,36},{5,133},{6,38},{7,135},{8,40}... | collective-permute-start | bytes 1634312 | tf_op jit(solution)/shard_map/ppermute | solution.py:187
  26.4 14.4 %collective-permute-start.4 = (bf16[112,2432]{1,0:T(8,128)(2,1)S(1)}, bf16[112,2432]{1,0:T(8,128)(2,1)S(1)}, u32[]{:S(2)}, u32[]{:S(2)}) collective-permute-start(bf16[112,2432]{1,0:T(8,128)(2,1)S(1)} %get-tuple-element.58), channel_id=1, source_target_pairs={{0,32},{1,129},{2,34},{3,131},{4,36},{5,133},{6,38},{7,135},{8,40}... | collective-permute-start | bytes 1634312 | tf_op jit(solution)/shard_map/ppermute | solution.py:191
  28.8 12.1 %collective-permute-start.5 = (bf16[112,2432]{1,0:T(8,128)(2,1)S(1)}, bf16[112,2432]{1,0:T(8,128)(2,1)S(1)}, u32[]{:S(2)}, u32[]{:S(2)}) collective-permute-start(bf16[112,2432]{1,0:T(8,128)(2,1)S(1)} %get-tuple-element.62), channel_id=1, source_target_pairs={{0,96},{1,385},{2,98},{3,387},{4,100},{5,389},{6,102},{7,391},{8,1... | collective-permute-start | bytes 1634312 | tf_op jit(solution)/shard_map/ppermute | solution.py:188
  33.9 14.5 %collective-permute-start.8 = (bf16[112,2432]{1,0:T(8,128)(2,1)S(1)}, bf16[112,2432]{1,0:T(8,128)(2,1)S(1)}, u32[]{:S(2)}, u32[]{:S(2)}) collective-permute-start(bf16[112,2432]{1,0:T(8,128)(2,1)S(1)} %collective-permute-done.6), channel_id=1, source_target_pairs={{0,96},{1,385},{2,98},{3,387},{4,100},{5,389},{6,102},{7,391},{8,1... | collective-permute-start | bytes 1634312 | tf_op jit(solution)/shard_map/ppermute | solution.py:193
  35.9 12.5 %collective-permute-start.7 = (bf16[112,2432]{1,0:T(8,128)(2,1)S(1)}, bf16[112,2432]{1,0:T(8,128)(2,1)S(1)}, u32[]{:S(2)}, u32[]{:S(2)}) collective-permute-start(bf16[112,2432]{1,0:T(8,128)(2,1)S(1)} %collective-permute-done.3), channel_id=1, source_target_pairs={{0,32},{1,129},{2,34},{3,131},{4,36},{5,133},{6,38},{7,135},{8,40}... | collective-permute-start | bytes 1634312 | tf_op jit(solution)/shard_map/ppermute | solution.py:193
  41.0 1.8 copy-start.2
  48.5 1.0 copy-start.3
  49.5 1.8 %copy-start = (f32[384,2432]{1,0:T(8,128)}, f32[384,2432]{1,0:T(8,128)S(1)}, u32[]{:S(2)}) copy-start(f32[384,2432]{1,0:T(8,128)S(1)} %get-tuple-element.78) | copy-start | bytes 11206660
  53.6 3.1 %collective-permute-start.9 = (f32[7,384]{1,0:T(8,128)S(1)}, f32[7,384]{1,0:T(8,128)S(1)}, u32[]{:S(2)}, u32[]{:S(2)}) collective-permute-start(f32[7,384]{1,0:T(8,128)S(1)} %stack.146), channel_id=1, source_target_pairs={{0,1},{1,0},{2,3},{3,2},{4,5},{5,4},{6,7},{7,6},{8,9},{9,8},{10,11... | collective-permute-start | bytes 32264 | tf_op jit(solution)/shard_map/ppermute | solution.py:215
  120.0 20.1 %all-to-all-start.3 = ((f32[32,1,384]{2,1,0:T(1,128)}), f32[32,1,384]{2,1,0:T(1,128)S(1)}, u32[]{:S(2)}, u32[]{:S(2)}) async-start(f32[32,1,384]{2,1,0:T(1,128)} %broadcast_in_dim.14), calls=%async_computation.3 | async-start | bytes 98304 | tf_op jit(solution)/shard_map/all_to_all | solution.py:56
  140.6 4.0 %collective-permute-start.10 = (f32[16,28,384]{2,0,1:T(8,128)S(1)}, f32[16,28,384]{2,0,1:T(8,128)S(1)}, u32[]{:S(2)}, u32[]{:S(2)}) collective-permute-start(f32[16,28,384]{2,0,1:T(8,128)S(1)} %copy.68), channel_id=1, source_target_pairs={{0,1},{1,0},{2,3},{3,2},{4,5},{5,4},{6,7},{7,6},{8,9},{9,8},{10,11... | collective-permute-start | bytes 2064392 | tf_op jit(solution)/shard_map/ppermute | solution.py:282
  145.7 31.8 %all-to-all-start.4 = ((bf16[16,28,384]{2,1,0:T(8,128)(2,1)}), bf16[16,28,384]{2,1,0:T(8,128)(2,1)S(1)}, u32[]{:S(2)}, u32[]{:S(2)}) async-start(bf16[16,28,384]{2,1,0:T(8,128)(2,1)} %shard_map.52), calls=%async_computation.4 | async-start | bytes 786432 | tf_op jit(solution)/shard_map/all_to_all | solution.py:284

commit v5 on v4

--- a/solution.py
+++ b/solution.py
@@ -97,16 +97,22 @@
         send_ref[j] = products_ref[0, 1, j] + shift * products_ref[1, 1, j]
 
 
-def add_kernel(a_ref, b_ref, out_ref):
+def add_kernel(a_ref, b_ref, out_ref, packed):
+    half, tok = a_ref.shape[1:]
     for j in range(out_ref.shape[0]):
-        out_ref[j] = (a_ref[j] + b_ref[j]).astype(BF16)
+        for k in range(tok // TILE):
+            at = slice(k * TILE, (k + 1) * TILE)
+            packed[j, k * half : (k + 1) * half] = a_ref[j, :, at] + b_ref[j, :, at]
+        out_ref[j] = packed[j].astype(BF16)
 
 
 def last_kernel(share_ref, out_ref):
+    half, tok = out_ref.shape
     total = share_ref[0].astype(F32)
     for j in range(1, share_ref.shape[0]):
         total = total + share_ref[j].astype(F32)
-    out_ref[...] = total
+    for k in range(tok // TILE):
+        out_ref[:, k * TILE : (k + 1) * TILE] = total[k * half : (k + 1) * half]
 
 
 def _call(kernel, steps, in_specs, out_specs, out_shape, scratch, flops, nbytes):
@@ -128,10 +134,11 @@
     return pltpu.with_memory_space_constraint(x, pltpu.HBM)
 
 
-def _small(kernel, out_shape, *args):
+def _small(kernel, out_shape, *args, scratch=()):
     return pl.pallas_call(
         kernel,
         out_shape=out_shape,
+        scratch_shapes=scratch,
         compiler_params=pltpu.CompilerParams(vmem_limit_bytes=GRANT),
         cost_estimate=pl.CostEstimate(flops=1000000, bytes_accessed=4000000, transcendentals=0),
     )(*args)
@@ -277,9 +284,10 @@
     )
     share = _small(
         add_kernel,
-        jax.ShapeDtypeStruct((DP, half, tok_rows), BF16),
+        jax.ShapeDtypeStruct((DP, half * steps, TILE), BF16),
         keep,
         lax.ppermute(send, "vocab", PAIR),
+        scratch=[pltpu.VMEM((DP, half * steps, TILE), F32)],
     )
     share = lax.all_to_all(share, "vocab", 0, 0, tiled=True, axis_index_groups=COLUMN)
     logit_grad = (prob_s * (coeff - row_dot[:, None]) / TEMP).astype(BF16)

time: 179 us -> 178 us (level)
  transfers between devices with their start and end apart: 13 -> 13, of which waited for: 7 -> 7; matrix products, arithmetic and copies ran while one was open for 5% -> 6% of each run, Pallas kernels for 5% -> 5%
where the time goes in v5:
time: 178 us; the launch traced here: 177 us
  starting transfers between devices  50.2 us (28%)
  blocking collectives  49.1 us (28%)
  waiting for transfers between devices  35.7 us (20%)
  other arithmetic  21.7 us (12%)
  Pallas kernels  10.3 us (6%)
  local copies, waits for them, and re-layouts  6.07 us (3%)
  matrix products  2.57 us (1%)
    all_to_all x3, blocking collectives, spread(): lax.all_to_all(copies, axis, 0, 0, tiled=True, axis_index_groups=groups)  49.1 us
    all_to_all x1, waiting for transfers between devices, body(): lax.all_to_all(share, 'vocab', 0, 0, tiled=True, axis_index_groups=COLUMN)  18 us
    ppermute x3, starting transfers between devices, body(): lax.ppermute(head_weight, AXES, pairs)  13.7 us
    pallas_call x1, Pallas kernels, body(): _call(product_kernel, steps, [pl.BlockSpec(memory_space=pltpu.SMEM), tile...  9.24 us
    all_to_all x1, starting transfers between devices, body(): lax.all_to_all(share, 'vocab', 0, 0, tiled=True, axis_index_groups=COLUMN)  7.48 us
    all_to_all x1, starting transfers between devices, spread(): lax.all_to_all(copies, axis, 0, 0, tiled=True, axis_index_groups=groups)  6.39 us
    reduce_sum x1, other arithmetic, body(): mean = own_dot / jnp.maximum(jnp.sum(prob_s, 1), 1e-30)  6.3 us
    reduce_sum x1, other arithmetic, body(): jnp.sum(prob_s * prob_t, 0)  6.25 us
  transfers between devices with their start and end apart: 13, of which 7 were waited for; matrix products, arithmetic and copies ran while one was open for 6% of the time, Pallas kernels for 5%

profile of v5, /device:TPU:2, one launch (start us, length us, event | category | flops | bytes accessed | tf_op | source)
XLA Modules:
  0.0 177.0 jit_solution(430231843817364102)
XLA Ops:
  0.6 3.4 %collective-permute-start = (bf16[56,2432]{1,0:T(8,128)(2,1)}, bf16[56,2432]{1,0:T(8,128)(2,1)S(1)}, u32[]{:S(2)}, u32[]{:S(2)}) collective-permute-start(bf16[56,2432]{1,0:T(8,128)(2,1)} %param.4), channel_id=1, source_target_pairs={{0,128},{1,33},{2,130},{3,35},{4,132},{5,37},{6,134},{7,39},{8,136... | collective-permute-start | bytes 817160 | tf_op jit(solution)/shard_map/ppermute | solution.py:170
  4.0 6.3 %collective-permute-start.1 = (bf16[56,2432]{1,0:T(8,128)(2,1)}, bf16[56,2432]{1,0:T(8,128)(2,1)S(1)}, u32[]{:S(2)}, u32[]{:S(2)}) collective-permute-start(bf16[56,2432]{1,0:T(8,128)(2,1)} %param.4), channel_id=1, source_target_pairs={{0,384},{1,97},{2,386},{3,99},{4,388},{5,101},{6,390},{7,103},{8,3... | collective-permute-start | bytes 817160 | tf_op jit(solution)/shard_map/ppermute | solution.py:170
  10.4 4.0 %collective-permute-start.2 = (bf16[56,2432]{1,0:T(8,128)(2,1)}, bf16[56,2432]{1,0:T(8,128)(2,1)S(1)}, u32[]{:S(2)}, u32[]{:S(2)}) collective-permute-start(bf16[56,2432]{1,0:T(8,128)(2,1)} %param.4), channel_id=1, source_target_pairs={{0,256},{1,65},{2,258},{3,67},{4,260},{5,69},{6,262},{7,71},{8,264... | collective-permute-start | bytes 817160 | tf_op jit(solution)/shard_map/ppermute | solution.py:170
  14.6 1.5 copy.56
  17.0 3.5 %collective-permute-done.2 = bf16[56,2432]{1,0:T(8,128)(2,1)S(1)} collective-permute-done((bf16[56,2432]{1,0:T(8,128)(2,1)}, bf16[56,2432]{1,0:T(8,128)(2,1)S(1)}, u32[]{:S(2)}, u32[]{:S(2)}) %collective-permute-start.2) | collective-permute-done | bytes 272416 | tf_op jit(solution)/shard_map/ppermute | solution.py:170
  20.5 1.9 %collective-permute-start.6 = (bf16[112,2432]{1,0:T(8,128)(2,1)S(1)}, bf16[112,2432]{1,0:T(8,128)(2,1)S(1)}, u32[]{:S(2)}, u32[]{:S(2)}) collective-permute-start(bf16[112,2432]{1,0:T(8,128)(2,1)S(1)} %get-tuple-element.58), channel_id=1, source_target_pairs={{0,96},{1,385},{2,98},{3,387},{4,100},{5,389},{6,102},{7,391},{8,1... | collective-permute-start | bytes 1634312 | tf_op jit(solution)/shard_map/ppermute | solution.py:197
  22.4 3.9 %collective-permute-start.3 = (bf16[112,2432]{1,0:T(8,128)(2,1)S(1)}, bf16[112,2432]{1,0:T(8,128)(2,1)S(1)}, u32[]{:S(2)}, u32[]{:S(2)}) collective-permute-start(bf16[112,2432]{1,0:T(8,128)(2,1)S(1)} %get-tuple-element.62), channel_id=1, source_target_pairs={{0,32},{1,129},{2,34},{3,131},{4,36},{5,133},{6,38},{7,135},{8,40}... | collective-permute-start | bytes 1634312 | tf_op jit(solution)/shard_map/ppermute | solution.py:194
  26.4 1.9 %collective-permute-start.4 = (bf16[112,2432]{1,0:T(8,128)(2,1)S(1)}, bf16[112,2432]{1,0:T(8,128)(2,1)S(1)}, u32[]{:S(2)}, u32[]{:S(2)}) collective-permute-start(bf16[112,2432]{1,0:T(8,128)(2,1)S(1)} %get-tuple-element.58), channel_id=1, source_target_pairs={{0,32},{1,129},{2,34},{3,131},{4,36},{5,133},{6,38},{7,135},{8,40}... | collective-permute-start | bytes 1634312 | tf_op jit(solution)/shard_map/ppermute | solution.py:198
  28.8 5.1 %collective-permute-start.5 = (bf16[112,2432]{1,0:T(8,128)(2,1)S(1)}, bf16[112,2432]{1,0:T(8,128)(2,1)S(1)}, u32[]{:S(2)}, u32[]{:S(2)}) collective-permute-start(bf16[112,2432]{1,0:T(8,128)(2,1)S(1)} %get-tuple-element.62), channel_id=1, source_target_pairs={{0,96},{1,385},{2,98},{3,387},{4,100},{5,389},{6,102},{7,391},{8,1... | collective-permute-start | bytes 1634312 | tf_op jit(solution)/shard_map/ppermute | solution.py:195
  33.9 1.9 %collective-permute-start.8 = (bf16[112,2432]{1,0:T(8,128)(2,1)S(1)}, bf16[112,2432]{1,0:T(8,128)(2,1)S(1)}, u32[]{:S(2)}, u32[]{:S(2)}) collective-permute-start(bf16[112,2432]{1,0:T(8,128)(2,1)S(1)} %collective-permute-done.6), channel_id=1, source_target_pairs={{0,96},{1,385},{2,98},{3,387},{4,100},{5,389},{6,102},{7,391},{8,1... | collective-permute-start | bytes 1634312 | tf_op jit(solution)/shard_map/ppermute | solution.py:200
  35.9 3.9 %collective-permute-start.7 = (bf16[112,2432]{1,0:T(8,128)(2,1)S(1)}, bf16[112,2432]{1,0:T(8,128)(2,1)S(1)}, u32[]{:S(2)}, u32[]{:S(2)}) collective-permute-start(bf16[112,2432]{1,0:T(8,128)(2,1)S(1)} %collective-permute-done.3), channel_id=1, source_target_pairs={{0,32},{1,129},{2,34},{3,131},{4,36},{5,133},{6,38},{7,135},{8,40}... | collective-permute-start | bytes 1634312 | tf_op jit(solution)/shard_map/ppermute | solution.py:200
  39.8 0.9 collective-permute-done.4
  41.0 1.7 fusion.51
  42.8 5.6 %collective-permute-done.7 = bf16[112,2432]{1,0:T(8,128)(2,1)S(1)} collective-permute-done((bf16[112,2432]{1,0:T(8,128)(2,1)S(1)}, bf16[112,2432]{1,0:T(8,128)(2,1)S(1)}, u32[]{:S(2)}, u32[]{:S(2)}) %collective-permute-start.7) | collective-permute-done | bytes 544800 | tf_op jit(solution)/shard_map/ppermute | solution.py:200
  49.5 1.8 %copy-done = f32[384,2432]{1,0:T(8,128)} copy-done((f32[384,2432]{1,0:T(8,128)}, f32[384,2432]{1,0:T(8,128)S(1)}, u32[]{:S(2)}) %copy-start) | copy-done | bytes 3735576
  51.3 2.2 %multiply_reduce_fusion.4 = (f32[384]{0:T(512)S(1)}, f32[384]{0:T(512)S(1)}, f32[384]{0:T(512)S(1)}, f32[384]{0:T(512)S(1)}, f32[384]{0:T(512)S(1)}) fusion(bf16[384,2432]{1,0:T(8,128)(2,1)S(1)} %copy-done.1, f32[384,2432]{1,0:T(8,128)S(1)} %get-tuple-element.78, f32[384]{0:T(512)S(1)} %fusion.1, f32[384]{0:T(512)S(1)} %get-tuple-element.77), kind=kLoop, calls=%fused_computation.8 | loop fusion | flops 11204736 | bytes 5614080 | tf_op jit(solution)/shard_map/reduce_sum | solution.py:219
  53.6 1.9 %collective-permute-start.9 = (f32[7,384]{1,0:T(8,128)S(1)}, f32[7,384]{1,0:T(8,128)S(1)}, u32[]{:S(2)}, u32[]{:S(2)}) collective-permute-start(f32[7,384]{1,0:T(8,128)S(1)} %stack.146), channel_id=1, source_target_pairs={{0,1},{1,0},{2,3},{3,2},{4,5},{5,4},{6,7},{7,6},{8,9},{9,8},{10,11... | collective-permute-start | bytes 32264 | tf_op jit(solution)/shard_map/ppermute | solution.py:222
  55.5 1.1 collective-permute-done.9
  56.9 29.7 %all_to_all.25 = f32[16,7,384]{2,1,0:T(8,128)S(1)} all-to-all(f32[16,7,384]{2,1,0:T(8,128)S(1)} %broadcast_in_dim.11), channel_id=1, replica_groups={{0,2,4,6,8,10,12,14,16,18,20,22,24,26,28,30},{1,3,5,7,9,11,13,15,17,19,..., dimensions={0} | all-to-all | bytes 344064 | tf_op jit(solution)/shard_map/all_to_all | solution.py:56
  86.8 6.2 %multiply_reduce_fusion.1 = (f32[2432]{0:T(1024)S(1)}, f32[2432]{0:T(1024)S(1)}, f32[2432]{0:T(1024)S(1)}, f32[2432]{0:T(1024)S(1)}, f32[2432]{0:T(1024)S(1)}, /*index=5*/f32[384,2432]{1,0:T(8,128)}) fusion(bf16[384,2432]{1,0:T(8,128)(2,1)S(1)} %copy-done.1, f32[384]{0:T(512)S(1)} %get-tuple-element.75, f32[384]{0:T(512)S(1)} %fusion.1, ...), kind=kLoop, calls=%fused_computation.5 | loop fusion | flops 13062272 | bytes 9393664 | tf_op jit(solution)/shard_map/reduce_sum | solution.py:239
  93.2 10.1 %all_to_all.26 = f32[4,5,2432]{2,1,0:T(8,128)S(1)} all-to-all(f32[4,5,2432]{2,1,0:T(8,128)S(1)} %broadcast_in_dim.12), channel_id=1, replica_groups={{0,128,256,384},{32,160,288,416},{64,192,320,448},{96,224,352,480},{1,3..., dimensions={0} | all-to-all | bytes 389120 | tf_op jit(solution)/shard_map/all_to_all | solution.py:56
  103.4 9.3 %all_to_all.27 = f32[4,5,2432]{2,1,0:T(8,128)S(1)} all-to-all(f32[4,5,2432]{2,1,0:T(8,128)S(1)} %broadcast_in_dim.13), channel_id=1, replica_groups={{0,32,64,96},{128,160,192,224},{256,288,320,352},{384,416,448,480},{1,1..., dimensions={0} | all-to-all | bytes 389120 | tf_op jit(solution)/shard_map/all_to_all | solution.py:56
  112.9 6.3 %fusion.44 = (f32[384]{0:T(512)S(1)}, f32[384]{0:T(512)S(1)}, f32[384,2432]{1,0:T(8,128)}) fusion(f32[384,2432]{1,0:T(8,128)} %get-tuple-element.45.q_ref, f32[2432]{0:T(1024)S(1)} %get-tuple-element.29, f32[2432]{0:T(1024)S(1)} %get-tuple-element.30, f32[2432]{0:T(1024)S(1)} %get-tuple-element.41, f32[2432]{0:T(1024)S(1)} %get-tuple-element.28, ...), kind=kLoop, calls=%fused_computation.128 | loop fusion | flops 15875328 | bytes 9387008 | tf_op jit(solution)/shard_map/reduce_sum | solution.py:260
  120.0 6.4 %all-to-all-start.3 = ((f32[32,1,384]{2,1,0:T(1,128)}), f32[32,1,384]{2,1,0:T(1,128)S(1)}, u32[]{:S(2)}, u32[]{:S(2)}) async-start(f32[32,1,384]{2,1,0:T(1,128)} %broadcast_in_dim.14), calls=%async_computation.3 | async-start | bytes 98304 | tf_op jit(solution)/shard_map/all_to_all | solution.py:56
  126.4 9.2 %shard_map.50.refs_2_ = f32[2,2,16,28,384]{4,3,2,1,0:T(8,128)S(1)} custom-call(s32[17]{0:T(128)S(1)} %pad_add_fusion.place_ref, f32[384,2432]{1,0:T(8,128)} %get-tuple-element.45.q_ref, f32[384,2432]{1,0:T(8,128)} %get-tuple-element.42.g_ref, f32[384,1]{1,0:T(8,128)S(1)} %div.157.mean_ref, bf16[672,2432]{1,0:T(8,128)(2,1)} %copy-done.2, ...), custom_call_target="tpu_custom_call" | custom-call | flops 3347054592 | bytes 14942208 | tf_op jit(solution)/shard_map/pallas_call | solution.py:263
  135.6 4.4 %all-to-all-done.3.refs_1_ = f32[32,1,384]{2,1,0:T(1,128)S(1)} async-done(((f32[32,1,384]{2,1,0:T(1,128)}), f32[32,1,384]{2,1,0:T(1,128)S(1)}, u32[]{:S(2)}, u32[]{:S(2)}) %all-to-all-start.3) | async-done | bytes 49184 | tf_op jit(solution)/shard_map/all_to_all | solution.py:56
  140.6 1.9 %collective-permute-start.10 = (f32[16,28,384]{2,0,1:T(8,128)S(1)}, f32[16,28,384]{2,0,1:T(8,128)S(1)}, u32[]{:S(2)}, u32[]{:S(2)}) collective-permute-start(f32[16,28,384]{2,0,1:T(8,128)S(1)} %copy.68), channel_id=1, source_target_pairs={{0,1},{1,0},{2,3},{3,2},{4,5},{5,4},{6,7},{7,6},{8,9},{9,8},{10,11... | collective-permute-start | bytes 2064392 | tf_op jit(solution)/shard_map/ppermute | solution.py:289
  142.6 2.1 %collective-permute-done.10 = f32[16,28,384]{2,0,1:T(8,128)S(1)} collective-permute-done((f32[16,28,384]{2,0,1:T(8,128)S(1)}, f32[16,28,384]{2,0,1:T(8,128)S(1)}, u32[]{:S(2)}, u32[]{:S(2)}) %collective-permute-start.10) | collective-permute-done | bytes 688160 | tf_op jit(solution)/shard_map/ppermute | solution.py:289
  144.9 0.9 shard_map.52
  145.8 7.5 %all-to-all-start.4 = ((bf16[16,84,128]{2,1,0:T(8,128)(2,1)}), bf16[16,84,128]{2,1,0:T(8,128)(2,1)S(1)}, u32[]{:S(2)}, u32[]{:S(2)}) async-start(bf16[16,84,128]{2,1,0:T(8,128)(2,1)} %shard_map.52), calls=%async_computation.4 | async-start | bytes 720896 | tf_op jit(solution)/shard_map/all_to_all | solution.py:292
  153.3 4.9 %multiply_convert_fusion = bf16[384,2432]{1,0:T(8,128)(2,1)} fusion(f32[384,2432]{1,0:T(8,128)} %get-tuple-element.45.q_ref, f32[384,2432]{1,0:T(8,128)} %get-tuple-element.42.g_ref, f32[384]{0:T(512)S(1)} %broadcast_multiply_fusion), kind=kLoop, calls=%fused_computation.2 | loop fusion | flops 3735552 | bytes 9340416 | tf_op jit(solution)/shard_map/convert_element_type | solution.py:293
  158.3 18.0 %all-to-all-done.4.share_ref = bf16[16,84,128]{2,1,0:T(8,128)(2,1)S(1)} async-done(((bf16[16,84,128]{2,1,0:T(8,128)(2,1)}), bf16[16,84,128]{2,1,0:T(8,128)(2,1)S(1)}, u32[]{:S(2)}, u32[]{:S(2)}) %all-to-all-start.4) | async-done | bytes 344096 | tf_op jit(solution)/shard_map/all_to_all | solution.py:292
  (82 shorter events, 5.8 us)
Async XLA Ops:
  0.6 16.3 %collective-permute-start = (bf16[56,2432]{1,0:T(8,128)(2,1)}, bf16[56,2432]{1,0:T(8,128)(2,1)S(1)}, u32[]{:S(2)}, u32[]{:S(2)}) collective-permute-start(bf16[56,2432]{1,0:T(8,128)(2,1)} %param.4), channel_id=1, source_target_pairs={{0,128},{1,33},{2,130},{3,35},{4,132},{5,37},{6,134},{7,39},{8,136... | collective-permute-start | bytes 817160 | tf_op jit(solution)/shard_map/ppermute | solution.py:170
  4.0 12.9 %collective-permute-start.1 = (bf16[56,2432]{1,0:T(8,128)(2,1)}, bf16[56,2432]{1,0:T(8,128)(2,1)S(1)}, u32[]{:S(2)}, u32[]{:S(2)}) collective-permute-start(bf16[56,2432]{1,0:T(8,128)(2,1)} %param.4), channel_id=1, source_target_pairs={{0,384},{1,97},{2,386},{3,99},{4,388},{5,101},{6,390},{7,103},{8,3... | collective-permute-start | bytes 817160 | tf_op jit(solution)/shard_map/ppermute | solution.py:170
  10.4 10.1 %collective-permute-start.2 = (bf16[56,2432]{1,0:T(8,128)(2,1)}, bf16[56,2432]{1,0:T(8,128)(2,1)S(1)}, u32[]{:S(2)}, u32[]{:S(2)}) collective-permute-start(bf16[56,2432]{1,0:T(8,128)(2,1)} %param.4), channel_id=1, source_target_pairs={{0,256},{1,65},{2,258},{3,67},{4,260},{5,69},{6,262},{7,71},{8,264... | collective-permute-start | bytes 817160 | tf_op jit(solution)/shard_map/ppermute | solution.py:170
  14.5 2.3 %copy-start.4 = (bf16[56,2432]{1,0:T(8,128)(2,1)S(1)}, bf16[56,2432]{1,0:T(8,128)(2,1)}, u32[]{:S(2)}) copy-start(bf16[56,2432]{1,0:T(8,128)(2,1)} %param.4) | copy-start | bytes 817156
  16.5 11.8 %copy-start.1 = (bf16[384,2432]{1,0:T(8,128)(2,1)S(1)}, bf16[384,2432]{1,0:T(8,128)(2,1)}, u32[]{:S(2)}) copy-start(bf16[384,2432]{1,0:T(8,128)(2,1)} %param.5) | copy-start | bytes 5603332
  20.5 13.4 %collective-permute-start.6 = (bf16[112,2432]{1,0:T(8,128)(2,1)S(1)}, bf16[112,2432]{1,0:T(8,128)(2,1)S(1)}, u32[]{:S(2)}, u32[]{:S(2)}) collective-permute-start(bf16[112,2432]{1,0:T(8,128)(2,1)S(1)} %get-tuple-element.58), channel_id=1, source_target_pairs={{0,96},{1,385},{2,98},{3,387},{4,100},{5,389},{6,102},{7,391},{8,1... | collective-permute-start | bytes 1634312 | tf_op jit(solution)/shard_map/ppermute | solution.py:197
  22.4 13.4 %collective-permute-start.3 = (bf16[112,2432]{1,0:T(8,128)(2,1)S(1)}, bf16[112,2432]{1,0:T(8,128)(2,1)S(1)}, u32[]{:S(2)}, u32[]{:S(2)}) collective-permute-start(bf16[112,2432]{1,0:T(8,128)(2,1)S(1)} %get-tuple-element.62), channel_id=1, source_target_pairs={{0,32},{1,129},{2,34},{3,131},{4,36},{5,133},{6,38},{7,135},{8,40}... | collective-permute-start | bytes 1634312 | tf_op jit(solution)/shard_map/ppermute | solution.py:194
  26.4 14.4 %collective-permute-start.4 = (bf16[112,2432]{1,0:T(8,128)(2,1)S(1)}, bf16[112,2432]{1,0:T(8,128)(2,1)S(1)}, u32[]{:S(2)}, u32[]{:S(2)}) collective-permute-start(bf16[112,2432]{1,0:T(8,128)(2,1)S(1)} %get-tuple-element.58), channel_id=1, source_target_pairs={{0,32},{1,129},{2,34},{3,131},{4,36},{5,133},{6,38},{7,135},{8,40}... | collective-permute-start | bytes 1634312 | tf_op jit(solution)/shard_map/ppermute | solution.py:198
  28.8 12.1 %collective-permute-start.5 = (bf16[112,2432]{1,0:T(8,128)(2,1)S(1)}, bf16[112,2432]{1,0:T(8,128)(2,1)S(1)}, u32[]{:S(2)}, u32[]{:S(2)}) collective-permute-start(bf16[112,2432]{1,0:T(8,128)(2,1)S(1)} %get-tuple-element.62), channel_id=1, source_target_pairs={{0,96},{1,385},{2,98},{3,387},{4,100},{5,389},{6,102},{7,391},{8,1... | collective-permute-start | bytes 1634312 | tf_op jit(solution)/shard_map/ppermute | solution.py:195
  33.9 14.5 %collective-permute-start.8 = (bf16[112,2432]{1,0:T(8,128)(2,1)S(1)}, bf16[112,2432]{1,0:T(8,128)(2,1)S(1)}, u32[]{:S(2)}, u32[]{:S(2)}) collective-permute-start(bf16[112,2432]{1,0:T(8,128)(2,1)S(1)} %collective-permute-done.6), channel_id=1, source_target_pairs={{0,96},{1,385},{2,98},{3,387},{4,100},{5,389},{6,102},{7,391},{8,1... | collective-permute-start | bytes 1634312 | tf_op jit(solution)/shard_map/ppermute | solution.py:200
  35.9 12.5 %collective-permute-start.7 = (bf16[112,2432]{1,0:T(8,128)(2,1)S(1)}, bf16[112,2432]{1,0:T(8,128)(2,1)S(1)}, u32[]{:S(2)}, u32[]{:S(2)}) collective-permute-start(bf16[112,2432]{1,0:T(8,128)(2,1)S(1)} %collective-permute-done.3), channel_id=1, source_target_pairs={{0,32},{1,129},{2,34},{3,131},{4,36},{5,133},{6,38},{7,135},{8,40}... | collective-permute-start | bytes 1634312 | tf_op jit(solution)/shard_map/ppermute | solution.py:200
  41.0 1.8 copy-start.2
  48.5 1.0 copy-start.3
  49.5 1.8 %copy-start = (f32[384,2432]{1,0:T(8,128)}, f32[384,2432]{1,0:T(8,128)S(1)}, u32[]{:S(2)}) copy-start(f32[384,2432]{1,0:T(8,128)S(1)} %get-tuple-element.78) | copy-start | bytes 11206660
  53.6 3.1 %collective-permute-start.9 = (f32[7,384]{1,0:T(8,128)S(1)}, f32[7,384]{1,0:T(8,128)S(1)}, u32[]{:S(2)}, u32[]{:S(2)}) collective-permute-start(f32[7,384]{1,0:T(8,128)S(1)} %stack.146), channel_id=1, source_target_pairs={{0,1},{1,0},{2,3},{3,2},{4,5},{5,4},{6,7},{7,6},{8,9},{9,8},{10,11... | collective-permute-start | bytes 32264 | tf_op jit(solution)/shard_map/ppermute | solution.py:222
  120.0 20.1 %all-to-all-start.3 = ((f32[32,1,384]{2,1,0:T(1,128)}), f32[32,1,384]{2,1,0:T(1,128)S(1)}, u32[]{:S(2)}, u32[]{:S(2)}) async-start(f32[32,1,384]{2,1,0:T(1,128)} %broadcast_in_dim.14), calls=%async_computation.3 | async-start | bytes 98304 | tf_op jit(solution)/shard_map/all_to_all | solution.py:56
  140.6 4.0 %collective-permute-start.10 = (f32[16,28,384]{2,0,1:T(8,128)S(1)}, f32[16,28,384]{2,0,1:T(8,128)S(1)}, u32[]{:S(2)}, u32[]{:S(2)}) collective-permute-start(f32[16,28,384]{2,0,1:T(8,128)S(1)} %copy.68), channel_id=1, source_target_pairs={{0,1},{1,0},{2,3},{3,2},{4,5},{5,4},{6,7},{7,6},{8,9},{9,8},{10,11... | collective-permute-start | bytes 2064392 | tf_op jit(solution)/shard_map/ppermute | solution.py:289
  145.8 30.5 %all-to-all-start.4 = ((bf16[16,84,128]{2,1,0:T(8,128)(2,1)}), bf16[16,84,128]{2,1,0:T(8,128)(2,1)S(1)}, u32[]{:S(2)}, u32[]{:S(2)}) async-start(bf16[16,84,128]{2,1,0:T(8,128)(2,1)} %shard_map.52), calls=%async_computation.4 | async-start | bytes 720896 | tf_op jit(solution)/shard_map/all_to_all | solution.py:292

commit v6 on v5

--- a/solution.py
+++ b/solution.py
@@ -18,22 +18,6 @@
 F32, BF16 = jnp.float32, jnp.bfloat16
 
 
-def _plane_groups(flip):
-    groups = []
-    for z in range(CHIPS):
-        for core in range(CORES):
-            for other in range(SIDE):
-                along_x = (core ^ flip) == 0
-                groups.append(
-                    [
-                        ((i * SIDE + other) if along_x else (other * SIDE + i)) * VOCAB + z * CORES + core
-                        for i in range(SIDE)
-                    ]
-                )
-    return groups
-
-
-FIRST, SECOND = _plane_groups(0), _plane_groups(1)
 def _step_pairs(step, second):
     pairs = []
     for x in range(SIDE):
@@ -239,8 +223,7 @@
             jnp.sum(prob_s * prob_t, 0),
         ]
     )
-    sums = jnp.sum(spread(sums, SIDE, AXES, FIRST), 0)
-    sums = jnp.sum(spread(sums, SIDE, AXES, SECOND), 0)
+    sums = jnp.sum(spread(sums, DP, "dp"), 0)
     mean_s = sums[0] / tokens
     mean_t = sums[1] / tokens
     col_var = sums[2] / tokens - mean_s * mean_s

time: 178 us -> 181 us (1.017)
  starting transfers between devices: 50.2 us -> 52.9 us
    all_to_all x1, starting transfers between devices: 6.39 us -> 9.11 us  [spread(): lax.all_to_all(copies, axis, 0, 0, tiled=True, axis_index_groups=groups)]
    all_to_all x3 -> x2, blocking collectives: 49.1 us -> 49.2 us  [spread(): lax.all_to_all(copies, axis, 0, 0, tiled=True, axis_index_groups=groups)]
  transfers between devices with their start and end apart: 13 -> 13, of which waited for: 7 -> 7; matrix products, arithmetic and copies ran while one was open for 6% -> 5% of each run, Pallas kernels for 5% -> 5%
where the time goes in v6:
time: 181 us; the launch traced here: 180 us
  starting transfers between devices  52.9 us (29%)
  blocking collectives  49.2 us (27%)
  waiting for transfers between devices  35.7 us (20%)
  other arithmetic  21.7 us (12%)
  Pallas kernels  10.3 us (6%)
  local copies, waits for them, and re-layouts  6.11 us (3%)
  matrix products  2.57 us (1%)
    all_to_all x2, blocking collectives, spread(): lax.all_to_all(copies, axis, 0, 0, tiled=True, axis_index_groups=groups)  49.2 us
    all_to_all x1, waiting for transfers between devices, body(): lax.all_to_all(share, 'vocab', 0, 0, tiled=True, axis_index_groups=COLUMN)  18 us
    ppermute x3, starting transfers between devices, body(): lax.ppermute(head_weight, AXES, pairs)  13.7 us
    pallas_call x1, Pallas kernels, body(): _call(product_kernel, steps, [pl.BlockSpec(memory_space=pltpu.SMEM), tile...  9.23 us
    all_to_all x1, starting transfers between devices, spread(): lax.all_to_all(copies, axis, 0, 0, tiled=True, axis_index_groups=groups)  9.11 us
    all_to_all x1, starting transfers between devices, body(): lax.all_to_all(share, 'vocab', 0, 0, tiled=True, axis_index_groups=COLUMN)  7.5 us
    reduce_sum x1, other arithmetic, body(): mean = own_dot / jnp.maximum(jnp.sum(prob_s, 1), 1e-30)  6.3 us
    reduce_sum x1, other arithmetic, body(): jnp.sum(prob_s * prob_t, 0)  6.25 us
  transfers between devices with their start and end apart: 13, of which 7 were waited for; matrix products, arithmetic and copies ran while one was open for 5% of the time, Pallas kernels for 5%

profile of v6, /device:TPU:2, one launch (start us, length us, event | category | flops | bytes accessed | tf_op | source)
XLA Modules:
  0.0 179.9 jit_solution(820780875593252678)
XLA Ops:
  0.6 3.4 %collective-permute-start = (bf16[56,2432]{1,0:T(8,128)(2,1)}, bf16[56,2432]{1,0:T(8,128)(2,1)S(1)}, u32[]{:S(2)}, u32[]{:S(2)}) collective-permute-start(bf16[56,2432]{1,0:T(8,128)(2,1)} %param.4), channel_id=1, source_target_pairs={{0,128},{1,33},{2,130},{3,35},{4,132},{5,37},{6,134},{7,39},{8,136... | collective-permute-start | bytes 817160 | tf_op jit(solution)/shard_map/ppermute | solution.py:154
  4.0 6.3 %collective-permute-start.1 = (bf16[56,2432]{1,0:T(8,128)(2,1)}, bf16[56,2432]{1,0:T(8,128)(2,1)S(1)}, u32[]{:S(2)}, u32[]{:S(2)}) collective-permute-start(bf16[56,2432]{1,0:T(8,128)(2,1)} %param.4), channel_id=1, source_target_pairs={{0,384},{1,97},{2,386},{3,99},{4,388},{5,101},{6,390},{7,103},{8,3... | collective-permute-start | bytes 817160 | tf_op jit(solution)/shard_map/ppermute | solution.py:154
  10.4 4.0 %collective-permute-start.2 = (bf16[56,2432]{1,0:T(8,128)(2,1)}, bf16[56,2432]{1,0:T(8,128)(2,1)S(1)}, u32[]{:S(2)}, u32[]{:S(2)}) collective-permute-start(bf16[56,2432]{1,0:T(8,128)(2,1)} %param.4), channel_id=1, source_target_pairs={{0,256},{1,65},{2,258},{3,67},{4,260},{5,69},{6,262},{7,71},{8,264... | collective-permute-start | bytes 817160 | tf_op jit(solution)/shard_map/ppermute | solution.py:154
  14.6 1.5 copy.56
  17.0 3.5 %collective-permute-done.2 = bf16[56,2432]{1,0:T(8,128)(2,1)S(1)} collective-permute-done((bf16[56,2432]{1,0:T(8,128)(2,1)}, bf16[56,2432]{1,0:T(8,128)(2,1)S(1)}, u32[]{:S(2)}, u32[]{:S(2)}) %collective-permute-start.2) | collective-permute-done | bytes 272416 | tf_op jit(solution)/shard_map/ppermute | solution.py:154
  20.5 1.9 %collective-permute-start.6 = (bf16[112,2432]{1,0:T(8,128)(2,1)S(1)}, bf16[112,2432]{1,0:T(8,128)(2,1)S(1)}, u32[]{:S(2)}, u32[]{:S(2)}) collective-permute-start(bf16[112,2432]{1,0:T(8,128)(2,1)S(1)} %get-tuple-element.58), channel_id=1, source_target_pairs={{0,96},{1,385},{2,98},{3,387},{4,100},{5,389},{6,102},{7,391},{8,1... | collective-permute-start | bytes 1634312 | tf_op jit(solution)/shard_map/ppermute | solution.py:181
  22.4 3.9 %collective-permute-start.3 = (bf16[112,2432]{1,0:T(8,128)(2,1)S(1)}, bf16[112,2432]{1,0:T(8,128)(2,1)S(1)}, u32[]{:S(2)}, u32[]{:S(2)}) collective-permute-start(bf16[112,2432]{1,0:T(8,128)(2,1)S(1)} %get-tuple-element.62), channel_id=1, source_target_pairs={{0,32},{1,129},{2,34},{3,131},{4,36},{5,133},{6,38},{7,135},{8,40}... | collective-permute-start | bytes 1634312 | tf_op jit(solution)/shard_map/ppermute | solution.py:178
  26.4 1.9 %collective-permute-start.4 = (bf16[112,2432]{1,0:T(8,128)(2,1)S(1)}, bf16[112,2432]{1,0:T(8,128)(2,1)S(1)}, u32[]{:S(2)}, u32[]{:S(2)}) collective-permute-start(bf16[112,2432]{1,0:T(8,128)(2,1)S(1)} %get-tuple-element.58), channel_id=1, source_target_pairs={{0,32},{1,129},{2,34},{3,131},{4,36},{5,133},{6,38},{7,135},{8,40}... | collective-permute-start | bytes 1634312 | tf_op jit(solution)/shard_map/ppermute | solution.py:182
  28.8 5.1 %collective-permute-start.5 = (bf16[112,2432]{1,0:T(8,128)(2,1)S(1)}, bf16[112,2432]{1,0:T(8,128)(2,1)S(1)}, u32[]{:S(2)}, u32[]{:S(2)}) collective-permute-start(bf16[112,2432]{1,0:T(8,128)(2,1)S(1)} %get-tuple-element.62), channel_id=1, source_target_pairs={{0,96},{1,385},{2,98},{3,387},{4,100},{5,389},{6,102},{7,391},{8,1... | collective-permute-start | bytes 1634312 | tf_op jit(solution)/shard_map/ppermute | solution.py:179
  33.9 1.9 %collective-permute-start.8 = (bf16[112,2432]{1,0:T(8,128)(2,1)S(1)}, bf16[112,2432]{1,0:T(8,128)(2,1)S(1)}, u32[]{:S(2)}, u32[]{:S(2)}) collective-permute-start(bf16[112,2432]{1,0:T(8,128)(2,1)S(1)} %collective-permute-done.6), channel_id=1, source_target_pairs={{0,96},{1,385},{2,98},{3,387},{4,100},{5,389},{6,102},{7,391},{8,1... | collective-permute-start | bytes 1634312 | tf_op jit(solution)/shard_map/ppermute | solution.py:184
  35.9 3.9 %collective-permute-start.7 = (bf16[112,2432]{1,0:T(8,128)(2,1)S(1)}, bf16[112,2432]{1,0:T(8,128)(2,1)S(1)}, u32[]{:S(2)}, u32[]{:S(2)}) collective-permute-start(bf16[112,2432]{1,0:T(8,128)(2,1)S(1)} %collective-permute-done.3), channel_id=1, source_target_pairs={{0,32},{1,129},{2,34},{3,131},{4,36},{5,133},{6,38},{7,135},{8,40}... | collective-permute-start | bytes 1634312 | tf_op jit(solution)/shard_map/ppermute | solution.py:184
  39.8 0.9 collective-permute-done.4
  41.0 1.7 fusion.51
  42.8 5.6 %collective-permute-done.7 = bf16[112,2432]{1,0:T(8,128)(2,1)S(1)} collective-permute-done((bf16[112,2432]{1,0:T(8,128)(2,1)S(1)}, bf16[112,2432]{1,0:T(8,128)(2,1)S(1)}, u32[]{:S(2)}, u32[]{:S(2)}) %collective-permute-start.7) | collective-permute-done | bytes 544800 | tf_op jit(solution)/shard_map/ppermute | solution.py:184
  48.5 0.8 fusion.50
  49.5 1.8 %copy-done = f32[384,2432]{1,0:T(8,128)} copy-done((f32[384,2432]{1,0:T(8,128)}, f32[384,2432]{1,0:T(8,128)S(1)}, u32[]{:S(2)}) %copy-start) | copy-done | bytes 3735576
  51.3 2.2 %multiply_reduce_fusion.4 = (f32[384]{0:T(512)S(1)}, f32[384]{0:T(512)S(1)}, f32[384]{0:T(512)S(1)}, f32[384]{0:T(512)S(1)}, f32[384]{0:T(512)S(1)}) fusion(bf16[384,2432]{1,0:T(8,128)(2,1)S(1)} %copy-done.1, f32[384,2432]{1,0:T(8,128)S(1)} %get-tuple-element.78, f32[384]{0:T(512)S(1)} %fusion.1, f32[384]{0:T(512)S(1)} %get-tuple-element.77), kind=kLoop, calls=%fused_computation.8 | loop fusion | flops 11204736 | bytes 5614080 | tf_op jit(solution)/shard_map/reduce_sum | solution.py:203
  53.6 1.9 %collective-permute-start.9 = (f32[7,384]{1,0:T(8,128)S(1)}, f32[7,384]{1,0:T(8,128)S(1)}, u32[]{:S(2)}, u32[]{:S(2)}) collective-permute-start(f32[7,384]{1,0:T(8,128)S(1)} %stack.146), channel_id=1, source_target_pairs={{0,1},{1,0},{2,3},{3,2},{4,5},{5,4},{6,7},{7,6},{8,9},{9,8},{10,11... | collective-permute-start | bytes 32264 | tf_op jit(solution)/shard_map/ppermute | solution.py:206
  55.5 1.1 collective-permute-done.9
  56.9 29.7 %all_to_all.20 = f32[16,7,384]{2,1,0:T(8,128)S(1)} all-to-all(f32[16,7,384]{2,1,0:T(8,128)S(1)} %broadcast_in_dim.9), channel_id=1, replica_groups={{0,2,4,6,8,10,12,14,16,18,20,22,24,26,28,30},{1,3,5,7,9,11,13,15,17,19,..., dimensions={0} | all-to-all | bytes 344064 | tf_op jit(solution)/shard_map/all_to_all | solution.py:40
  86.8 6.2 %multiply_reduce_fusion.1 = (f32[2432]{0:T(1024)S(1)}, f32[2432]{0:T(1024)S(1)}, f32[2432]{0:T(1024)S(1)}, f32[2432]{0:T(1024)S(1)}, f32[2432]{0:T(1024)S(1)}, /*index=5*/f32[384,2432]{1,0:T(8,128)}) fusion(bf16[384,2432]{1,0:T(8,128)(2,1)S(1)} %copy-done.1, f32[384]{0:T(512)S(1)} %get-tuple-element.75, f32[384]{0:T(512)S(1)} %fusion.1, ...), kind=kLoop, calls=%fused_computation.5 | loop fusion | flops 13062272 | bytes 9393664 | tf_op jit(solution)/shard_map/reduce_sum | solution.py:223
  93.3 19.5 %all_to_all.21 = f32[16,5,2432]{2,1,0:T(8,128)S(1)} all-to-all(f32[16,5,2432]{2,1,0:T(8,128)S(1)} %broadcast_in_dim.10), channel_id=1, replica_groups=mesh['dp'=16,'vocab'=32] {'dp'}, dimensions={0} | all-to-all | bytes 1556480 | tf_op jit(solution)/shard_map/all_to_all | solution.py:40
  113.1 6.3 %fusion.44 = (f32[384]{0:T(512)S(1)}, f32[384]{0:T(512)S(1)}, f32[384,2432]{1,0:T(8,128)}) fusion(f32[384,2432]{1,0:T(8,128)} %get-tuple-element.45.q_ref, f32[2432]{0:T(1024)S(1)} %get-tuple-element.29, f32[2432]{0:T(1024)S(1)} %get-tuple-element.30, f32[2432]{0:T(1024)S(1)} %get-tuple-element.41, f32[2432]{0:T(1024)S(1)} %get-tuple-element.28, ...), kind=kLoop, calls=%fused_computation.128 | loop fusion | flops 15875328 | bytes 9387008 | tf_op jit(solution)/shard_map/reduce_sum | solution.py:243
  120.2 9.1 %all-to-all-start.2 = ((f32[32,1,384]{2,1,0:T(1,128)}), f32[32,1,384]{2,1,0:T(1,128)S(1)}, u32[]{:S(2)}, u32[]{:S(2)}) async-start(f32[32,1,384]{2,1,0:T(1,128)} %broadcast_in_dim.11), calls=%async_computation.2 | async-start | bytes 98304 | tf_op jit(solution)/shard_map/all_to_all | solution.py:40
  129.3 9.2 %shard_map.50.refs_2_ = f32[2,2,16,28,384]{4,3,2,1,0:T(8,128)S(1)} custom-call(s32[17]{0:T(128)S(1)} %pad_add_fusion.place_ref, f32[384,2432]{1,0:T(8,128)} %get-tuple-element.45.q_ref, f32[384,2432]{1,0:T(8,128)} %get-tuple-element.42.g_ref, f32[384,1]{1,0:T(8,128)S(1)} %div.157.mean_ref, bf16[672,2432]{1,0:T(8,128)(2,1)} %copy-done.2, ...), custom_call_target="tpu_custom_call" | custom-call | flops 3347054592 | bytes 14942208 | tf_op jit(solution)/shard_map/pallas_call | solution.py:246
  138.5 4.4 %all-to-all-done.2.refs_1_ = f32[32,1,384]{2,1,0:T(1,128)S(1)} async-done(((f32[32,1,384]{2,1,0:T(1,128)}), f32[32,1,384]{2,1,0:T(1,128)S(1)}, u32[]{:S(2)}, u32[]{:S(2)}) %all-to-all-start.2) | async-done | bytes 49184 | tf_op jit(solution)/shard_map/all_to_all | solution.py:40
  143.5 1.9 %collective-permute-start.10 = (f32[16,28,384]{2,0,1:T(8,128)S(1)}, f32[16,28,384]{2,0,1:T(8,128)S(1)}, u32[]{:S(2)}, u32[]{:S(2)}) collective-permute-start(f32[16,28,384]{2,0,1:T(8,128)S(1)} %copy.67), channel_id=1, source_target_pairs={{0,1},{1,0},{2,3},{3,2},{4,5},{5,4},{6,7},{7,6},{8,9},{9,8},{10,11... | collective-permute-start | bytes 2064392 | tf_op jit(solution)/shard_map/ppermute | solution.py:272
  145.5 2.1 %collective-permute-done.10 = f32[16,28,384]{2,0,1:T(8,128)S(1)} collective-permute-done((f32[16,28,384]{2,0,1:T(8,128)S(1)}, f32[16,28,384]{2,0,1:T(8,128)S(1)}, u32[]{:S(2)}, u32[]{:S(2)}) %collective-permute-start.10) | collective-permute-done | bytes 688160 | tf_op jit(solution)/shard_map/ppermute | solution.py:272
  147.8 0.9 shard_map.52
  148.7 7.5 %all-to-all-start.3 = ((bf16[16,84,128]{2,1,0:T(8,128)(2,1)}), bf16[16,84,128]{2,1,0:T(8,128)(2,1)S(1)}, u32[]{:S(2)}, u32[]{:S(2)}) async-start(bf16[16,84,128]{2,1,0:T(8,128)(2,1)} %shard_map.52), calls=%async_computation.3 | async-start | bytes 720896 | tf_op jit(solution)/shard_map/all_to_all | solution.py:275
  156.2 4.9 %multiply_convert_fusion = bf16[384,2432]{1,0:T(8,128)(2,1)} fusion(f32[384,2432]{1,0:T(8,128)} %get-tuple-element.45.q_ref, f32[384,2432]{1,0:T(8,128)} %get-tuple-element.42.g_ref, f32[384]{0:T(512)S(1)} %broadcast_multiply_fusion), kind=kLoop, calls=%fused_computation.2 | loop fusion | flops 3735552 | bytes 9340416 | tf_op jit(solution)/shard_map/convert_element_type | solution.py:276
  161.2 18.0 %all-to-all-done.3.share_ref = bf16[16,84,128]{2,1,0:T(8,128)(2,1)S(1)} async-done(((bf16[16,84,128]{2,1,0:T(8,128)(2,1)}), bf16[16,84,128]{2,1,0:T(8,128)(2,1)S(1)}, u32[]{:S(2)}, u32[]{:S(2)}) %all-to-all-start.3) | async-done | bytes 344096 | tf_op jit(solution)/shard_map/all_to_all | solution.py:275
  (79 shorter events, 5.1 us)
Async XLA Ops:
  0.6 16.3 %collective-permute-start = (bf16[56,2432]{1,0:T(8,128)(2,1)}, bf16[56,2432]{1,0:T(8,128)(2,1)S(1)}, u32[]{:S(2)}, u32[]{:S(2)}) collective-permute-start(bf16[56,2432]{1,0:T(8,128)(2,1)} %param.4), channel_id=1, source_target_pairs={{0,128},{1,33},{2,130},{3,35},{4,132},{5,37},{6,134},{7,39},{8,136... | collective-permute-start | bytes 817160 | tf_op jit(solution)/shard_map/ppermute | solution.py:154
  4.0 12.9 %collective-permute-start.1 = (bf16[56,2432]{1,0:T(8,128)(2,1)}, bf16[56,2432]{1,0:T(8,128)(2,1)S(1)}, u32[]{:S(2)}, u32[]{:S(2)}) collective-permute-start(bf16[56,2432]{1,0:T(8,128)(2,1)} %param.4), channel_id=1, source_target_pairs={{0,384},{1,97},{2,386},{3,99},{4,388},{5,101},{6,390},{7,103},{8,3... | collective-permute-start | bytes 817160 | tf_op jit(solution)/shard_map/ppermute | solution.py:154
  10.4 10.1 %collective-permute-start.2 = (bf16[56,2432]{1,0:T(8,128)(2,1)}, bf16[56,2432]{1,0:T(8,128)(2,1)S(1)}, u32[]{:S(2)}, u32[]{:S(2)}) collective-permute-start(bf16[56,2432]{1,0:T(8,128)(2,1)} %param.4), channel_id=1, source_target_pairs={{0,256},{1,65},{2,258},{3,67},{4,260},{5,69},{6,262},{7,71},{8,264... | collective-permute-start | bytes 817160 | tf_op jit(solution)/shard_map/ppermute | solution.py:154
  14.5 2.3 %copy-start.4 = (bf16[56,2432]{1,0:T(8,128)(2,1)S(1)}, bf16[56,2432]{1,0:T(8,128)(2,1)}, u32[]{:S(2)}) copy-start(bf16[56,2432]{1,0:T(8,128)(2,1)} %param.4) | copy-start | bytes 817156
  16.5 11.8 %copy-start.1 = (bf16[384,2432]{1,0:T(8,128)(2,1)S(1)}, bf16[384,2432]{1,0:T(8,128)(2,1)}, u32[]{:S(2)}) copy-start(bf16[384,2432]{1,0:T(8,128)(2,1)} %param.5) | copy-start | bytes 5603332
  20.5 13.4 %collective-permute-start.6 = (bf16[112,2432]{1,0:T(8,128)(2,1)S(1)}, bf16[112,2432]{1,0:T(8,128)(2,1)S(1)}, u32[]{:S(2)}, u32[]{:S(2)}) collective-permute-start(bf16[112,2432]{1,0:T(8,128)(2,1)S(1)} %get-tuple-element.58), channel_id=1, source_target_pairs={{0,96},{1,385},{2,98},{3,387},{4,100},{5,389},{6,102},{7,391},{8,1... | collective-permute-start | bytes 1634312 | tf_op jit(solution)/shard_map/ppermute | solution.py:181
  22.4 13.4 %collective-permute-start.3 = (bf16[112,2432]{1,0:T(8,128)(2,1)S(1)}, bf16[112,2432]{1,0:T(8,128)(2,1)S(1)}, u32[]{:S(2)}, u32[]{:S(2)}) collective-permute-start(bf16[112,2432]{1,0:T(8,128)(2,1)S(1)} %get-tuple-element.62), channel_id=1, source_target_pairs={{0,32},{1,129},{2,34},{3,131},{4,36},{5,133},{6,38},{7,135},{8,40}... | collective-permute-start | bytes 1634312 | tf_op jit(solution)/shard_map/ppermute | solution.py:178
  26.4 14.4 %collective-permute-start.4 = (bf16[112,2432]{1,0:T(8,128)(2,1)S(1)}, bf16[112,2432]{1,0:T(8,128)(2,1)S(1)}, u32[]{:S(2)}, u32[]{:S(2)}) collective-permute-start(bf16[112,2432]{1,0:T(8,128)(2,1)S(1)} %get-tuple-element.58), channel_id=1, source_target_pairs={{0,32},{1,129},{2,34},{3,131},{4,36},{5,133},{6,38},{7,135},{8,40}... | collective-permute-start | bytes 1634312 | tf_op jit(solution)/shard_map/ppermute | solution.py:182
  28.8 12.1 %collective-permute-start.5 = (bf16[112,2432]{1,0:T(8,128)(2,1)S(1)}, bf16[112,2432]{1,0:T(8,128)(2,1)S(1)}, u32[]{:S(2)}, u32[]{:S(2)}) collective-permute-start(bf16[112,2432]{1,0:T(8,128)(2,1)S(1)} %get-tuple-element.62), channel_id=1, source_target_pairs={{0,96},{1,385},{2,98},{3,387},{4,100},{5,389},{6,102},{7,391},{8,1... | collective-permute-start | bytes 1634312 | tf_op jit(solution)/shard_map/ppermute | solution.py:179
  33.9 14.5 %collective-permute-start.8 = (bf16[112,2432]{1,0:T(8,128)(2,1)S(1)}, bf16[112,2432]{1,0:T(8,128)(2,1)S(1)}, u32[]{:S(2)}, u32[]{:S(2)}) collective-permute-start(bf16[112,2432]{1,0:T(8,128)(2,1)S(1)} %collective-permute-done.6), channel_id=1, source_target_pairs={{0,96},{1,385},{2,98},{3,387},{4,100},{5,389},{6,102},{7,391},{8,1... | collective-permute-start | bytes 1634312 | tf_op jit(solution)/shard_map/ppermute | solution.py:184
  35.9 12.5 %collective-permute-start.7 = (bf16[112,2432]{1,0:T(8,128)(2,1)S(1)}, bf16[112,2432]{1,0:T(8,128)(2,1)S(1)}, u32[]{:S(2)}, u32[]{:S(2)}) collective-permute-start(bf16[112,2432]{1,0:T(8,128)(2,1)S(1)} %collective-permute-done.3), channel_id=1, source_target_pairs={{0,32},{1,129},{2,34},{3,131},{4,36},{5,133},{6,38},{7,135},{8,40}... | collective-permute-start | bytes 1634312 | tf_op jit(solution)/shard_map/ppermute | solution.py:184
  41.0 1.8 copy-start.2
  48.5 1.0 copy-start.3
  49.5 1.8 %copy-start = (f32[384,2432]{1,0:T(8,128)}, f32[384,2432]{1,0:T(8,128)S(1)}, u32[]{:S(2)}) copy-start(f32[384,2432]{1,0:T(8,128)S(1)} %get-tuple-element.78) | copy-start | bytes 11206660
  53.6 3.1 %collective-permute-start.9 = (f32[7,384]{1,0:T(8,128)S(1)}, f32[7,384]{1,0:T(8,128)S(1)}, u32[]{:S(2)}, u32[]{:S(2)}) collective-permute-start(f32[7,384]{1,0:T(8,128)S(1)} %stack.146), channel_id=1, source_target_pairs={{0,1},{1,0},{2,3},{3,2},{4,5},{5,4},{6,7},{7,6},{8,9},{9,8},{10,11... | collective-permute-start | bytes 32264 | tf_op jit(solution)/shard_map/ppermute | solution.py:206
  120.2 22.8 %all-to-all-start.2 = ((f32[32,1,384]{2,1,0:T(1,128)}), f32[32,1,384]{2,1,0:T(1,128)S(1)}, u32[]{:S(2)}, u32[]{:S(2)}) async-start(f32[32,1,384]{2,1,0:T(1,128)} %broadcast_in_dim.11), calls=%async_computation.2 | async-start | bytes 98304 | tf_op jit(solution)/shard_map/all_to_all | solution.py:40
  143.5 4.0 %collective-permute-start.10 = (f32[16,28,384]{2,0,1:T(8,128)S(1)}, f32[16,28,384]{2,0,1:T(8,128)S(1)}, u32[]{:S(2)}, u32[]{:S(2)}) collective-permute-start(f32[16,28,384]{2,0,1:T(8,128)S(1)} %copy.67), channel_id=1, source_target_pairs={{0,1},{1,0},{2,3},{3,2},{4,5},{5,4},{6,7},{7,6},{8,9},{9,8},{10,11... | collective-permute-start | bytes 2064392 | tf_op jit(solution)/shard_map/ppermute | solution.py:272
  148.7 30.5 %all-to-all-start.3 = ((bf16[16,84,128]{2,1,0:T(8,128)(2,1)}), bf16[16,84,128]{2,1,0:T(8,128)(2,1)S(1)}, u32[]{:S(2)}, u32[]{:S(2)}) async-start(bf16[16,84,128]{2,1,0:T(8,128)(2,1)} %shard_map.52), calls=%async_computation.3 | async-start | bytes 720896 | tf_op jit(solution)/shard_map/all_to_all | solution.py:275
